TPU v7x, 32 devices: a whole 2x2x4 slice. The times are simulated.
32 devices in a mesh: dp: 16 (over z, x, core), tensor: 2 (over y).
Axes of the slice: x: 2, y: 2, z: 4, core: 2. Of those that a mesh axis runs over, the one named last changes fastest.
Arguments:
- tokens: bfloat16 [64, 256, 768], P('dp'), may hold values from -6 to 6
- segment_ids: int32 [64, 256], P('dp'), may hold values from 0 to 3, never falling along the last dimension, each value on 1 to 128 neighbouring positions
- pass_embed: float32 [768], replicated, may hold values from -5 to 5
- w_qkv: bfloat16 [3, 768, 768], P(None, None, 'tensor'), may hold values from -0.21875 to 0.21875
- w_out: bfloat16 [768, 768], P('tensor'), may hold values from -0.75 to 0.75
- w_up: bfloat16 [768, 3072], P(None, 'tensor'), may hold values from -0.21875 to 0.21875
- w_down: bfloat16 [3072, 768], P('tensor'), may hold values from -0.109375 to 0.109375
- ln_gain: float32 [2, 768], replicated, may hold values from 0.5 to 1.5
- ln_bias: float32 [2, 768], replicated, may hold values from -1.5 to 1.5
- cotangent: bfloat16 [64, 512, 768], P('dp'), may hold values from -6 to 6
Outputs:
- out: bfloat16 [64, 512, 768], P('dp')
- grad_tokens: float32 [64, 256, 768], P('dp')
- grad_qkv: float32 [3, 768, 768], P(None, None, 'tensor')
- grad_out: float32 [768, 768], P('tensor')
- grad_up: float32 [768, 3072], P(None, 'tensor')
- grad_down: float32 [3072, 768], P('tensor')
- grad_gain: float32 [2, 768], replicated
- grad_bias: float32 [2, 768], replicated
- grad_pass: float32 [768], replicated
Inputs may be any that keep to these rules, and one draw needn't show every extreme that they name: `segment_ids`: along a row the ids never fall; a document holds at most 128 tokens and one in each row holds exactly 128.
All inputs are finite; a program needn't handle non-finite values.
Results may differ from a plain program's by a relative error of at most 0.019.
Values may be sent and summed in bfloat16 or wider, within the bound.
No kernel may reach another device: no remote copies, remote signals or barrier semaphores. Data moves between devices by JAX's collectives and lax.ppermute only.
A program may use at most 256 MiB of HBM per device.

v0:
```python
import functools

import jax
import jax.numpy as jnp
from jax import lax
from jax.experimental import pallas as pl
from jax.experimental.pallas import tpu as pltpu
from jax.sharding import Mesh
from jax.sharding import PartitionSpec as P

HD = 64
EPS = 1e-05
NEG = -1000000000.0
F32 = jnp.float32
BF16 = jnp.bfloat16
ROWS_OVER = ("o", "x", "core")
FLIP = ((0, 1), (1, 0))
VMEM_LIMIT = 60 * 1024 * 1024


def ordered(flag, mine, theirs):
    first = flag == 0
    return jnp.stack([jnp.where(first, mine, theirs), jnp.where(first, theirs, mine)])


def take_half(array, index):
    half = array.shape[0] // 2
    return lax.dynamic_slice_in_dim(array, index * half, half, 0)


def flip_bit(array, axis, size, bit):
    return lax.ppermute(array, axis, [(i, i ^ bit) for i in range(size)])


def steps_of(outer):
    steps = [("x", 2, 1)]
    bit = 1
    while bit < outer:
        steps.append(("o", outer, bit))
        bit *= 2
    return steps


def my_bit(axis, bit):
    return (lax.axis_index(axis) // bit) % 2


def fetch_half(own):
    shape = own.shape
    flat = own.reshape(-1, shape[-1])
    x, core = lax.axis_index("x"), lax.axis_index("core")
    piece = take_half(take_half(flat, core), x)
    got = lax.ppermute(piece, "tensor", FLIP)
    got = ordered(x, got, lax.ppermute(got, "x", FLIP)).reshape(-1, shape[-1])
    got = ordered(core, got, lax.ppermute(got, "core", FLIP)).reshape(shape)
    return got


def sum_small(small, outer):
    for axis, size, bit in [("core", 2, 1), ("tensor", 2, 1)] + steps_of(outer):
        small = small + flip_bit(small, axis, size, bit)
    return small


def dot(a, b):
    return lax.dot_general(a, b, (((1,), (0,)), ((), ())), preferred_element_type=F32)


def dot_nt(a, b):
    return lax.dot_general(a, b, (((1,), (1,)), ((), ())), preferred_element_type=F32)


def dot_tn(a, b):
    return lax.dot_general(a, b, (((0,), (0,)), ((), ())), preferred_element_type=F32)


def norm_stats(h):
    centred = h - jnp.mean(h, axis=-1, keepdims=True)
    inverse = lax.rsqrt(jnp.mean(centred * centred, axis=-1, keepdims=True) + EPS)
    return centred * inverse, inverse


def norm_back(grad, normal, inverse, gain):
    scaled = grad * gain
    centre = jnp.mean(scaled, axis=-1, keepdims=True)
    proj = jnp.mean(scaled * normal, axis=-1, keepdims=True)
    return inverse * (scaled - centre - normal * proj)


def gelu_parts(u):
    c = 0.7978845608028654
    a = 0.044715 * c
    square = u * u
    half = 0.5 + 0.5 * jnp.tanh(u * (c + a * square))
    g = u * half
    return g, half + g * (1.0 - half) * (2.0 * c + 6.0 * a * square)


def whole(shape):
    return pl.BlockSpec(shape, lambda *_: (0,) * len(shape))


def call(body, grid, ins, outs, scratch=(), cost=(0, 0), name=None):
    return pl.pallas_call(
        body,
        grid=grid,
        in_specs=[s for _, s in ins],
        out_specs=[s for _, s in outs],
        out_shape=[a for a, _ in outs],
        scratch_shapes=scratch,
        compiler_params=pltpu.CompilerParams(
            dimension_semantics=("arbitrary",) * len(grid), vmem_limit_bytes=VMEM_LIMIT
        ),
        cost_estimate=pl.CostEstimate(
            flops=int(cost[0]), bytes_accessed=int(cost[1]), transcendentals=0
        ),
        name=name,
    )(*[a for a, _ in ins])


def sds(shape, dtype):
    return jax.ShapeDtypeStruct(shape, dtype)


def head_mask(h):
    lane = lax.broadcasted_iota(jnp.int32, (1, 2 * HD), 1)
    return jnp.where((lane >= h * HD) & (lane < (h + 1) * HD), 1.0, 0.0)


def first_half_lanes(shape):
    return lax.broadcasted_iota(jnp.int32, shape, 1) < HD


def pair_column(t, h):
    return t[:, h * HD : h * HD + 1]


def attend_first_body(rows, seq, pairs, a_ref, w_ref, bias_ref, qkv_ref, o_ref, lse_ref):
    a = a_ref[...]
    for j in range(3):
        qkv_ref[j] = dot(a, w_ref[j]).astype(BF16)
    for r in range(rows):
        sl = slice(r * seq, (r + 1) * seq)
        bias = bias_ref[r]
        for p in range(pairs):
            ln = slice(p * 2 * HD, (p + 1) * 2 * HD)
            q, k, v = (qkv_ref[j, sl, ln] for j in range(3))
            got = []
            for h in range(2):
                qm = q * (head_mask(h) * HD**-0.5).astype(BF16)
                s = dot_nt(qm, k) + bias
                top = jnp.max(s, axis=1, keepdims=True)
                e = jnp.exp(s - top)
                mass = jnp.sum(e, axis=1, keepdims=True)
                got.append((dot(e.astype(BF16), v) * (1.0 / mass), top + jnp.log(mass)))
            first = first_half_lanes((seq, 2 * HD))
            o_ref[sl, ln] = jnp.where(first, got[0][0], got[1][0]).astype(BF16)
            lse_ref[sl, ln] = jnp.where(first, got[0][1], got[1][1])


def attend_first(a, w, bias):
    rows, seq = bias.shape[0], bias.shape[1]
    n, d = a.shape
    f = w.shape[2]
    return call(
        functools.partial(attend_first_body, rows, seq, f // (2 * HD)),
        (1,),
        [(a, whole(a.shape)), (w, whole(w.shape)), (bias, whole(bias.shape))],
        [
            (sds((3, n, f), BF16), whole((3, n, f))),
            (sds((n, f), BF16), whole((n, f))),
            (sds((n, f), F32), whole((n, f))),
        ],
        cost=(6 * n * d * f + 16 * n * seq * f, 0),
        name="attend_first",
    )


def mlp_first_body(
    x_ref, o_ref, wout_ref, gb_ref, wup_ref, wdown_ref,
    h1_ref, n2_ref, g_ref, d_ref, ho_ref, ao_ref,
):
    j = pl.program_id(0)

    @pl.when(j == 0)
    def _():
        h1 = x_ref[...].astype(F32) + dot(o_ref[...], wout_ref[...])
        h1_ref[...] = h1
        normal, _ = norm_stats(h1)
        n2_ref[...] = (normal * gb_ref[1:2] + gb_ref[3:4]).astype(BF16)
        ho_ref[...] = h1 + gb_ref[4:5]

    u = dot(n2_ref[...], wup_ref[...])
    g, d = gelu_parts(u)
    g = g.astype(BF16)
    g_ref[...] = g
    d_ref[...] = d.astype(BF16)
    ho_ref[...] += dot(g, wdown_ref[...])

    @pl.when(j == pl.num_programs(0) - 1)
    def _():
        normal, _ = norm_stats(ho_ref[...])
        ao_ref[...] = (normal * gb_ref[0:1] + gb_ref[2:3]).astype(BF16)


def mlp_first(x, o, wout, gb, wup, wdown):
    n, d = x.shape
    ff = wup.shape[1]
    c = 512
    return call(
        mlp_first_body,
        (ff // c,),
        [
            (x, whole(x.shape)),
            (o, whole(o.shape)),
            (wout, whole(wout.shape)),
            (gb, whole(gb.shape)),
            (wup, pl.BlockSpec((d, c), lambda j: (0, j))),
            (wdown, pl.BlockSpec((c, d), lambda j: (j, 0))),
        ],
        [
            (sds((n, d), F32), whole((n, d))),
            (sds((n, d), BF16), whole((n, d))),
            (sds((n, ff), BF16), pl.BlockSpec((n, c), lambda j: (0, j))),
            (sds((n, ff), BF16), pl.BlockSpec((n, c), lambda j: (0, j))),
            (sds((n, d), F32), whole((n, d))),
            (sds((n, d), BF16), whole((n, d))),
        ],
        cost=(2 * n * d * (2 * ff + d), 0),
        name="mlp_first",
    )


def attend_second_body(
    rows, seq, pairs, a_ref, w_ref, incl_ref, strict_ref, qkve_ref, o1_ref, lse1_ref,
    qkvo_ref, o2_ref, lse2_ref,
):
    a = a_ref[...]
    for j in range(3):
        qkvo_ref[j] = dot(a, w_ref[j]).astype(BF16)

    def row(r, _):
        sl = pl.ds(pl.multiple_of(r * seq, seq), seq)
        incl, strict = incl_ref[r], strict_ref[r]
        for p in range(pairs):
            ln = slice(p * 2 * HD, (p + 1) * 2 * HD)
            qe, ke, ve = (qkve_ref[j, sl, ln] for j in range(3))
            qo, ko, vo = (qkvo_ref[j, sl, ln] for j in range(3))
            o1 = o1_ref[sl, ln].astype(F32)
            lse1 = lse1_ref[sl, ln]
            even, odd = [], []
            for h in range(2):
                scale = (head_mask(h) * HD**-0.5).astype(BF16)
                s = dot_nt(qe * scale, ko) + strict
                old = pair_column(lse1, h)
                top = jnp.maximum(old, jnp.max(s, axis=1, keepdims=True))
                e = jnp.exp(s - top)
                kept = jnp.exp(old - top)
                mass = kept + jnp.sum(e, axis=1, keepdims=True)
                o = (kept * o1 + dot(e.astype(BF16), vo)) * (1.0 / mass)
                even.append((o, top + jnp.log(mass)))
                qm = qo * scale
                s1 = dot_nt(qm, ke) + incl
                s2 = dot_nt(qm, ko) + incl
                top = jnp.max(jnp.maximum(s1, s2), axis=1, keepdims=True)
                e1 = jnp.exp(s1 - top)
                e2 = jnp.exp(s2 - top)
                mass = jnp.sum(e1 + e2, axis=1, keepdims=True)
                o = (dot(e1.astype(BF16), ve) + dot(e2.astype(BF16), vo)) * (1.0 / mass)
                odd.append((o, top + jnp.log(mass)))
            first = first_half_lanes((seq, 2 * HD))
            for i, got in enumerate((even, odd)):
                o2_ref[i, sl, ln] = jnp.where(first, got[0][0], got[1][0]).astype(BF16)
                lse2_ref[i, sl, ln] = jnp.where(first, got[0][1], got[1][1])
        return 0

    lax.fori_loop(0, rows, row, 0)


def attend_second(a, w, incl, strict, qkve, o1, lse1):
    rows, seq = incl.shape[0], incl.shape[1]
    n, d = a.shape
    f = w.shape[2]
    b = 256
    col = lambda lead: pl.BlockSpec(lead + (b,), lambda i: (0,) * len(lead) + (i,))
    return call(
        functools.partial(attend_second_body, rows, seq, b // (2 * HD)),
        (f // b,),
        [
            (a, whole(a.shape)),
            (w, col((3, d))),
            (incl, whole(incl.shape)),
            (strict, whole(strict.shape)),
            (qkve, col((3, n))),
            (o1, col((n,))),
            (lse1, col((n,))),
        ],
        [
            (sds((3, n, f), BF16), col((3, n))),
            (sds((2, n, f), BF16), col((2, n))),
            (sds((2, n, f), F32), col((2, n))),
        ],
        cost=(6 * n * d * f + 48 * n * seq * f, 0),
        name="attend_second",
    )


def weave(seq):
    i = lax.broadcasted_iota(jnp.int32, (2 * seq, 2 * seq), 0)
    k = lax.broadcasted_iota(jnp.int32, (2 * seq, 2 * seq), 1)
    place = jnp.where(k < seq, 2 * k, 2 * (k - seq) + 1)
    return jnp.where(i == place, 1.0, 0.0).astype(BF16)


def mlp_second_body(
    rows, seq, x_ref, ho_ref, o_ref, cot_ref, wout_ref, gb_ref, wup_ref, wdown_ref,
    out_ref, n2_ref, g_ref, du_ref, dh1_ref, dp_ref, do_ref, sums_ref, dm_ref,
    h1_ref, z_ref, dn_ref,
):
    j = pl.program_id(0)
    n = rows * seq
    halves = (slice(0, n), slice(n, 2 * n))

    @pl.when(j == 0)
    def _():
        for i, sl in enumerate(halves):
            start = x_ref[...].astype(F32) if i == 0 else ho_ref[...]
            h1 = start + dot(o_ref[i], wout_ref[...])
            h1_ref[sl] = h1
            normal, _ = norm_stats(h1)
            n2_ref[sl] = (normal * gb_ref[1:2] + gb_ref[3:4]).astype(BF16)
        z_ref[...] = jnp.zeros_like(z_ref)
        dn_ref[...] = jnp.zeros_like(dn_ref)
        mix = weave(seq)
        for r in range(rows):
            parted = dot_tn(mix, cot_ref[r]).astype(BF16)
            for i in range(2):
                dm_ref[i * n + r * seq : i * n + (r + 1) * seq] = parted[i * seq : (i + 1) * seq]

    for sl in halves:
        u = dot(n2_ref[sl], wup_ref[...])
        dg = dot_nt(dm_ref[sl], wdown_ref[...])
        g, d = gelu_parts(u)
        g = g.astype(BF16)
        du = (dg * d).astype(BF16)
        g_ref[sl] = g
        du_ref[sl] = du
        z_ref[sl] += dot(g, wdown_ref[...])
        dn_ref[sl] += dot_nt(du, wup_ref[...])

    @pl.when(j == pl.num_programs(0) - 1)
    def _():
        mix = weave(seq)
        for r in range(rows):
            pair = [slice(i * n + r * seq, i * n + (r + 1) * seq) for i in range(2)]
            z = jnp.concatenate([(h1_ref[s] + z_ref[s]).astype(BF16) for s in pair], axis=0)
            out_ref[r] = dot(mix, z).astype(BF16)
        gain_sum = jnp.zeros_like(gb_ref[0:1])
        bias_sum = jnp.zeros_like(gb_ref[0:1])
        for i in range(2 * rows):
            sl = slice(i * seq, (i + 1) * seq)
            normal, inverse = norm_stats(h1_ref[sl])
            dn = dn_ref[sl]
            gain_sum += jnp.sum(dn * normal, axis=0, keepdims=True)
            bias_sum += jnp.sum(dn, axis=0, keepdims=True)
            dh1 = dm_ref[sl].astype(F32) + norm_back(dn, normal, inverse, gb_ref[1:2])
            dh1_ref[sl] = dh1
            dp = dh1.astype(BF16)
            dp_ref[sl] = dp
            do_ref[sl] = dot_nt(dp, wout_ref[...]).astype(BF16)
        sums_ref[0:1] = gain_sum
        sums_ref[1:2] = bias_sum


def mlp_second(x, ho, o2, cot, wout, gb, wup, wdown, seq):
    n, d = x.shape
    ff = wup.shape[1]
    rows = n // seq
    c = 512
    blk = pl.BlockSpec((2 * n, c), lambda j: (0, j))
    return call(
        functools.partial(mlp_second_body, rows, seq),
        (ff // c,),
        [
            (x, whole(x.shape)),
            (ho, whole(ho.shape)),
            (o2, whole(o2.shape)),
            (cot, whole(cot.shape)),
            (wout, whole(wout.shape)),
            (gb, whole(gb.shape)),
            (wup, pl.BlockSpec((d, c), lambda j: (0, j))),
            (wdown, pl.BlockSpec((c, d), lambda j: (j, 0))),
        ],
        [
            (sds((rows, 2 * seq, d), BF16), whole((rows, 2 * seq, d))),
            (sds((2 * n, d), BF16), whole((2 * n, d))),
            (sds((2 * n, ff), BF16), blk),
            (sds((2 * n, ff), BF16), blk),
            (sds((2 * n, d), F32), whole((2 * n, d))),
            (sds((2 * n, d), BF16), whole((2 * n, d))),
            (sds((2 * n, d), BF16), whole((2 * n, d))),
            (sds((2, d), F32), whole((2, d))),
            (sds((2 * n, d), BF16), whole((2 * n, d))),
        ],
        scratch=[pltpu.VMEM((2 * n, d), F32)] * 3,
        cost=(2 * n * d * (8 * ff + 4 * d), 0),
        name="mlp_second",
    )


def attend_back_body(
    rows, seq, pairs, w_ref, incl_ref, strict_ref, qkve_ref, qkvo_ref, o2_ref, lse2_ref, do_ref,
    dh1_ref, ho_ref, gb_ref,
    dqkvo_ref, dqkve_ref, dy_ref, sums_ref, da_ref,
):
    j = pl.program_id(0)

    def row(r, _):
        sl = pl.ds(pl.multiple_of(r * seq, seq), seq)
        incl, strict = incl_ref[r], strict_ref[r]
        for p in range(pairs):
            ln = slice(p * 2 * HD, (p + 1) * 2 * HD)
            qe, ke, ve = (qkve_ref[t, sl, ln] for t in range(3))
            qo, ko, vo = (qkvo_ref[t, sl, ln] for t in range(3))
            doe, doo = do_ref[0, sl, ln], do_ref[1, sl, ln]
            de = doe.astype(F32) * o2_ref[0, sl, ln].astype(F32)
            dd = doo.astype(F32) * o2_ref[1, sl, ln].astype(F32)
            lse_e, lse_o = lse2_ref[0, sl, ln], lse2_ref[1, sl, ln]
            acc = [None] * 6
            first = first_half_lanes((seq, 2 * HD))
            for h in range(2):
                on = head_mask(h)
                low = on.astype(BF16)
                scale = (on * HD**-0.5).astype(BF16)
                delta_e = jnp.sum(de * on, axis=1, keepdims=True)
                delta_o = jnp.sum(dd * on, axis=1, keepdims=True)
                le, lo = pair_column(lse_e, h), pair_column(lse_o, h)
                qme, qmo = qe * scale, qo * scale
                dme, dmo = doe * low, doo * low

                def block(qm, k, bias, lse, dm, v, delta):
                    pr = jnp.exp(dot_nt(qm, k) + bias - lse)
                    ds = (pr * (dot_nt(dm, v) - delta)).astype(BF16)
                    return pr.astype(BF16), ds

                p1, s1 = block(qme, ko, strict, le, dme, vo, delta_e)
                p2, s2 = block(qmo, ke, incl, lo, dmo, ve, delta_o)
                p3, s3 = block(qmo, ko, incl, lo, dmo, vo, delta_o)
                new = [
                    dot(s1, ko),
                    dot_tn(s2, qo),
                    dot_tn(p2, doo),
                    dot(s2, ke) + dot(s3, ko),
                    dot_tn(s1, qe) + dot_tn(s3, qo),
                    dot_tn(p1, doe) + dot_tn(p3, doo),
                ]
                acc = [t if o is None else jnp.where(first, o, t) for o, t in zip(acc, new)]
            sc = HD**-0.5
            for t in range(3):
                k = 1.0 if t == 2 else sc
                dqkve_ref[t, sl, ln] = acc[t] * k
                dqkvo_ref[t, sl, ln] = (acc[3 + t] * k).astype(BF16)
        return 0

    lax.fori_loop(0, rows, row, 0)
    da = dot_nt(dqkvo_ref[0], w_ref[0])
    da += dot_nt(dqkvo_ref[1], w_ref[1])
    da += dot_nt(dqkvo_ref[2], w_ref[2])

    @pl.when(j == 0)
    def _():
        da_ref[...] = da

    @pl.when(j > 0)
    def _():
        da_ref[...] += da

    @pl.when(j == pl.num_programs(0) - 1)
    def _():
        gain_sum = jnp.zeros_like(gb_ref[0:1])
        bias_sum = jnp.zeros_like(gb_ref[0:1])
        pass_sum = jnp.zeros_like(gb_ref[0:1])
        for i in range(rows):
            sl = slice(i * seq, (i + 1) * seq)
            normal, inverse = norm_stats(ho_ref[sl])
            da = da_ref[sl]
            gain_sum += jnp.sum(da * normal, axis=0, keepdims=True)
            bias_sum += jnp.sum(da, axis=0, keepdims=True)
            dy = dh1_ref[sl] + norm_back(da, normal, inverse, gb_ref[0:1])
            dy_ref[sl] = dy
            pass_sum += jnp.sum(dy, axis=0, keepdims=True)
        sums_ref[0:1] = gain_sum
        sums_ref[1:2] = bias_sum
        sums_ref[2:3] = pass_sum


def attend_back(w, incl, strict, qkve, qkvo, o2, lse2, do, dh1, ho, gb):
    rows, seq = incl.shape[0], incl.shape[1]
    n, d = ho.shape
    f = w.shape[2]
    b = 256
    col = lambda lead: pl.BlockSpec(lead + (b,), lambda i: (0,) * len(lead) + (i,))
    return call(
        functools.partial(attend_back_body, rows, seq, b // (2 * HD)),
        (f // b,),
        [
            (w, col((3, d))),
            (incl, whole(incl.shape)),
            (strict, whole(strict.shape)),
            (qkve, col((3, n))),
            (qkvo, col((3, n))),
            (o2, col((2, n))),
            (lse2, col((2, n))),
            (do.reshape(2, n, f), col((2, n))),
            (dh1, pl.BlockSpec((n, d), lambda i: (1, 0))),
            (ho, whole(ho.shape)),
            (gb, whole(gb.shape)),
        ],
        [
            (sds((3, n, f), BF16), col((3, n))),
            (sds((3, n, f), F32), col((3, n))),
            (sds((n, d), F32), whole((n, d))),
            (sds((3, d), F32), whole((3, d))),
        ],
        scratch=[pltpu.VMEM((n, d), F32)],
        cost=(6 * n * d * f + 120 * n * seq * f, 0),
        name="attend_back",
    )


def mlp_back_body(
    rows, seq, dy_ref, h1_ref, wout_ref, gb_ref, d_ref, wup_ref, wdown_ref,
    du_ref, dh1_ref, dp_ref, do_ref, sums_ref, dm_ref, dn_ref,
):
    j = pl.program_id(0)

    @pl.when(j == 0)
    def _():
        dm_ref[...] = dy_ref[...].astype(BF16)
        dn_ref[...] = jnp.zeros_like(dn_ref)

    dg = dot_nt(dm_ref[...], wdown_ref[...])
    du = (dg * d_ref[...].astype(F32)).astype(BF16)
    du_ref[...] = du
    dn_ref[...] += dot_nt(du, wup_ref[...])

    @pl.when(j == pl.num_programs(0) - 1)
    def _():
        gain_sum = jnp.zeros_like(gb_ref[0:1])
        bias_sum = jnp.zeros_like(gb_ref[0:1])
        for i in range(rows):
            sl = slice(i * seq, (i + 1) * seq)
            normal, inverse = norm_stats(h1_ref[sl])
            dn = dn_ref[sl]
            gain_sum += jnp.sum(dn * normal, axis=0, keepdims=True)
            bias_sum += jnp.sum(dn, axis=0, keepdims=True)
            dh1 = dy_ref[sl] + norm_back(dn, normal, inverse, gb_ref[1:2])
            dh1_ref[sl] = dh1
            dp = dh1.astype(BF16)
            dp_ref[sl] = dp
            do_ref[sl] = dot_nt(dp, wout_ref[...]).astype(BF16)
        sums_ref[0:1] = gain_sum
        sums_ref[1:2] = bias_sum


def mlp_back(dy, h1, wout, gb, dgelu, wup, wdown, seq):
    n, d = dy.shape
    ff = wup.shape[1]
    c = 512
    blk = pl.BlockSpec((n, c), lambda j: (0, j))
    return call(
        functools.partial(mlp_back_body, n // seq, seq),
        (ff // c,),
        [
            (dy, whole(dy.shape)),
            (h1, whole(h1.shape)),
            (wout, whole(wout.shape)),
            (gb, whole(gb.shape)),
            (dgelu, blk),
            (wup, pl.BlockSpec((d, c), lambda j: (0, j))),
            (wdown, pl.BlockSpec((c, d), lambda j: (j, 0))),
        ],
        [
            (sds((n, ff), BF16), blk),
            (sds((n, d), F32), whole((n, d))),
            (sds((n, d), BF16), whole((n, d))),
            (sds((n, d), BF16), whole((n, d))),
            (sds((2, d), F32), whole((2, d))),
        ],
        scratch=[pltpu.VMEM((n, d), BF16), pltpu.VMEM((n, d), F32)],
        cost=(2 * n * d * (2 * ff + d), 0),
        name="mlp_back",
    )


def attend_back_even_body(
    rows, seq, pairs, w_ref, incl_ref, qkve_ref, o1_ref, lse1_ref, do1_ref, o2_ref, lse2_ref, do2_ref,
    part_ref, dh1_ref, dh2_ref, x_ref, gb_ref,
    dqkv_ref, gt_ref, sums_ref, da_ref,
):
    j = pl.program_id(0)

    def row(r, _):
        sl = pl.ds(pl.multiple_of(r * seq, seq), seq)
        incl = incl_ref[r]
        for p in range(pairs):
            ln = slice(p * 2 * HD, (p + 1) * 2 * HD)
            q, k, v = (qkve_ref[t, sl, ln] for t in range(3))
            do1 = do1_ref[sl, ln].astype(F32)
            do2 = do2_ref[0, sl, ln].astype(F32)
            lse1 = lse1_ref[sl, ln]
            ratio = jnp.exp(lse1 - lse2_ref[0, sl, ln])
            do2 = do2 * ratio
            both = (do1 + do2).astype(BF16)
            dd = do1 * o1_ref[sl, ln].astype(F32) + do2 * o2_ref[0, sl, ln].astype(F32)
            acc = [None] * 3
            first = first_half_lanes((seq, 2 * HD))
            for h in range(2):
                on = head_mask(h)
                delta = jnp.sum(dd * on, axis=1, keepdims=True)
                qm = q * (on * HD**-0.5).astype(BF16)
                pr = jnp.exp(dot_nt(qm, k) + incl - pair_column(lse1, h))
                ds = (pr * (dot_nt(both * on.astype(BF16), v) - delta)).astype(BF16)
                new = [dot(ds, k), dot_tn(ds, q), dot_tn(pr.astype(BF16), both)]
                acc = [t if o is None else jnp.where(first, o, t) for o, t in zip(acc, new)]
            for t in range(3):
                sc = 1.0 if t == 2 else HD**-0.5
                dqkv_ref[t, sl, ln] = (acc[t] * sc + part_ref[t, sl, ln]).astype(BF16)
        return 0

    lax.fori_loop(0, rows, row, 0)
    da = dot_nt(dqkv_ref[0], w_ref[0])
    da += dot_nt(dqkv_ref[1], w_ref[1])
    da += dot_nt(dqkv_ref[2], w_ref[2])

    @pl.when(j == 0)
    def _():
        da_ref[...] = da

    @pl.when(j > 0)
    def _():
        da_ref[...] += da

    @pl.when(j == pl.num_programs(0) - 1)
    def _():
        gain_sum = jnp.zeros_like(gb_ref[0:1])
        bias_sum = jnp.zeros_like(gb_ref[0:1])
        for i in range(rows):
            sl = slice(i * seq, (i + 1) * seq)
            normal, inverse = norm_stats(x_ref[sl].astype(F32))
            da = da_ref[sl]
            gain_sum += jnp.sum(da * normal, axis=0, keepdims=True)
            bias_sum += jnp.sum(da, axis=0, keepdims=True)
            back = norm_back(da, normal, inverse, gb_ref[0:1])
            gt_ref[sl] = (dh1_ref[sl] + dh2_ref[sl] + back).astype(BF16)
        sums_ref[0:1] = gain_sum
        sums_ref[1:2] = bias_sum


def attend_back_even(w, incl, qkve, o1, lse1, do1, o2, lse2, do2, part, dh1, dh2, x, gb):
    rows, seq = incl.shape[0], incl.shape[1]
    n, d = x.shape
    f = w.shape[2]
    b = 256
    col = lambda lead: pl.BlockSpec(lead + (b,), lambda i: (0,) * len(lead) + (i,))
    return call(
        functools.partial(attend_back_even_body, rows, seq, b // (2 * HD)),
        (f // b,),
        [
            (w, col((3, d))),
            (incl, whole(incl.shape)),
            (qkve, col((3, n))),
            (o1, col((n,))),
            (lse1, col((n,))),
            (do1, col((n,))),
            (o2, col((1, n))),
            (lse2, col((1, n))),
            (do2.reshape(2, n, f), col((1, n))),
            (part, col((3, n))),
            (dh1, whole((n, d))),
            (dh2, whole((n, d))),
            (x, whole(x.shape)),
            (gb, whole(gb.shape)),
        ],
        [
            (sds((3, n, f), BF16), col((3, n))),
            (sds((n, d), BF16), whole((n, d))),
            (sds((2, d), F32), whole((2, d))),
        ],
        scratch=[pltpu.VMEM((n, d), F32)],
        cost=(6 * n * d * f + 40 * n * seq * f, 0),
        name="attend_back_even",
    )


def packed_call(body, grid, me, ins, outs, scratch=(), flops=0, name=None):
    return pl.pallas_call(
        body,
        grid_spec=pltpu.PrefetchScalarGridSpec(
            num_scalar_prefetch=1,
            grid=grid,
            in_specs=[s for _, s in ins],
            out_specs=[s for _, s in outs],
            scratch_shapes=scratch,
        ),
        out_shape=[a for a, _ in outs],
        compiler_params=pltpu.CompilerParams(
            dimension_semantics=("arbitrary",) * len(grid), vmem_limit_bytes=VMEM_LIMIT
        ),
        cost_estimate=pl.CostEstimate(flops=int(flops), bytes_accessed=0, transcendentals=0),
        name=name,
    )(me, *[a for a, _ in ins])


def grad_down_body(me_ref, g1_ref, g2_ref, dm1_ref, dm2_ref, out_ref, acc_ref):
    low = me_ref[0] % 4
    acc = dot_tn(g1_ref[...], dm1_ref[...])
    acc += dot_tn(g2_ref[...], dm2_ref[...])
    acc_ref[...] = acc.reshape(acc_ref.shape)
    for s in range(4):
        out_ref[0, s] = acc_ref[s ^ low].astype(BF16)


def grad_down(me, side, g1, g2, dm1, dm2):
    n, d = dm1.shape
    ff = g1.shape[1]
    b = ff // 8
    pick = lambda y, h, me: (0, (1 - y) * 4 + ((me[0] // 8) ^ side) * 2 + h)
    const = lambda y, h, me: (0, 0)
    return packed_call(
        grad_down_body,
        (2, 2),
        me,
        [
            (g1, pl.BlockSpec((n, b), pick)),
            (g2, pl.BlockSpec((2 * n, b), pick)),
            (dm1, pl.BlockSpec((n, d), const)),
            (dm2, pl.BlockSpec((2 * n, d), const)),
        ],
        [
            (
                sds((2, 8, b // 4, d), BF16),
                pl.BlockSpec((1, 4, b // 4, d), lambda y, h, me: (y, h ^ ((me[0] // 4) % 2), 0, 0)),
            )
        ],
        scratch=[pltpu.VMEM((4, b // 4, d), F32)],
        flops=2 * 3 * n * d * ff // 2,
        name="grad_down",
    )[0]


def grad_up_body(me_ref, n1_ref, n2_ref, du1_ref, du2_ref, out_ref, t1_ref, t2_ref, acc_ref):
    low = me_ref[0] % 8

    @pl.when((pl.program_id(0) == 0) & (pl.program_id(1) == 0))
    def _():
        t1_ref[...] = n1_ref[...].T
        t2_ref[...] = n2_ref[...].T

    acc = dot(t1_ref[...], du1_ref[...])
    acc += dot(t2_ref[...], du2_ref[...])
    acc_ref[...] = acc.reshape(acc_ref.shape)
    for s in range(8):
        out_ref[0, s] = acc_ref[s ^ low].astype(BF16)


def grad_up(me, side, n1, n2, du1, du2):
    n, d = n1.shape
    ff = du1.shape[1]
    b, c, parts = d // 2, 512, ff // 2 // 512
    rows = lambda y, j, me: (0, (me[0] // 8) ^ side)
    cols = lambda y, j, me: (0, (1 - y) * parts + j)
    return packed_call(
        grad_up_body,
        (2, parts),
        me,
        [
            (n1, pl.BlockSpec((n, b), rows)),
            (n2, pl.BlockSpec((2 * n, b), rows)),
            (du1, pl.BlockSpec((n, c), cols)),
            (du2, pl.BlockSpec((2 * n, c), cols)),
        ],
        [
            (
                sds((2, 8, b // 8, ff // 2), BF16),
                pl.BlockSpec((1, 8, b // 8, c), lambda y, j, me: (y, 0, 0, j)),
            )
        ],
        scratch=[
            pltpu.VMEM((b, n), BF16),
            pltpu.VMEM((b, 2 * n), BF16),
            pltpu.VMEM((8, b // 8, c), F32),
        ],
        flops=2 * 3 * n * d * ff // 2,
        name="grad_up",
    )[0]


def grad_heads_body(
    me_ref, ae_ref, ao_ref, dp1_ref, dp2_ref, de_ref, do_ref, o1_ref, o2_ref, out_ref, acc_ref
):
    low = me_ref[0] % 8
    f = o1_ref.shape[1]
    for j in range(4):
        if j < 3:
            acc = dot_tn(ae_ref[...], de_ref[j])
            acc += dot_tn(ao_ref[...], do_ref[j])
        else:
            acc = dot_tn(dp1_ref[...], o1_ref[...])
            acc += dot_tn(dp2_ref[...], o2_ref[...])
        acc_ref[...] = acc.reshape(acc_ref.shape)
        for s in range(8):
            out_ref[0, s, :, j * f : (j + 1) * f] = acc_ref[s ^ low].astype(BF16)


def grad_heads(me, side, ae, ao, dp1, dp2, dqkv_e, dqkv_o, o1, o2):
    n, d = ae.shape
    b, f = d // 2, o1.shape[1] // 2
    rows = lambda y, me: (0, (me[0] // 8) ^ side)
    cols = lambda y, me: (0, 1 - y)
    cols3 = lambda y, me: (0, 0, 1 - y)
    return packed_call(
        grad_heads_body,
        (2,),
        me,
        [
            (ae, pl.BlockSpec((n, b), rows)),
            (ao, pl.BlockSpec((n, b), rows)),
            (dp1, pl.BlockSpec((n, b), rows)),
            (dp2, pl.BlockSpec((2 * n, b), rows)),
            (dqkv_e, pl.BlockSpec((3, n, f), cols3)),
            (dqkv_o, pl.BlockSpec((3, n, f), cols3)),
            (o1, pl.BlockSpec((n, f), cols)),
            (o2, pl.BlockSpec((2 * n, f), cols)),
        ],
        [
            (
                sds((2, 8, b // 8, 4 * f), BF16),
                pl.BlockSpec((1, 8, b // 8, 4 * f), lambda y, me: (y, 0, 0, 0)),
            )
        ],
        scratch=[pltpu.VMEM((8, b // 8, f), F32)],
        flops=2 * (2 * 3 + 3) * n * d * f,
        name="grad_heads",
    )[0]


def unpack_body(heads, me_ref, mine_ref, got_ref, *out_refs):
    low = me_ref[0] % 8
    other = pl.program_id(0) ^ (me_ref[0] // 8)
    rows = mine_ref.shape[1]

    def write(ref):
        for s in range(8):
            sl = slice(s * rows, (s + 1) * rows)
            if not heads:
                out_refs[0][sl] = ref[s ^ low].astype(F32)
            else:
                f = out_refs[0].shape[2]
                for j in range(3):
                    out_refs[0][j, sl] = ref[s ^ low, :, j * f : (j + 1) * f].astype(F32)
                out_refs[2][sl] = ref[s ^ low, :, 3 * f :].astype(F32)
        if heads:
            out_refs[1][...] = out_refs[2][...].T

    pl.when(other == 0)(lambda: write(mine_ref))
    pl.when(other != 0)(lambda: write(got_ref))


def unpack(me, mine, got, heads=False):
    _, r, w = mine.shape
    half = 8 * r
    ins = [(t, pl.BlockSpec(t.shape, lambda i, me: (0, 0, 0))) for t in (mine, got)]
    if heads:
        f = w // 4
        outs = [
            (sds((3, 2 * half, f), F32), pl.BlockSpec((3, half, f), lambda i, me: (0, i, 0))),
            (sds((f, 2 * half), F32), pl.BlockSpec((f, half), lambda i, me: (0, i))),
        ]
        scratch = [pltpu.VMEM((half, f), F32)]
    else:
        outs = [(sds((2 * half, w), F32), pl.BlockSpec((half, w), lambda i, me: (i, 0)))]
        scratch = []
    return packed_call(
        functools.partial(unpack_body, heads), (2,), me, ins, outs, scratch=scratch, name="unpack"
    )


def fold(*parts):
    return sum(p.astype(F32) for p in parts).astype(BF16)


def after(value, *first):
    return lax.optimization_barrier((value, first))[0]


def over_core(send):
    return lax.ppermute(send, "core", FLIP)


class Summing:
    def __init__(self, outer, keep, got):
        self.steps = [("x", 2, 1), ("o", outer, 1), ("o", outer, 2)]
        self.extra = [("o", outer, 1 << b) for b in range(2, outer.bit_length() - 1)]
        self.own = (keep[1], got[1])
        self.got = lax.ppermute(fold(keep[0], got[0]), "tensor", FLIP)
        self.total = None

    def step(self, axis, size, bit):
        if self.total is None:
            total = fold(*self.own, self.got)
        else:
            total = fold(self.total, self.got)
        half = total.shape[0] // 2
        self.total = total[:half]
        self.got = flip_bit(total[half:], axis, size, bit)

    def scatter(self):
        for s in self.steps:
            self.step(*s)

    def gather(self):
        total = fold(self.total, self.got)
        for s in self.extra:
            total = fold(total, flip_bit(total, *s))
        for s in reversed(self.steps):
            total = jnp.concatenate([total, flip_bit(total, *s)], axis=0)
        return total, over_core(total)


def mask_biases(seg):
    seq = seg.shape[1]
    place = jnp.arange(seq, dtype=jnp.int32)
    same = seg[:, :, None] == seg[:, None, :]
    below = (place[:, None] > place[None, :])[None]
    incl = (place[:, None] >= place[None, :])[None]
    bias = lambda m: jnp.where(same & m, 0.0, NEG).astype(F32)
    return bias(incl), bias(below)


class Link:
    def __init__(self, outer, w_qkv, w_out, w_up, w_down):
        self.outer = outer
        self.own = (w_qkv, w_out, w_up, w_down)
        core, x, o = (lax.axis_index(a) for a in ("core", "x", "o"))
        self.me = (core * 8 + x * 4 + (o % 2) * 2 + (o // 2) % 2).astype(jnp.int32).reshape(1)

    def fetch_qkv(self):
        return self.own[0], fetch_half(self.own[0])

    def fetch_rest(self):
        return (
            jnp.concatenate([self.own[1], fetch_half(self.own[1])], axis=0),
            jnp.concatenate([self.own[2], fetch_half(self.own[2])], axis=1),
            jnp.concatenate([self.own[3], fetch_half(self.own[3])], axis=0),
        )

    def partner(self, t):
        return lax.ppermute(t, "tensor", FLIP)

    def core(self, t):
        return over_core(t)

    def summing(self, keep, got):
        return Summing(self.outer, keep, got)

    def small(self, t):
        return sum_small(t, self.outer)


def local_part(x, seg, cot, gb, link):
    rows, seq = seg.shape
    n, width = x.shape
    me = link.me
    incl, strict = mask_biases(seg)
    normal, _ = norm_stats(x.astype(F32))
    a_e = (normal * gb[0] + gb[2]).astype(BF16)
    wq_own, fetched = link.fetch_qkv()
    first = attend_first(a_e, wq_own, incl)
    second = attend_first(a_e, fetched, incl)
    qkv_e, o1, lse1 = (jnp.concatenate([s, t], axis=-1) for s, t in zip(first, second))
    wqkv = jnp.concatenate([wq_own, fetched], axis=2)
    wout, wup, wdown = link.fetch_rest()
    h1, n2_1, g1, d1, ho, a_o = mlp_first(x, o1, wout, gb, wup, wdown)
    qkv_o, o2, lse2 = attend_second(a_o, wqkv, incl, strict, qkv_e, o1, lse1)
    out, n2_2, g2, du2, dh1_2, dp2, do2, sums2, dm2 = mlp_second(x, ho, o2, cot, wout, gb, wup, wdown, seq)
    out_got = link.partner(out)
    dqkv_o, part, dy, sums_o = attend_back(wqkv, incl, strict, qkv_e, qkv_o, o2, lse2, do2, dh1_2, ho, gb)
    o2_flat = o2.reshape(2 * n, width)

    dm1 = dy.astype(BF16)
    down_go = grad_down(me, 1, g1, g2, dm1, dm2)
    down_got = link.core(down_go)
    down_keep = grad_down(me, 0, g1, g2, dm1, after(dm2, down_go))
    dy = after(dy, down_keep)
    du1, dh1_1, dp1, do1, sums1 = mlp_back(dy, h1, wout, gb, d1, wup, wdown, seq)
    down = link.summing(down_keep, after(down_got, du1))
    up_go = grad_up(me, 1, n2_1, n2_2, du1, du2)
    up_got = link.core(up_go)
    up_keep = grad_up(me, 0, n2_1, n2_2, du1, after(du2, up_go))
    do1 = after(do1, up_keep)
    dqkv_e, gt, sums_e = attend_back_even(wqkv, incl, qkv_e, o1, lse1, do1, o2, lse2, do2, part, dh1_1, dh1_2, x, gb)
    up = link.summing(up_keep, after(up_got, dqkv_e))
    heads = (a_e, a_o, dp1, dp2, dqkv_e, dqkv_o, o1)
    heads_go = grad_heads(me, 1, *heads, o2_flat)
    heads_got = link.core(heads_go)
    heads_keep = grad_heads(me, 0, *heads, after(o2_flat, heads_go))
    head = link.summing(heads_keep, heads_got)
    gt_got = link.partner(gt)
    small = jnp.stack([sums_e[0] + sums_o[0], sums1[0] + sums2[0], sums_e[1] + sums_o[1], sums1[1] + sums2[1], sums_o[2]])
    small = link.small(small)
    for s in (down, up, head):
        s.scatter()
    g_down, g_up, g_head = (s.gather() for s in (down, up, head))
    (g_down,) = unpack(me, *g_down)
    (g_up,) = unpack(me, *g_up)
    g_qkv, g_out = unpack(me, *g_head, heads=True)
    return (out, out_got), (gt, gt_got), (g_qkv, g_out, g_up, g_down), small


def shards(outer, tokens, segments, pass_embed, w_qkv, w_out, w_up, w_down, gain, bias, cotangent):
    ty = lax.axis_index("tensor")
    rows = tokens.shape[0] // 2
    width = tokens.shape[2]
    mine = lambda t: lax.dynamic_slice_in_dim(t, ty * rows, rows, 0)
    x = mine(tokens).reshape(-1, width)
    gb = jnp.concatenate([gain, bias, pass_embed[None]], axis=0)
    link = Link(outer, w_qkv, w_out, w_up, w_down)
    out, gt, grads, small = local_part(x, mine(segments), mine(cotangent), gb, link)
    out = ordered(ty, *out).reshape(cotangent.shape)
    gt = ordered(ty, *gt).reshape(tokens.shape).astype(F32)
    return out, gt, *grads, small[0:2], small[2:4], small[4]


def solution(mesh):
    outer = mesh.shape["dp"] // 4
    fine = Mesh(mesh.devices.reshape(outer, 2, 2, mesh.shape["tensor"]), ("o", "x", "core", "tensor"))
    rows = ROWS_OVER
    placed = (
        P(rows, None, None),
        P(rows, None),
        P(),
        P(None, None, "tensor"),
        P("tensor", None),
        P(None, "tensor"),
        P("tensor", None),
        P(),
        P(),
        P(rows, None, None),
    )

    def body(*args):
        return shards(outer, *args)

    return jax.shard_map(
        body,
        mesh=fine,
        in_specs=placed,
        out_specs=(
            P(rows, None, None),
            P(rows, None, None),
            P(None, None, "tensor"),
            P("tensor", None),
            P(None, "tensor"),
            P("tensor", None),
            P(),
            P(),
            P(),
        ),
        check_vma=False,
    )
```

profile of v0, /device:TPU:0, one launch (start us, length us, event | category | flops | bytes accessed | tf_op | source)
XLA Modules:
  0.0 540.7 jit_solution(2772777846570605488)
XLA Ops:
  0.7 2.2 constant_dynamic-slice_fusion.1
  2.9 3.0 collective-permute-start.9
  5.8 2.0 constant_dynamic-slice_fusion.2
  7.8 1.9 constant_dynamic-slice_fusion.4
  9.7 2.0 collective-permute-start
  17.1 5.5 %attend_first.2 = (bf16[3,512,384]{2,1,0:T(8,128)(2,1)}, bf16[512,384]{1,0:T(8,128)(2,1)}, f32[512,384]{1,0:T(8,128)}) custom-call(bf16[512,768]{1,0:T(8,128)(2,1)} %add_convert_fusion.3.a_ref.ae_ref, bf16[3,768,384]{2,1,0:T(8,128)(2,1)} %w_ref.1, f32[2,256,256]{2,1,0:T(8,128)} %get-tuple-element.129.bias_ref.incl_ref), custom_call_target="tpu_custom_call" | custom-call | flops 1711276032 | tf_op jit(solution)/shard_map/attend_first/pallas_call | solution.py:104
  22.7 22.1 %collective-permute-done.3 = bf16[96,768]{1,0:T(8,128)(2,1)} collective-permute-done((bf16[96,768]{1,0:T(8,128)(2,1)S(1)}, bf16[96,768]{1,0:T(8,128)(2,1)}, u32[]{:S(2)}, u32[]{:S(2)}) %collective-permute-start.3) | collective-permute-done | bytes 147488 | tf_op jit(solution)/shard_map/ppermute | solution.py:53
  46.5 2.2 constant_dynamic-update-slice_fusion.5
  48.7 2.5 constant_dynamic-update-slice_fusion.3
  59.9 8.2 %collective-permute-done.1 = bf16[576,384]{1,0:T(8,128)(2,1)S(1)} collective-permute-done((bf16[576,384]{1,0:T(8,128)(2,1)}, bf16[576,384]{1,0:T(8,128)(2,1)S(1)}, u32[]{:S(2)}, u32[]{:S(2)}) %collective-permute-start.1) | collective-permute-done | bytes 442400 | tf_op jit(solution)/shard_map/ppermute | solution.py:54
  69.4 11.3 %collective-permute-done.10 = bf16[384,768]{1,0:T(8,128)(2,1)S(1)} collective-permute-done((bf16[384,768]{1,0:T(8,128)(2,1)}, bf16[384,768]{1,0:T(8,128)(2,1)S(1)}, u32[]{:S(2)}, u32[]{:S(2)}) %collective-permute-start.10) | collective-permute-done | bytes 589856 | tf_op jit(solution)/shard_map/ppermute | solution.py:54
  83.0 10.0 %collective-permute-done.7 = bf16[192,1536]{1,0:T(8,128)(2,1)S(1)} collective-permute-done((bf16[192,1536]{1,0:T(8,128)(2,1)}, bf16[192,1536]{1,0:T(8,128)(2,1)S(1)}, u32[]{:S(2)}, u32[]{:S(2)}) %collective-permute-start.7) | collective-permute-done | bytes 589856 | tf_op jit(solution)/shard_map/ppermute | solution.py:54
  97.0 5.5 %attend_first.3 = (bf16[3,512,384]{2,1,0:T(8,128)(2,1)}, bf16[512,384]{1,0:T(8,128)(2,1)}, f32[512,384]{1,0:T(8,128)}) custom-call(bf16[512,768]{1,0:T(8,128)(2,1)} %add_convert_fusion.3.a_ref.ae_ref, bf16[3,768,384]{2,1,0:T(8,128)(2,1)} %bitcast.96, f32[2,256,256]{2,1,0:T(8,128)} %get-tuple-element.129.bias_ref.incl_ref), custom_call_target="tpu_custom_call" | custom-call | flops 1711276032 | tf_op jit(solution)/shard_map/attend_first/pallas_call | solution.py:104
  102.5 2.2 constant_dynamic-update-slice_fusion.4.lse1_ref
  104.8 2.6 constant_dynamic-update-slice_fusion.2.qkve_ref
  107.5 2.1 pad_maximum_fusion.2.w_ref
  113.0 2.5 pad_maximum_fusion.1.wdown_ref
  119.0 2.8 pad_maximum_fusion.wup_ref
  121.7 15.9 %mlp_first.1 = (f32[512,768]{1,0:T(8,128)}, bf16[512,768]{1,0:T(8,128)(2,1)}, bf16[512,3072]{1,0:T(8,128)(2,1)}, bf16[512,3072]{1,0:T(8,128)(2,1)}, f32[512,768]{1,0:T(8,128)}, /*index=5*/bf16[512,768]{1,0:T(8,128)(2,1)}) custom-call(bf16[512,768]{1,0:T(8,128)(2,1)} %bitcast.91, bf16[512,768]{1,0:T(8,128)(2,1)} %copy-done.4, ...), custom_call_target="tpu_custom_call" | custom-call | flops 5435817984 | tf_op jit(solution)/shard_map/mlp_first/pallas_call | solution.py:104
  137.6 25.8 %attend_second.1 = (bf16[3,512,768]{2,1,0:T(8,128)(2,1)}, bf16[2,512,768]{2,1,0:T(8,128)(2,1)}, f32[2,512,768]{2,1,0:T(8,128)}) custom-call(bf16[512,768]{1,0:T(8,128)(2,1)} %get-tuple-element.57.a_ref.ao_ref, bf16[3,768,768]{2,1,0:T(8,128)(2,1)} %pad_maximum_fusion.2.w_ref, f32[2,256,256]{2,1,0:T(8,128)} %get-tuple-element.129.bias_ref.incl_ref, ...), custom_call_target="tpu_custom_call" | custom-call | flops 6643777536 | tf_op jit(solution)/shard_map/attend_second/pallas_call | solution.py:104
  163.4 37.8 %mlp_second.1 = (bf16[2,512,768]{2,1,0:T(8,128)(2,1)}, bf16[1024,768]{1,0:T(8,128)(2,1)}, bf16[1024,3072]{1,0:T(8,128)(2,1)}, bf16[1024,3072]{1,0:T(8,128)(2,1)}...) custom-call(bf16[512,768]{1,0:T(8,128)(2,1)} %bitcast.92, ...), custom_call_target="tpu_custom_call" | custom-call | flops 21743271936 | tf_op jit(solution)/shard_map/mlp_second/pallas_call | solution.py:104
  201.2 26.4 %attend_back.1 = (bf16[3,512,768]{2,1,0:T(8,128)(2,1)}, f32[3,512,768]{2,1,0:T(8,128)}, f32[512,768]{1,0:T(8,128)}, f32[3,768]{1,0:T(4,128)}) custom-call(bf16[3,768,768]{2,1,0:T(8,128)(2,1)} %pad_maximum_fusion.2.w_ref, f32[2,256,256]{2,1,0:T(8,128)} %get-tuple-element.129.bias_ref.incl_ref, f32[2,256,256]{2,1,0:T(8,128)} %get-tuple-element.128.strict_ref, ...), custom_call_target="tpu_custom_call" | custom-call | flops 13891534848 | tf_op jit(solution)/shard_map/attend_back/pallas_call | solution.py:104
  227.6 2.4 convert_element_type.187.dm1_ref
  230.0 8.0 %grad_down.2 = bf16[2,8,96,768]{3,2,1,0:T(8,128)(2,1)} custom-call(s32[1]{0:T(128)} %bitcast.30.me_ref, bf16[512,3072]{1,0:T(8,128)(2,1)} %get-tuple-element.69.g1_ref, bf16[1024,3072]{1,0:T(8,128)(2,1)} %get-tuple-element.70.g2_ref, bf16[512,768]{1,0:T(8,128)(2,1)} %convert_element_type.187.dm1_ref, bf16[1024,768]{1,0:T(8,128)(2,1)} %get-tuple-element.72.dm2_ref), custom_call_target="tpu_custom_call" | custom-call | flops 3623878656 | tf_op jit(solution)/shard_map/grad_down/pallas_call | solution.py:697
  238.5 8.0 %grad_down.3 = bf16[2,8,96,768]{3,2,1,0:T(8,128)(2,1)} custom-call(s32[1]{0:T(128)} %bitcast.30.me_ref, bf16[512,3072]{1,0:T(8,128)(2,1)} %get-tuple-element.69.g1_ref, bf16[1024,3072]{1,0:T(8,128)(2,1)} %get-tuple-element.70.g2_ref, bf16[512,768]{1,0:T(8,128)(2,1)} %convert_element_type.187.dm1_ref, bf16[1024,768]{1,0:T(8,128)(2,1)} %get-tuple-element.72.dm2_ref), custom_call_target="tpu_custom_call" | custom-call | flops 3623878656 | tf_op jit(solution)/shard_map/grad_down/pallas_call | solution.py:697
  246.5 15.2 %mlp_back.1 = (bf16[512,3072]{1,0:T(8,128)(2,1)}, f32[512,768]{1,0:T(8,128)}, bf16[512,768]{1,0:T(8,128)(2,1)}, bf16[512,768]{1,0:T(8,128)(2,1)}, f32[2,768]{1,0:T(2,128)}) custom-call(f32[512,768]{1,0:T(8,128)} %get-tuple-element.73.dy_ref, f32[512,768]{1,0:T(8,128)} %get-tuple-element.74.h1_ref, bf16[768,768]{1,0:T(8,128)(2,1)} %pad_maximum_fusion.8.wout_ref, ...), custom_call_target="tpu_custom_call" | custom-call | flops 5435817984 | tf_op jit(solution)/shard_map/mlp_back/pallas_call | solution.py:104
  261.6 9.5 %grad_up.2 = bf16[2,8,48,1536]{3,2,1,0:T(8,128)(2,1)} custom-call(s32[1]{0:T(128)} %bitcast.30.me_ref, bf16[512,768]{1,0:T(8,128)(2,1)} %get-tuple-element.77.n1_ref, bf16[1024,768]{1,0:T(8,128)(2,1)} %get-tuple-element.78.n2_ref, bf16[512,3072]{1,0:T(8,128)(2,1)} %get-tuple-element.79.du1_ref, bf16[1024,3072]{1,0:T(8,128)(2,1)} %get-tuple-element.81.du2_ref), custom_call_target="tpu_custom_call" | custom-call | flops 3623878656 | tf_op jit(solution)/shard_map/grad_up/pallas_call | solution.py:697
  271.2 9.5 %grad_up.3 = bf16[2,8,48,1536]{3,2,1,0:T(8,128)(2,1)} custom-call(s32[1]{0:T(128)} %bitcast.30.me_ref, bf16[512,768]{1,0:T(8,128)(2,1)} %get-tuple-element.77.n1_ref, bf16[1024,768]{1,0:T(8,128)(2,1)} %get-tuple-element.78.n2_ref, bf16[512,3072]{1,0:T(8,128)(2,1)} %get-tuple-element.79.du1_ref, bf16[1024,3072]{1,0:T(8,128)(2,1)} %get-tuple-element.81.du2_ref), custom_call_target="tpu_custom_call" | custom-call | flops 3623878656 | tf_op jit(solution)/shard_map/grad_up/pallas_call | solution.py:697
  280.7 19.7 %attend_back_even.1 = (bf16[3,512,768]{2,1,0:T(8,128)(2,1)}, bf16[512,768]{1,0:T(8,128)(2,1)}, f32[2,768]{1,0:T(2,128)}) custom-call(bf16[3,768,768]{2,1,0:T(8,128)(2,1)} %pad_maximum_fusion.2.w_ref, f32[2,256,256]{2,1,0:T(8,128)} %get-tuple-element.129.bias_ref.incl_ref, bf16[3,512,768]{2,1,0:T(8,128)(2,1)} %constant_dynamic-update-slice_fusion.2.qkve_ref, ...), custom_call_target="tpu_custom_call" | custom-call | flops 5838471168 | tf_op jit(solution)/shard_map/attend_back_even/pallas_call | solution.py:104
  300.4 8.3 %grad_heads.2 = bf16[2,8,48,1536]{3,2,1,0:T(8,128)(2,1)} custom-call(s32[1]{0:T(128)} %bitcast.30.me_ref, bf16[512,768]{1,0:T(8,128)(2,1)} %add_convert_fusion.3.a_ref.ae_ref, bf16[512,768]{1,0:T(8,128)(2,1)} %get-tuple-element.57.a_ref.ao_ref, bf16[512,768]{1,0:T(8,128)(2,1)} %get-tuple-element.86.dp1_ref, bf16[1024,768]{1,0:T(8,128)(2,1)} %get-tuple-element.87.dp2_ref, ...), custom_call_target="tpu_custom_call" | custom-call | flops 2717908992 | tf_op jit(solution)/shard_map/grad_heads/pallas_call | solution.py:697
  309.2 2.9 fusion.7
  313.6 2.6 fusion.6
  316.7 8.3 %grad_heads.3 = bf16[2,8,48,1536]{3,2,1,0:T(8,128)(2,1)} custom-call(s32[1]{0:T(128)} %bitcast.30.me_ref, bf16[512,768]{1,0:T(8,128)(2,1)} %add_convert_fusion.3.a_ref.ae_ref, bf16[512,768]{1,0:T(8,128)(2,1)} %get-tuple-element.57.a_ref.ao_ref, bf16[512,768]{1,0:T(8,128)(2,1)} %get-tuple-element.86.dp1_ref, bf16[1024,768]{1,0:T(8,128)(2,1)} %get-tuple-element.87.dp2_ref, ...), custom_call_target="tpu_custom_call" | custom-call | flops 2717908992 | tf_op jit(solution)/shard_map/grad_heads/pallas_call | solution.py:697
  325.1 1.9 fusion.5
  329.1 12.1 %collective-permute-done.33 = bf16[8,96,768]{2,1,0:T(8,128)(2,1)} collective-permute-done((bf16[8,96,768]{2,1,0:T(8,128)(2,1)}, bf16[8,96,768]{2,1,0:T(8,128)(2,1)}, u32[]{:S(2)}, u32[]{:S(2)}) %collective-permute-start.33) | collective-permute-done | bytes 1179680 | tf_op jit(solution)/shard_map/ppermute | solution.py:906
  341.2 2.2 fusion
  344.2 22.3 %collective-permute-done.24 = bf16[8,48,1536]{2,1,0:T(8,128)(2,1)} collective-permute-done((bf16[8,48,1536]{2,1,0:T(8,128)(2,1)}, bf16[8,48,1536]{2,1,0:T(8,128)(2,1)}, u32[]{:S(2)}, u32[]{:S(2)}) %collective-permute-start.24) | collective-permute-done | bytes 1179680 | tf_op jit(solution)/shard_map/ppermute | solution.py:906
  366.5 2.2 fusion.1
  369.5 22.1 %collective-permute-done.15 = bf16[8,48,1536]{2,1,0:T(8,128)(2,1)S(1)} collective-permute-done((bf16[8,48,1536]{2,1,0:T(8,128)(2,1)S(1)}, bf16[8,48,1536]{2,1,0:T(8,128)(2,1)S(1)}, u32[]{:S(2)}, u32[]{:S(2)}) %collective-permute-start.15) | collective-permute-done | bytes 1179680 | tf_op jit(solution)/shard_map/ppermute | solution.py:906
  396.7 10.2 %collective-permute-done.16 = bf16[4,48,1536]{2,1,0:T(8,128)(2,1)S(1)} collective-permute-done((bf16[4,48,1536]{2,1,0:T(8,128)(2,1)S(1)}, bf16[4,48,1536]{2,1,0:T(8,128)(2,1)S(1)}, u32[]{:S(2)}, u32[]{:S(2)}) %collective-permute-start.16) | collective-permute-done | bytes 589856 | tf_op jit(solution)/shard_map/ppermute | solution.py:32
  408.8 2.7 collective-permute-start.36
  411.9 7.4 %collective-permute-done.17 = bf16[2,48,1536]{2,1,0:T(8,128)(2,1)S(1)} collective-permute-done((bf16[2,48,1536]{2,1,0:T(8,128)(2,1)S(1)}, bf16[2,48,1536]{2,1,0:T(8,128)(2,1)S(1)}, u32[]{:S(2)}, u32[]{:S(2)}) %collective-permute-start.17) | collective-permute-done | bytes 294944 | tf_op jit(solution)/shard_map/ppermute | solution.py:32
  422.5 9.0 %collective-permute-done.27 = bf16[1,48,1536]{2,1,0:T(8,128)(2,1)S(1)} collective-permute-done((bf16[1,48,1536]{2,1,0:T(8,128)(2,1)S(1)}, bf16[1,48,1536]{2,1,0:T(8,128)(2,1)S(1)}, u32[]{:S(2)}, u32[]{:S(2)}) %collective-permute-start.27) | collective-permute-done | bytes 147488 | tf_op jit(solution)/shard_map/ppermute | solution.py:32
  431.7 4.6 collective-permute-done.18
  436.4 6.2 %collective-permute-done.37 = bf16[1,96,768]{2,1,0:T(8,128)(2,1)S(1)} collective-permute-done((bf16[1,96,768]{2,1,0:T(8,128)(2,1)S(1)}, bf16[1,96,768]{2,1,0:T(8,128)(2,1)S(1)}, u32[]{:S(2)}, u32[]{:S(2)}) %collective-permute-start.37) | collective-permute-done | bytes 147488 | tf_op jit(solution)/shard_map/ppermute | solution.py:32
  442.7 3.1 collective-permute-done.28
  446.0 2.3 collective-permute-done.19
  448.5 6.2 %collective-permute-done.38 = bf16[2,96,768]{2,1,0:T(8,128)(2,1)S(1)} collective-permute-done((bf16[2,96,768]{2,1,0:T(8,128)(2,1)S(1)}, bf16[2,96,768]{2,1,0:T(8,128)(2,1)S(1)}, u32[]{:S(2)}, u32[]{:S(2)}) %collective-permute-start.38) | collective-permute-done | bytes 294944 | tf_op jit(solution)/shard_map/ppermute | solution.py:32
  454.8 6.2 %collective-permute-done.29 = bf16[2,48,1536]{2,1,0:T(8,128)(2,1)S(1)} collective-permute-done((bf16[2,48,1536]{2,1,0:T(8,128)(2,1)S(1)}, bf16[2,48,1536]{2,1,0:T(8,128)(2,1)S(1)}, u32[]{:S(2)}, u32[]{:S(2)}) %collective-permute-start.29) | collective-permute-done | bytes 294944 | tf_op jit(solution)/shard_map/ppermute | solution.py:32
  461.8 5.3 collective-permute-done.20
  470.9 2.3 collective-permute-done.42
  473.2 2.0 collective-permute-start.43
  475.2 20.5 %collective-permute-done.43 = f32[5,768]{1,0:T(8,128)S(1)} collective-permute-done((f32[5,768]{1,0:T(8,128)S(1)}, f32[5,768]{1,0:T(8,128)S(1)}, u32[]{:S(2)}, u32[]{:S(2)}) %collective-permute-start.43) | collective-permute-done | bytes 15392 | tf_op jit(solution)/shard_map/ppermute | solution.py:32
  495.7 3.8 collective-permute-done.44
  499.9 4.4 collective-permute-done.45
  507.1 2.5 pad_maximum_fusion.12.mine_ref
  509.8 2.2 pad_maximum_fusion.11.mine_ref
  513.6 7.2 %collective-permute-done.13 = bf16[512,768]{1,0:T(8,128)(2,1)S(1)} collective-permute-done((bf16[512,768]{1,0:T(8,128)(2,1)}, bf16[512,768]{1,0:T(8,128)(2,1)S(1)}, u32[]{:S(2)}, u32[]{:S(2)}) %collective-permute-start.13) | collective-permute-done | bytes 786464 | tf_op jit(solution)/shard_map/ppermute | solution.py:959
  522.2 1.9 convert.1
  524.1 2.1 select_bitcast_fusion.1
  526.2 1.9 pad_maximum_fusion.3
  528.2 4.0 unpack.5
  532.1 4.1 unpack.4
  536.3 4.0 unpack.3
  (188 shorter events, 59.0 us)
Async XLA Ops:
  0.6 53.0 %copy-start = (bf16[4,512,768]{2,1,0:T(8,128)(2,1)S(1)}, bf16[4,512,768]{2,1,0:T(8,128)(2,1)}, u32[]{:S(2)}) copy-start(bf16[4,512,768]{2,1,0:T(8,128)(2,1)} %param.19) | copy-start | bytes 9437188
  2.9 52.8 %collective-permute-start.9 = (bf16[384,768]{1,0:T(8,128)(2,1)}, bf16[384,768]{1,0:T(8,128)(2,1)}, u32[]{:S(2)}, u32[]{:S(2)}) collective-permute-start(bf16[384,768]{1,0:T(8,128)(2,1)} %constant_dynamic-slice_fusion.1), channel_id=1, source_target_pairs={{0,1},{1,0},{2,3},{3,2},{4,5},{5,4},{6,7},{7,6},{8,9},{9,8},{10,11... | collective-permute-start | bytes 1769480 | tf_op jit(solution)/shard_map/ppermute | solution.py:53
  7.8 50.2 %collective-permute-start.6 = (bf16[192,1536]{1,0:T(8,128)(2,1)}, bf16[192,1536]{1,0:T(8,128)(2,1)}, u32[]{:S(2)}, u32[]{:S(2)}) collective-permute-start(bf16[192,1536]{1,0:T(8,128)(2,1)} %constant_dynamic-slice_fusion.2), channel_id=1, source_target_pairs={{0,1},{1,0},{2,3},{3,2},{4,5},{5,4},{6,7},{7,6},{8,9},{9,8},{10,11... | collective-permute-start | bytes 1769480 | tf_op jit(solution)/shard_map/ppermute | solution.py:53
  9.7 4.9 copy-start.24
  9.7 4.9 copy-start.17
  9.7 4.9 copy-start.18
  9.7 45.2 %collective-permute-start = (bf16[576,384]{1,0:T(8,128)(2,1)}, bf16[576,384]{1,0:T(8,128)(2,1)}, u32[]{:S(2)}, u32[]{:S(2)}) collective-permute-start(bf16[576,384]{1,0:T(8,128)(2,1)} %constant_dynamic-slice_fusion.4), channel_id=1, source_target_pairs={{0,1},{1,0},{2,3},{3,2},{4,5},{5,4},{6,7},{7,6},{8,9},{9,8},{10,11... | collective-permute-start | bytes 1327112 | tf_op jit(solution)/shard_map/ppermute | solution.py:53
  12.7 32.0 %collective-permute-start.3 = (bf16[96,768]{1,0:T(8,128)(2,1)S(1)}, bf16[96,768]{1,0:T(8,128)(2,1)}, u32[]{:S(2)}, u32[]{:S(2)}) collective-permute-start(bf16[96,768]{1,0:T(8,128)(2,1)S(1)} %constant_dynamic-slice_fusion.3), channel_id=1, source_target_pairs={{0,1},{1,0},{2,3},{3,2},{4,5},{5,4},{6,7},{7,6},{8,9},{9,8},{10,11... | collective-permute-start | bytes 442376 | tf_op jit(solution)/shard_map/ppermute | solution.py:53
  14.2 2.9 copy-start.2
  44.7 6.4 %collective-permute-start.4 = (bf16[96,768]{1,0:T(8,128)(2,1)}, bf16[96,768]{1,0:T(8,128)(2,1)S(1)}, u32[]{:S(2)}, u32[]{:S(2)}) collective-permute-start(bf16[96,768]{1,0:T(8,128)(2,1)} %collective-permute-done.3), channel_id=1, source_target_pairs={{0,4},{4,0},{1,5},{5,1},{2,6},{6,2},{3,7},{7,3},{8,12},{12,8},{9,1... | collective-permute-start | bytes 442376 | tf_op jit(solution)/shard_map/ppermute | solution.py:54
  48.6 3.6 copy-start.15
  52.1 4.9 collective-permute-start.5
  55.0 3.9 copy-start.14
  55.0 13.2 %collective-permute-start.1 = (bf16[576,384]{1,0:T(8,128)(2,1)}, bf16[576,384]{1,0:T(8,128)(2,1)S(1)}, u32[]{:S(2)}, u32[]{:S(2)}) collective-permute-start(bf16[576,384]{1,0:T(8,128)(2,1)} %collective-permute-done), channel_id=1, source_target_pairs={{0,4},{4,0},{1,5},{5,1},{2,6},{6,2},{3,7},{7,3},{8,12},{12,8},{9,1... | collective-permute-start | bytes 1327112 | tf_op jit(solution)/shard_map/ppermute | solution.py:54
  55.6 25.1 %collective-permute-start.10 = (bf16[384,768]{1,0:T(8,128)(2,1)}, bf16[384,768]{1,0:T(8,128)(2,1)S(1)}, u32[]{:S(2)}, u32[]{:S(2)}) collective-permute-start(bf16[384,768]{1,0:T(8,128)(2,1)} %collective-permute-done.9), channel_id=1, source_target_pairs={{0,4},{4,0},{1,5},{5,1},{2,6},{6,2},{3,7},{7,3},{8,12},{12,8},{9,1... | collective-permute-start | bytes 1769480 | tf_op jit(solution)/shard_map/ppermute | solution.py:54
  58.1 34.9 %collective-permute-start.7 = (bf16[192,1536]{1,0:T(8,128)(2,1)}, bf16[192,1536]{1,0:T(8,128)(2,1)S(1)}, u32[]{:S(2)}, u32[]{:S(2)}) collective-permute-start(bf16[192,1536]{1,0:T(8,128)(2,1)} %collective-permute-done.6), channel_id=1, source_target_pairs={{0,4},{4,0},{1,5},{5,1},{2,6},{6,2},{3,7},{7,3},{8,12},{12,8},{9,1... | collective-permute-start | bytes 1769480 | tf_op jit(solution)/shard_map/ppermute | solution.py:54
  69.3 25.9 %collective-permute-start.2 = (bf16[1152,384]{1,0:T(8,128)(2,1)S(1)}, bf16[1152,384]{1,0:T(8,128)(2,1)S(1)}, u32[]{:S(2)}, u32[]{:S(2)}) collective-permute-start(bf16[1152,384]{1,0:T(8,128)(2,1)S(1)} %bitcast.99), channel_id=1, source_target_pairs={{0,2},{2,0},{1,3},{3,1},{4,6},{6,4},{5,7},{7,5},{8,10},{10,8},{9,1... | collective-permute-start | bytes 2654216 | tf_op jit(solution)/shard_map/ppermute | solution.py:55
  83.0 26.5 %collective-permute-start.11 = (bf16[768,768]{1,0:T(8,128)(2,1)}, bf16[768,768]{1,0:T(8,128)(2,1)}, u32[]{:S(2)}, u32[]{:S(2)}) collective-permute-start(bf16[768,768]{1,0:T(8,128)(2,1)} %bitcast.22), channel_id=1, source_target_pairs={{0,2},{2,0},{1,3},{3,1},{4,6},{6,4},{5,7},{7,5},{8,10},{10,8},{9,1... | collective-permute-start | bytes 3538952 | tf_op jit(solution)/shard_map/ppermute | solution.py:55
  95.3 20.2 %collective-permute-start.8 = (bf16[384,1536]{1,0:T(8,128)(2,1)}, bf16[384,1536]{1,0:T(8,128)(2,1)}, u32[]{:S(2)}, u32[]{:S(2)}) collective-permute-start(bf16[384,1536]{1,0:T(8,128)(2,1)} %bitcast.16), channel_id=1, source_target_pairs={{0,2},{2,0},{1,3},{3,1},{4,6},{6,4},{5,7},{7,5},{8,10},{10,8},{9,1... | collective-permute-start | bytes 3538952 | tf_op jit(solution)/shard_map/ppermute | solution.py:55
  102.5 4.9 copy-start.13
  238.0 71.2 %collective-permute-start.32 = (bf16[2,8,96,768]{3,2,1,0:T(8,128)(2,1)}, bf16[2,8,96,768]{3,2,1,0:T(8,128)(2,1)}, u32[]{:S(2)}, u32[]{:S(2)}) collective-permute-start(bf16[2,8,96,768]{3,2,1,0:T(8,128)(2,1)} %grad_down.2), channel_id=1, source_target_pairs={{0,2},{2,0},{1,3},{3,1},{4,6},{6,4},{5,7},{7,5},{8,10},{10,8},{9,1... | collective-permute-start | bytes 7077896 | tf_op jit(solution)/shard_map/ppermute | solution.py:898
  271.2 42.4 %collective-permute-start.23 = (bf16[2,8,48,1536]{3,2,1,0:T(8,128)(2,1)}, bf16[2,8,48,1536]{3,2,1,0:T(8,128)(2,1)}, u32[]{:S(2)}, u32[]{:S(2)}) collective-permute-start(bf16[2,8,48,1536]{3,2,1,0:T(8,128)(2,1)} %grad_up.2), channel_id=1, source_target_pairs={{0,2},{2,0},{1,3},{3,1},{4,6},{6,4},{5,7},{7,5},{8,10},{10,8},{9,1... | collective-permute-start | bytes 7077896 | tf_op jit(solution)/shard_map/ppermute | solution.py:898
  300.4 8.8 %copy-start.5 = (bf16[2,8,96,768]{3,2,1,0:T(8,128)(2,1)S(1)}, bf16[2,8,96,768]{3,2,1,0:T(8,128)(2,1)}, u32[]{:S(2)}) copy-start(bf16[2,8,96,768]{3,2,1,0:T(8,128)(2,1)} %grad_down.3) | copy-start | bytes 7077892
  308.7 4.9 copy-start.6
  308.7 16.3 %collective-permute-start.14 = (bf16[2,8,48,1536]{3,2,1,0:T(8,128)(2,1)}, bf16[2,8,48,1536]{3,2,1,0:T(8,128)(2,1)}, u32[]{:S(2)}, u32[]{:S(2)}) collective-permute-start(bf16[2,8,48,1536]{3,2,1,0:T(8,128)(2,1)} %grad_heads.2), channel_id=1, source_target_pairs={{0,2},{2,0},{1,3},{3,1},{4,6},{6,4},{5,7},{7,5},{8,10},{10,8},{9,1... | collective-permute-start | bytes 7077896 | tf_op jit(solution)/shard_map/ppermute | solution.py:898
  312.0 29.1 %collective-permute-start.33 = (bf16[8,96,768]{2,1,0:T(8,128)(2,1)}, bf16[8,96,768]{2,1,0:T(8,128)(2,1)}, u32[]{:S(2)}, u32[]{:S(2)}) collective-permute-start(bf16[8,96,768]{2,1,0:T(8,128)(2,1)} %fusion.7), channel_id=1, source_target_pairs={{0,1},{1,0},{2,3},{3,2},{4,5},{5,4},{6,7},{7,6},{8,9},{9,8},{10,11... | collective-permute-start | bytes 3538952 | tf_op jit(solution)/shard_map/ppermute | solution.py:906
  316.2 50.3 %collective-permute-start.24 = (bf16[8,48,1536]{2,1,0:T(8,128)(2,1)}, bf16[8,48,1536]{2,1,0:T(8,128)(2,1)}, u32[]{:S(2)}, u32[]{:S(2)}) collective-permute-start(bf16[8,48,1536]{2,1,0:T(8,128)(2,1)} %fusion.6), channel_id=1, source_target_pairs={{0,1},{1,0},{2,3},{3,2},{4,5},{5,4},{6,7},{7,6},{8,9},{9,8},{10,11... | collective-permute-start | bytes 3538952 | tf_op jit(solution)/shard_map/ppermute | solution.py:906
  325.0 4.1 copy-start.19
  325.0 4.0 copy-start.22
  327.0 64.7 %collective-permute-start.15 = (bf16[8,48,1536]{2,1,0:T(8,128)(2,1)S(1)}, bf16[8,48,1536]{2,1,0:T(8,128)(2,1)S(1)}, u32[]{:S(2)}, u32[]{:S(2)}) collective-permute-start(bf16[8,48,1536]{2,1,0:T(8,128)(2,1)S(1)} %fusion.5), channel_id=1, source_target_pairs={{0,1},{1,0},{2,3},{3,2},{4,5},{5,4},{6,7},{7,6},{8,9},{9,8},{10,11... | collective-permute-start | bytes 3538952 | tf_op jit(solution)/shard_map/ppermute | solution.py:906
  328.6 195.6 %collective-permute-start.12 = (bf16[2,512,768]{2,1,0:T(8,128)(2,1)}, bf16[2,512,768]{2,1,0:T(8,128)(2,1)}, u32[]{:S(2)}, u32[]{:S(2)}) collective-permute-start(bf16[2,512,768]{2,1,0:T(8,128)(2,1)} %get-tuple-element.63), channel_id=1, source_target_pairs={{0,1},{1,0},{2,3},{3,2},{4,5},{5,4},{6,7},{7,6},{8,9},{9,8},{10,11... | collective-permute-start | bytes 4718600 | tf_op jit(solution)/shard_map/ppermute | solution.py:959
  341.2 25.3 %copy-start.7 = (bf16[2,8,48,1536]{3,2,1,0:T(8,128)(2,1)S(1)}, bf16[2,8,48,1536]{3,2,1,0:T(8,128)(2,1)}, u32[]{:S(2)}) copy-start(bf16[2,8,48,1536]{3,2,1,0:T(8,128)(2,1)} %grad_up.3) | copy-start | bytes 7077892
  343.5 50.7 %collective-permute-start.34 = (bf16[4,96,768]{2,1,0:T(8,128)(2,1)S(1)}, bf16[4,96,768]{2,1,0:T(8,128)(2,1)S(1)}, u32[]{:S(2)}, u32[]{:S(2)}) collective-permute-start(bf16[4,96,768]{2,1,0:T(8,128)(2,1)S(1)} %slice.197), channel_id=1, source_target_pairs={{0,4},{4,0},{1,5},{5,1},{2,6},{6,2},{3,7},{7,3},{8,12},{12,8},{9,1... | collective-permute-start | bytes 1769480 | tf_op jit(solution)/shard_map/ppermute | solution.py:32
  366.5 25.2 %copy-start.8 = (bf16[2,8,48,1536]{3,2,1,0:T(8,128)(2,1)S(1)}, bf16[2,8,48,1536]{3,2,1,0:T(8,128)(2,1)}, u32[]{:S(2)}) copy-start(bf16[2,8,48,1536]{3,2,1,0:T(8,128)(2,1)} %grad_heads.3) | copy-start | bytes 7077892
  368.8 27.2 %collective-permute-start.25 = (bf16[4,48,1536]{2,1,0:T(8,128)(2,1)S(1)}, bf16[4,48,1536]{2,1,0:T(8,128)(2,1)S(1)}, u32[]{:S(2)}, u32[]{:S(2)}) collective-permute-start(bf16[4,48,1536]{2,1,0:T(8,128)(2,1)S(1)} %slice.189), channel_id=1, source_target_pairs={{0,4},{4,0},{1,5},{5,1},{2,6},{6,2},{3,7},{7,3},{8,12},{12,8},{9,1... | collective-permute-start | bytes 1769480 | tf_op jit(solution)/shard_map/ppermute | solution.py:32
  393.4 13.4 %collective-permute-start.16 = (bf16[4,48,1536]{2,1,0:T(8,128)(2,1)S(1)}, bf16[4,48,1536]{2,1,0:T(8,128)(2,1)S(1)}, u32[]{:S(2)}, u32[]{:S(2)}) collective-permute-start(bf16[4,48,1536]{2,1,0:T(8,128)(2,1)S(1)} %slice.181), channel_id=1, source_target_pairs={{0,4},{4,0},{1,5},{5,1},{2,6},{6,2},{3,7},{7,3},{8,12},{12,8},{9,1... | collective-permute-start | bytes 1769480 | tf_op jit(solution)/shard_map/ppermute | solution.py:32
  394.4 14.3 %collective-permute-start.35 = (bf16[2,96,768]{2,1,0:T(8,128)(2,1)S(1)}, bf16[2,96,768]{2,1,0:T(8,128)(2,1)S(1)}, u32[]{:S(2)}, u32[]{:S(2)}) collective-permute-start(bf16[2,96,768]{2,1,0:T(8,128)(2,1)S(1)} %slice.199), channel_id=1, source_target_pairs={{0,8},{8,0},{16,24},{24,16},{1,9},{9,1},{17,25},{25,17},{2,10},{10... | collective-permute-start | bytes 884744 | tf_op jit(solution)/shard_map/ppermute | solution.py:32
  396.2 15.3 %collective-permute-start.26 = (bf16[2,48,1536]{2,1,0:T(8,128)(2,1)S(1)}, bf16[2,48,1536]{2,1,0:T(8,128)(2,1)S(1)}, u32[]{:S(2)}, u32[]{:S(2)}) collective-permute-start(bf16[2,48,1536]{2,1,0:T(8,128)(2,1)S(1)} %slice.191), channel_id=1, source_target_pairs={{0,8},{8,0},{16,24},{24,16},{1,9},{9,1},{17,25},{25,17},{2,10},{10... | collective-permute-start | bytes 884744 | tf_op jit(solution)/shard_map/ppermute | solution.py:32
  407.1 12.3 %collective-permute-start.17 = (bf16[2,48,1536]{2,1,0:T(8,128)(2,1)S(1)}, bf16[2,48,1536]{2,1,0:T(8,128)(2,1)S(1)}, u32[]{:S(2)}, u32[]{:S(2)}) collective-permute-start(bf16[2,48,1536]{2,1,0:T(8,128)(2,1)S(1)} %slice.183), channel_id=1, source_target_pairs={{0,8},{8,0},{16,24},{24,16},{1,9},{9,1},{17,25},{25,17},{2,10},{10... | collective-permute-start | bytes 884744 | tf_op jit(solution)/shard_map/ppermute | solution.py:32
  408.8 12.1 %collective-permute-start.36 = (bf16[1,96,768]{2,1,0:T(8,128)(2,1)S(1)}, bf16[1,96,768]{2,1,0:T(8,128)(2,1)S(1)}, u32[]{:S(2)}, u32[]{:S(2)}) collective-permute-start(bf16[1,96,768]{2,1,0:T(8,128)(2,1)S(1)} %slice.201), channel_id=1, source_target_pairs={{0,16},{8,24},{16,0},{24,8},{1,17},{9,25},{17,1},{25,9},{2,18},{10... | collective-permute-start | bytes 442376 | tf_op jit(solution)/shard_map/ppermute | solution.py:32
  411.5 20.0 %collective-permute-start.27 = (bf16[1,48,1536]{2,1,0:T(8,128)(2,1)S(1)}, bf16[1,48,1536]{2,1,0:T(8,128)(2,1)S(1)}, u32[]{:S(2)}, u32[]{:S(2)}) collective-permute-start(bf16[1,48,1536]{2,1,0:T(8,128)(2,1)S(1)} %slice.193), channel_id=1, source_target_pairs={{0,16},{8,24},{16,0},{24,8},{1,17},{9,25},{17,1},{25,9},{2,18},{10... | collective-permute-start | bytes 442376 | tf_op jit(solution)/shard_map/ppermute | solution.py:32
  419.4 16.8 %collective-permute-start.18 = (bf16[1,48,1536]{2,1,0:T(8,128)(2,1)S(1)}, bf16[1,48,1536]{2,1,0:T(8,128)(2,1)S(1)}, u32[]{:S(2)}, u32[]{:S(2)}) collective-permute-start(bf16[1,48,1536]{2,1,0:T(8,128)(2,1)S(1)} %slice.185), channel_id=1, source_target_pairs={{0,16},{8,24},{16,0},{24,8},{1,17},{9,25},{17,1},{25,9},{2,18},{10... | collective-permute-start | bytes 442376 | tf_op jit(solution)/shard_map/ppermute | solution.py:32
  421.0 21.6 %collective-permute-start.37 = (bf16[1,96,768]{2,1,0:T(8,128)(2,1)S(1)}, bf16[1,96,768]{2,1,0:T(8,128)(2,1)S(1)}, u32[]{:S(2)}, u32[]{:S(2)}) collective-permute-start(bf16[1,96,768]{2,1,0:T(8,128)(2,1)S(1)} %add_convert_fusion.10), channel_id=1, source_target_pairs={{0,16},{8,24},{16,0},{24,8},{1,17},{9,25},{17,1},{25,9},{2,18},{10... | collective-permute-start | bytes 442376 | tf_op jit(solution)/shard_map/ppermute | solution.py:32
  431.6 14.3 %collective-permute-start.28 = (bf16[1,48,1536]{2,1,0:T(8,128)(2,1)S(1)}, bf16[1,48,1536]{2,1,0:T(8,128)(2,1)S(1)}, u32[]{:S(2)}, u32[]{:S(2)}) collective-permute-start(bf16[1,48,1536]{2,1,0:T(8,128)(2,1)S(1)} %add_convert_fusion.11), channel_id=1, source_target_pairs={{0,16},{8,24},{16,0},{24,8},{1,17},{9,25},{17,1},{25,9},{2,18},{10... | collective-permute-start | bytes 442376 | tf_op jit(solution)/shard_map/ppermute | solution.py:32
  436.3 12.0 %collective-permute-start.19 = (bf16[1,48,1536]{2,1,0:T(8,128)(2,1)S(1)}, bf16[1,48,1536]{2,1,0:T(8,128)(2,1)S(1)}, u32[]{:S(2)}, u32[]{:S(2)}) collective-permute-start(bf16[1,48,1536]{2,1,0:T(8,128)(2,1)S(1)} %add_convert_fusion.12), channel_id=1, source_target_pairs={{0,16},{8,24},{16,0},{24,8},{1,17},{9,25},{17,1},{25,9},{2,18},{10... | collective-permute-start | bytes 442376 | tf_op jit(solution)/shard_map/ppermute | solution.py:32
  442.6 12.0 %collective-permute-start.38 = (bf16[2,96,768]{2,1,0:T(8,128)(2,1)S(1)}, bf16[2,96,768]{2,1,0:T(8,128)(2,1)S(1)}, u32[]{:S(2)}, u32[]{:S(2)}) collective-permute-start(bf16[2,96,768]{2,1,0:T(8,128)(2,1)S(1)} %pad_maximum_fusion.22), channel_id=1, source_target_pairs={{0,8},{8,0},{16,24},{24,16},{1,9},{9,1},{17,25},{25,17},{2,10},{10... | collective-permute-start | bytes 884744 | tf_op jit(solution)/shard_map/ppermute | solution.py:32
  445.9 15.1 %collective-permute-start.29 = (bf16[2,48,1536]{2,1,0:T(8,128)(2,1)S(1)}, bf16[2,48,1536]{2,1,0:T(8,128)(2,1)S(1)}, u32[]{:S(2)}, u32[]{:S(2)}) collective-permute-start(bf16[2,48,1536]{2,1,0:T(8,128)(2,1)S(1)} %pad_maximum_fusion.21), channel_id=1, source_target_pairs={{0,8},{8,0},{16,24},{24,16},{1,9},{9,1},{17,25},{25,17},{2,10},{10... | collective-permute-start | bytes 884744 | tf_op jit(solution)/shard_map/ppermute | solution.py:32
  448.3 19.7 %copy-start.20 = (f32[2,768]{1,0:T(2,128)S(1)}, f32[2,768]{1,0:T(2,128)}, u32[]{:S(2)}) copy-start(f32[2,768]{1,0:T(2,128)} %get-tuple-element.98) | copy-start | bytes 18436
  448.4 19.7 %copy-start.21 = (f32[2,768]{1,0:T(2,128)S(1)}, f32[2,768]{1,0:T(2,128)}, u32[]{:S(2)}) copy-start(f32[2,768]{1,0:T(2,128)} %get-tuple-element.97) | copy-start | bytes 18436
  448.4 18.8 %collective-permute-start.20 = (bf16[2,48,1536]{2,1,0:T(8,128)(2,1)S(1)}, bf16[2,48,1536]{2,1,0:T(8,128)(2,1)S(1)}, u32[]{:S(2)}, u32[]{:S(2)}) collective-permute-start(bf16[2,48,1536]{2,1,0:T(8,128)(2,1)S(1)} %pad_maximum_fusion.20), channel_id=1, source_target_pairs={{0,8},{8,0},{16,24},{24,16},{1,9},{9,1},{17,25},{25,17},{2,10},{10... | collective-permute-start | bytes 884744 | tf_op jit(solution)/shard_map/ppermute | solution.py:32
  454.7 51.1 %collective-permute-start.39 = (bf16[4,96,768]{2,1,0:T(8,128)(2,1)S(1)}, bf16[4,96,768]{2,1,0:T(8,128)(2,1)}, u32[]{:S(2)}, u32[]{:S(2)}) collective-permute-start(bf16[4,96,768]{2,1,0:T(8,128)(2,1)S(1)} %pad_maximum_fusion.18), channel_id=1, source_target_pairs={{0,4},{4,0},{1,5},{5,1},{2,6},{6,2},{3,7},{7,3},{8,12},{12,8},{9,1... | collective-permute-start | bytes 1769480 | tf_op jit(solution)/shard_map/ppermute | solution.py:32
  461.8 45.3 %collective-permute-start.30 = (bf16[4,48,1536]{2,1,0:T(8,128)(2,1)}, bf16[4,48,1536]{2,1,0:T(8,128)(2,1)}, u32[]{:S(2)}, u32[]{:S(2)}) collective-permute-start(bf16[4,48,1536]{2,1,0:T(8,128)(2,1)} %pad_maximum_fusion.17), channel_id=1, source_target_pairs={{0,4},{4,0},{1,5},{5,1},{2,6},{6,2},{3,7},{7,3},{8,12},{12,8},{9,1... | collective-permute-start | bytes 1769480 | tf_op jit(solution)/shard_map/ppermute | solution.py:32
  468.0 41.7 %collective-permute-start.21 = (bf16[4,48,1536]{2,1,0:T(8,128)(2,1)}, bf16[4,48,1536]{2,1,0:T(8,128)(2,1)}, u32[]{:S(2)}, u32[]{:S(2)}) collective-permute-start(bf16[4,48,1536]{2,1,0:T(8,128)(2,1)} %pad_maximum_fusion.16), channel_id=1, source_target_pairs={{0,4},{4,0},{1,5},{5,1},{2,6},{6,2},{3,7},{7,3},{8,12},{12,8},{9,1... | collective-permute-start | bytes 1769480 | tf_op jit(solution)/shard_map/ppermute | solution.py:32
  468.1 1.3 collective-permute-start.41
  469.4 3.8 collective-permute-start.42
  473.2 22.5 %collective-permute-start.43 = (f32[5,768]{1,0:T(8,128)S(1)}, f32[5,768]{1,0:T(8,128)S(1)}, u32[]{:S(2)}, u32[]{:S(2)}) collective-permute-start(f32[5,768]{1,0:T(8,128)S(1)} %add.218), channel_id=1, source_target_pairs={{0,4},{4,0},{1,5},{5,1},{2,6},{6,2},{3,7},{7,3},{8,12},{12,8},{9,1... | collective-permute-start | bytes 46088 | tf_op jit(solution)/shard_map/ppermute | solution.py:32
  495.7 3.8 collective-permute-start.44
  499.6 4.7 collective-permute-start.45
  504.3 16.5 %collective-permute-start.13 = (bf16[512,768]{1,0:T(8,128)(2,1)}, bf16[512,768]{1,0:T(8,128)(2,1)S(1)}, u32[]{:S(2)}, u32[]{:S(2)}) collective-permute-start(bf16[512,768]{1,0:T(8,128)(2,1)} %get-tuple-element.85), channel_id=1, source_target_pairs={{0,1},{1,0},{2,3},{3,2},{4,5},{5,4},{6,7},{7,6},{8,9},{9,8},{10,11... | collective-permute-start | bytes 2359304 | tf_op jit(solution)/shard_map/ppermute | solution.py:959
  507.0 5.0 copy-start.10
  507.0 21.2 %collective-permute-start.40 = (bf16[8,96,768]{2,1,0:T(8,128)(2,1)S(1)}, bf16[8,96,768]{2,1,0:T(8,128)(2,1)}, u32[]{:S(2)}, u32[]{:S(2)}) collective-permute-start(bf16[8,96,768]{2,1,0:T(8,128)(2,1)S(1)} %pad_maximum_fusion.13.mine_ref), channel_id=1, source_target_pairs={{0,2},{2,0},{1,3},{3,1},{4,6},{6,4},{5,7},{7,5},{8,10},{10,8},{9,1... | collective-permute-start | bytes 3538952 | tf_op jit(solution)/shard_map/ppermute | solution.py:898
  509.6 22.5 %collective-permute-start.31 = (bf16[8,48,1536]{2,1,0:T(8,128)(2,1)}, bf16[8,48,1536]{2,1,0:T(8,128)(2,1)}, u32[]{:S(2)}, u32[]{:S(2)}) collective-permute-start(bf16[8,48,1536]{2,1,0:T(8,128)(2,1)} %pad_maximum_fusion.12.mine_ref), channel_id=1, source_target_pairs={{0,2},{2,0},{1,3},{3,1},{4,6},{6,4},{5,7},{7,5},{8,10},{10,8},{9,1... | collective-permute-start | bytes 3538952 | tf_op jit(solution)/shard_map/ppermute | solution.py:898
  512.0 24.3 %collective-permute-start.22 = (bf16[8,48,1536]{2,1,0:T(8,128)(2,1)}, bf16[8,48,1536]{2,1,0:T(8,128)(2,1)}, u32[]{:S(2)}, u32[]{:S(2)}) collective-permute-start(bf16[8,48,1536]{2,1,0:T(8,128)(2,1)} %pad_maximum_fusion.11.mine_ref), channel_id=1, source_target_pairs={{0,2},{2,0},{1,3},{3,1},{4,6},{6,4},{5,7},{7,5},{8,10},{10,8},{9,1... | collective-permute-start | bytes 3538952 | tf_op jit(solution)/shard_map/ppermute | solution.py:898
  532.1 8.2 %copy-start.1 = (bf16[4,512,768]{2,1,0:T(8,128)(2,1)S(1)}, bf16[4,512,768]{2,1,0:T(8,128)(2,1)}, u32[]{:S(2)}) copy-start(bf16[4,512,768]{2,1,0:T(8,128)(2,1)} %param.19) | copy-start | bytes 9437188
  (7 other events, 15.2 us)
where the time goes:
time: 551 us; the launch traced here: 541 us
  Pallas kernels  216 us (39%)
  waiting for transfers between devices  208 us (38%)
  other arithmetic  58.6 us (11%)
  starting transfers between devices  33.6 us (6%)
  local copies, waits for them, and re-layouts  23.2 us (4%)
    pallas_call x8, Pallas kernels, call(): pl.pallas_call(body, grid=grid, in_specs=[s for _, s in ins], out_specs=[...  152 us
    ppermute x23, waiting for transfers between devices, flip_bit(): return lax.ppermute(array, axis, [(i, i ^ bit) for i in range(size)])  92.7 us
    pallas_call x9, Pallas kernels, packed_call(): pl.pallas_call(body, grid_spec=pltpu.PrefetchScalarGridSpec(num_scalar_pr...  63.8 us
    ppermute x3, waiting for transfers between devices, __init__(): self.got = lax.ppermute(fold(keep[0], got[0]), 'tensor', FLIP)  56.5 us
    ppermute x4, waiting for transfers between devices, fetch_half(): got = ordered(x, got, lax.ppermute(got, 'x', FLIP)).reshape(-1, shape[-1])  29.6 us
    ppermute x4, waiting for transfers between devices, fetch_half(): got = lax.ppermute(piece, 'tensor', FLIP)  22.1 us
    another operation x20, other arithmetic, ordered(): jnp.stack([jnp.where(first, mine, theirs), jnp.where(first, theirs, mine)])  18.8 us
    ppermute x23, starting transfers between devices, flip_bit(): return lax.ppermute(array, axis, [(i, i ^ bit) for i in range(size)])  16.7 us
  transfers between devices with their start and end apart: 46, of which 23 were waited for; matrix products, arithmetic and copies ran while one was open for 13% of the time, Pallas kernels for 18%

commit v1 on v0

v1 whole, which is shorter than its diff:
```python
import functools

import jax
import jax.numpy as jnp
from jax import lax
from jax.experimental import pallas as pl
from jax.experimental.pallas import tpu as pltpu
from jax.sharding import Mesh
from jax.sharding import PartitionSpec as P

HD = 64
EPS = 1e-05
NEG = -1000000000.0
F32 = jnp.float32
BF16 = jnp.bfloat16
ROWS_OVER = ("o", "x", "core")
FLIP = ((0, 1), (1, 0))
VMEM_LIMIT = 60 * 1024 * 1024


def ordered(flag, mine, theirs):
    first = flag == 0
    return jnp.stack([jnp.where(first, mine, theirs), jnp.where(first, theirs, mine)])


def take_half(array, index):
    half = array.shape[0] // 2
    return lax.dynamic_slice_in_dim(array, index * half, half, 0)


def flip_bit(array, axis, size, bit):
    return lax.ppermute(array, axis, [(i, i ^ bit) for i in range(size)])


def steps_of(outer):
    steps = [("x", 2, 1)]
    bit = 1
    while bit < outer:
        steps.append(("o", outer, bit))
        bit *= 2
    return steps


def my_bit(axis, bit):
    return (lax.axis_index(axis) // bit) % 2


def dot(a, b):
    return lax.dot_general(a, b, (((1,), (0,)), ((), ())), preferred_element_type=F32)


def dot_nt(a, b):
    return lax.dot_general(a, b, (((1,), (1,)), ((), ())), preferred_element_type=F32)


def dot_tn(a, b):
    return lax.dot_general(a, b, (((0,), (0,)), ((), ())), preferred_element_type=F32)


def norm_stats(h):
    centred = h - jnp.mean(h, axis=-1, keepdims=True)
    inverse = lax.rsqrt(jnp.mean(centred * centred, axis=-1, keepdims=True) + EPS)
    return centred * inverse, inverse


def norm_back(grad, normal, inverse, gain):
    scaled = grad * gain
    centre = jnp.mean(scaled, axis=-1, keepdims=True)
    proj = jnp.mean(scaled * normal, axis=-1, keepdims=True)
    return inverse * (scaled - centre - normal * proj)


def gelu_parts(u):
    c = 0.7978845608028654
    a = 0.044715 * c
    square = u * u
    half = 0.5 + 0.5 * jnp.tanh(u * (c + a * square))
    g = u * half
    return g, half + g * (1.0 - half) * (2.0 * c + 6.0 * a * square)


def whole(shape):
    return pl.BlockSpec(shape, lambda *_: (0,) * len(shape))


def call(body, grid, ins, outs, scratch=(), cost=(0, 0), name=None, vmem=VMEM_LIMIT):
    return pl.pallas_call(
        body,
        grid=grid,
        in_specs=[s for _, s in ins],
        out_specs=[s for _, s in outs],
        out_shape=[a for a, _ in outs],
        scratch_shapes=scratch,
        compiler_params=pltpu.CompilerParams(
            dimension_semantics=("arbitrary",) * len(grid), vmem_limit_bytes=vmem
        ),
        cost_estimate=pl.CostEstimate(
            flops=int(cost[0]) // 16, bytes_accessed=int(cost[1]), transcendentals=0
        ),
        name=name,
    )(*[a for a, _ in ins])


FAR = pl.BlockSpec(memory_space=pl.ANY)


def resident(body, ins, outs, scratch=(), flops=0, vmem=16, name=None):
    spec = pl.BlockSpec(memory_space=pltpu.VMEM)
    ins, outs = ([o if isinstance(o, tuple) else (o, spec) for o in t] for t in (ins, outs))
    ins = [(pltpu.with_memory_space_constraint(a, pltpu.HBM) if s is FAR else a, s) for a, s in ins]
    outs = [(pltpu.HBM(a.shape, a.dtype) if s is FAR else a, s) for a, s in outs]
    return pl.pallas_call(
        body,
        in_specs=[s for _, s in ins],
        out_specs=[s for _, s in outs],
        out_shape=[a for a, _ in outs],
        scratch_shapes=scratch,
        compiler_params=pltpu.CompilerParams(vmem_limit_bytes=vmem * 1024 * 1024),
        cost_estimate=pl.CostEstimate(flops=int(flops) // 16, bytes_accessed=0, transcendentals=0),
        name=name,
    )(*[a for a, _ in ins])


def sds(shape, dtype):
    return jax.ShapeDtypeStruct(shape, dtype)


QB = 128
GROUP = 256


def lanes_of(ref, g):
    return ref.at[(slice(None),) * (len(ref.shape) - 1) + (pl.ds(pl.multiple_of(g * GROUP, GROUP), GROUP),)]


class Moves:
    def __init__(self, sems):
        self.sems, self.used = sems, 0

    def whole(self, source, target):
        copy = pltpu.make_async_copy(source, target, self.sems.at[self.used])
        self.used += 1
        copy.start()
        return copy.wait

    def groups(self, source, target):
        first = self.used
        self.used += source.shape[-1] // GROUP

        def copy(g):
            return pltpu.make_async_copy(lanes_of(source, g), lanes_of(target, g), self.sems.at[first + g])

        return (lambda g: copy(g).start()), (lambda g: copy(g).wait())


def cat_heads(t, scale=1.0):
    lane = lax.broadcasted_iota(jnp.int32, (1, 2 * HD), 1)
    parts = [t * jnp.where((lane < HD) == (h == 0), scale, 0.0).astype(t.dtype) for h in range(2)]
    return jnp.concatenate(parts, axis=0)


def own_lanes(t, scale=None):
    if scale is not None:
        t = t * scale
    return jnp.concatenate([t[:HD, :QB], t[HD:, QB:]], axis=0)


def twice(t):
    return jnp.concatenate([t, t], axis=1)


def pair_row(rows, p):
    return jnp.concatenate([rows[2 * p : 2 * p + 1], rows[2 * p + 1 : 2 * p + 2]], axis=1)


def put_pair(ref, p, cols, value):
    ref[2 * p : 2 * p + 1, cols] = value[:, :QB]
    ref[2 * p + 1 : 2 * p + 2, cols] = value[:, QB:]


def columns(t, r, seq, qb):
    return t[:, pl.ds(pl.multiple_of(r * seq + qb * QB, QB), QB)]


def rows_of(r, seq, qb):
    return pl.ds(pl.multiple_of(r * seq + qb * QB, QB), QB)


def attend_first_body(rows, seq, pairs, a_ref, w_ref, bias_ref, qkv_ref, o_ref, lse_ref):
    a = a_ref[...]
    for j in range(3):
        qkv_ref[j] = dot(a, w_ref[j]).astype(BF16)
    for r in range(rows):
        work = []
        for p in range(pairs):
            ln = slice(p * 2 * HD, (p + 1) * 2 * HD)
            k = qkv_ref[1, r * seq : (r + 1) * seq, ln]
            for b in range(seq // QB):
                sl, n = slice(r * seq + b * QB, r * seq + (b + 1) * QB), (b + 1) * QB
                q = cat_heads(qkv_ref[0, sl, ln], HD**-0.5)
                s = dot_nt(k[:n], q) + twice(bias_ref[r, :n, b * QB : n])
                work.append((p, ln, sl, n, s))
        done = []
        for p, ln, sl, n, s in work:
            top = jnp.max(s, axis=0, keepdims=True)
            e = jnp.exp(s - top)
            mass = jnp.sum(e, axis=0, keepdims=True)
            put_pair(lse_ref, p, sl, top + jnp.log(mass))
            done.append((e.astype(BF16), 1.0 / mass))
        for (p, ln, sl, n, _), (e, inv) in zip(work, done):
            vt = qkv_ref[2, r * seq : (r + 1) * seq, ln].T
            o_ref[sl, ln] = own_lanes(dot(vt[:, :n], e), inv).T.astype(BF16)


def attend_first(a, w, bias):
    rows, seq = bias.shape[0], bias.shape[1]
    n, d = a.shape
    f = w.shape[2]
    return resident(
        functools.partial(attend_first_body, rows, seq, f // (2 * HD)),
        (a, w, bias),
        [sds((3, n, f), BF16), sds((n, f), BF16), sds((f // HD, n), F32)],
        flops=6 * n * d * f + 16 * n * seq * f,
        name="attend_first",
    )


def attend_second_body(
    rows, seq, a_far, w_far, incl_far, strict_far, qkve_far, o1_far, lse1_ref,
    qkvo_far, o2_far, lse2_ref,
    a_ref, w_ref, incl_ref, strict_ref, qkve_ref, o1_ref, qkvo_ref, o2_ref, sems,
):
    groups = lse1_ref.shape[0]
    moves = Moves(sems)
    ready = [moves.whole(a_far, a_ref)]
    ready += [moves.whole(w_far.at[j], w_ref.at[j]) for j in range(3)]
    masks = [moves.whole(*t) for t in ((incl_far, incl_ref), (strict_far, strict_ref))]
    arrive = [moves.groups(*t) for t in ((qkve_far, qkve_ref), (o1_far, o1_ref))]
    leave = moves.groups(o2_ref, o2_far)
    for g in range(groups):
        for start, _ in arrive:
            start(g)
    ready[0]()
    a = a_ref[...]
    sent = []
    for j in range(3):
        ready[1 + j]()
        qkvo_ref[j] = dot(a, w_ref[j]).astype(BF16)
        sent.append(moves.whole(qkvo_ref.at[j], qkvo_far.at[j]))
    for wait in masks:
        wait()

    def row(i, _):
        r, group = i % rows, i // rows
        lanes = pl.multiple_of(group * GROUP, GROUP)
        all_of = pl.ds(pl.multiple_of(r * seq, seq), seq)

        @pl.when(r == 0)
        def _():
            for _, wait in arrive:
                wait(group)

        for p in range(GROUP // (2 * HD)):
            ln = pl.ds(lanes + p * 2 * HD, 2 * HD)
            ke, ko = qkve_ref[1, all_of, ln], qkvo_ref[1, all_of, ln]
            vte, vto = qkve_ref[2, all_of, ln].T, qkvo_ref[2, all_of, ln].T
            work = []
            for b in range(seq // QB):
                sl, n = rows_of(r, seq, b), (b + 1) * QB
                cols = slice(b * QB, n)
                incl, strict = twice(incl_ref[r, :n, cols]), twice(strict_ref[r, :n, cols])
                q = cat_heads(qkve_ref[0, sl, ln], HD**-0.5)
                work.append([dot_nt(ko[:n], q) + strict])
                q = cat_heads(qkvo_ref[0, sl, ln], HD**-0.5)
                work.append([dot_nt(ko[:n], q) + incl, dot_nt(ke[:n], q) + incl])
            for b in range(seq // QB):
                sl, n = rows_of(r, seq, b), (b + 1) * QB
                (s,), (so, se) = work[2 * b : 2 * b + 2]
                old = pair_row(lse1_ref[group, :, sl], p)
                top = jnp.maximum(old, jnp.max(s, axis=0, keepdims=True))
                e = jnp.exp(s - top)
                kept = jnp.exp(old - top)
                mass = kept + jnp.sum(e, axis=0, keepdims=True)
                work[2 * b] = (e.astype(BF16), kept, 1.0 / mass)
                put_pair(lse2_ref.at[0, group], p, sl, top + jnp.log(mass))
                top = jnp.max(jnp.maximum(se, so), axis=0, keepdims=True)
                ee, eo = jnp.exp(se - top), jnp.exp(so - top)
                mass = jnp.sum(ee + eo, axis=0, keepdims=True)
                work[2 * b + 1] = (ee.astype(BF16), eo.astype(BF16), 1.0 / mass)
                put_pair(lse2_ref.at[1, group], p, sl, top + jnp.log(mass))
            for b in range(seq // QB):
                sl, n = rows_of(r, seq, b), (b + 1) * QB
                (e, kept, inv), (ee, eo, inv2) = work[2 * b : 2 * b + 2]
                o1 = o1_ref[sl, ln].astype(F32).T
                o = own_lanes(dot(vto[:, :n], e), inv) + own_lanes(twice(o1), kept * inv)
                o2_ref[0, sl, ln] = o.T.astype(BF16)
                o = dot(vte[:, :n], ee) + dot(vto[:, :n], eo)
                o2_ref[1, sl, ln] = own_lanes(o, inv2).T.astype(BF16)

        @pl.when(r == rows - 1)
        def _():
            leave[0](group)

        return 0

    lax.fori_loop(0, rows * groups, row, 0)
    for wait in sent:
        wait()
    for g in range(groups):
        leave[1](g)


def attend_second(a, w, incl, strict, qkve, o1, lse1):
    rows, seq = incl.shape[0], incl.shape[1]
    n, d = a.shape
    f = w.shape[2]
    qkv, o2 = sds((3, n, f), BF16), sds((2, n, f), BF16)
    near = (a, w, incl, strict, qkve, o1, qkv, o2)
    return resident(
        functools.partial(attend_second_body, rows, seq),
        [(t, FAR) for t in (a, w, incl, strict, qkve, o1)] + [lse1],
        [(qkv, FAR), (o2, FAR), sds((2, *lse1.shape), F32)],
        scratch=[pltpu.VMEM(t.shape, t.dtype) for t in near] + [pltpu.SemaphoreType.DMA((32,))],
        flops=6 * n * d * f + 48 * n * seq * f,
        vmem=32,
        name="attend_second",
    )


def row_products(a, b):
    prod = cat_heads((a * b).astype(BF16))
    return dot_nt(jnp.ones((8, 2 * HD), BF16), prod)[:1]


def query_parts(sl, ln, group, p, i, qkv_ref, o_ref, lse_ref, do_ref):
    do = do_ref[i, sl, ln]
    delta = row_products(do.astype(F32), o_ref[i, sl, ln].astype(F32))
    return cat_heads(qkv_ref[0, sl, ln], HD**-0.5), cat_heads(do), pair_row(lse_ref[i, group, :, sl], p), delta


def blocks_back(tasks):
    scores = [dot_nt(k, q) + bias - lse for k, _, _, bias, q, _, lse, _ in tasks]
    moved = [dot_nt(v, do) - delta for _, v, _, _, _, do, _, delta in tasks]
    probs = [jnp.exp(s) for s in scores]
    ds = [(p * m).astype(BF16) for p, m in zip(probs, moved)]
    return [
        (dot(p.astype(BF16), do), dot(d, q), dot(kt, d))
        for (_, _, kt, _, q, do, _, _), p, d in zip(tasks, probs, ds)
    ]


def add_rows(total, part):
    if total is None:
        return part
    n = part.shape[0]
    return jnp.concatenate([total[:n] + part, total[n:]], axis=0)


def attend_back_body(
    rows, seq, w_far, incl_far, strict_far, qkve_far, qkvo_far, o2_far, lse2_ref, do_far,
    dh1_far, ho_far, gb_ref,
    dqkvo_far, dqkve_far, dy_ref, sums_ref,
    w_ref, incl_ref, strict_ref, qkve_ref, qkvo_ref, o2_ref, do_ref, dh1_ref, ho_ref,
    dqkvo_ref, dqkve_ref, da_ref, sems,
):
    groups = lse2_ref.shape[1]
    moves = Moves(sems)
    arrive = [
        moves.groups(*t)
        for t in ((qkve_far, qkve_ref), (qkvo_far, qkvo_ref), (o2_far, o2_ref), (do_far, do_ref))
    ]
    leave = [moves.groups(*t) for t in ((dqkvo_ref, dqkvo_far), (dqkve_ref, dqkve_far))]
    for start, _ in arrive:
        start(0)
    masks = [moves.whole(*t) for t in ((incl_far, incl_ref), (strict_far, strict_ref))]
    for g in range(1, groups):
        for start, _ in arrive:
            start(g)
    odd = pl.ds(rows * seq, rows * seq)
    late = [moves.whole(*t) for t in ((w_far, w_ref), (dh1_far.at[odd], dh1_ref), (ho_far, ho_ref))]
    for wait in masks:
        wait()
    sc = HD**-0.5

    def row(i, _):
        r, group = i % rows, i // rows
        lanes = pl.multiple_of(group * GROUP, GROUP)
        all_of = pl.ds(pl.multiple_of(r * seq, seq), seq)

        @pl.when(r == 0)
        def _():
            for _, wait in arrive:
                wait(group)

        for p in range(GROUP // (2 * HD)):
            ln = pl.ds(lanes + p * 2 * HD, 2 * HD)
            ke, ve = qkve_ref[1, all_of, ln], qkve_ref[2, all_of, ln]
            ko, vo = qkvo_ref[1, all_of, ln], qkvo_ref[2, all_of, ln]
            kte, kto = ke.T, ko.T
            tasks = []
            for b in reversed(range(seq // QB)):
                sl, n = rows_of(r, seq, b), (b + 1) * QB
                cols = slice(b * QB, n)
                incl, strict = twice(incl_ref[r, :n, cols]), twice(strict_ref[r, :n, cols])
                even = query_parts(sl, ln, group, p, 0, qkve_ref, o2_ref, lse2_ref, do_ref)
                odd = query_parts(sl, ln, group, p, 1, qkvo_ref, o2_ref, lse2_ref, do_ref)
                tasks.append((ko[:n], vo[:n], kto[:, :n], strict, *even))
                tasks.append((ko[:n], vo[:n], kto[:, :n], incl, *odd))
                tasks.append((ke[:n], ve[:n], kte[:, :n], incl, *odd))
            done = blocks_back(tasks)
            dke = dve = dko = dvo = None
            for b in reversed(range(seq // QB)):
                sl = rows_of(r, seq, b)
                (dv, dk, dqe), (dv2, dk2, dqo), (dv3, dk3, dqo2) = done[:3]
                done = done[3:]
                dvo, dko = add_rows(dvo, dv + dv2), add_rows(dko, dk + dk2)
                dve, dke = add_rows(dve, dv3), add_rows(dke, dk3)
                dqkve_ref[0, sl, ln] = (own_lanes(dqe).T * sc).astype(BF16)
                dqkvo_ref[0, sl, ln] = (own_lanes(dqo + dqo2).T * sc).astype(BF16)
            dqkve_ref[1, all_of, ln] = dke.astype(BF16)
            dqkve_ref[2, all_of, ln] = dve.astype(BF16)
            dqkvo_ref[1, all_of, ln] = dko.astype(BF16)
            dqkvo_ref[2, all_of, ln] = dvo.astype(BF16)

        @pl.when(r == rows - 1)
        def _():
            for start, _ in leave:
                start(group)

        return 0

    lax.fori_loop(0, rows * groups, row, 0)
    for wait in late:
        wait()
    da = dot_nt(dqkvo_ref[0], w_ref[0])
    da += dot_nt(dqkvo_ref[1], w_ref[1])
    da += dot_nt(dqkvo_ref[2], w_ref[2])
    da_ref[...] = da
    gain_sum = jnp.zeros_like(gb_ref[0:1])
    bias_sum = jnp.zeros_like(gb_ref[0:1])
    pass_sum = jnp.zeros_like(gb_ref[0:1])
    for i in range(rows):
        sl = slice(i * seq, (i + 1) * seq)
        normal, inverse = norm_stats(ho_ref[sl])
        da = da_ref[sl]
        gain_sum += jnp.sum(da * normal, axis=0, keepdims=True)
        bias_sum += jnp.sum(da, axis=0, keepdims=True)
        dy = dh1_ref[sl] + norm_back(da, normal, inverse, gb_ref[0:1])
        dy_ref[sl] = dy
        pass_sum += jnp.sum(dy, axis=0, keepdims=True)
    sums_ref[0:1] = gain_sum
    sums_ref[1:2] = bias_sum
    sums_ref[2:3] = pass_sum
    for g in range(groups):
        for _, wait in leave:
            wait(g)


def attend_back(w, incl, strict, qkve, qkvo, o2, lse2, do, dh1, ho, gb):
    rows, seq = incl.shape[0], incl.shape[1]
    n, d = ho.shape
    f = w.shape[2]
    do = do.reshape(2, n, f)
    qkv = sds((3, n, f), BF16)
    near = (w, incl, strict, qkve, qkvo, o2, do, sds((n, d), F32), ho, qkv, qkv, sds((n, d), F32))
    return resident(
        functools.partial(attend_back_body, rows, seq),
        [(t, FAR) for t in (w, incl, strict, qkve, qkvo, o2)]
        + [lse2]
        + [(t, FAR) for t in (do, dh1, ho)]
        + [gb],
        [(qkv, FAR), (qkv, FAR), sds((n, d), F32), sds((3, d), F32)],
        scratch=[pltpu.VMEM(t.shape, t.dtype) for t in near] + [pltpu.SemaphoreType.DMA((32,))],
        flops=6 * n * d * f + 120 * n * seq * f,
        vmem=44,
        name="attend_back",
    )


def attend_back_even_body(
    rows, seq, w_far, incl_far, qkve_far, o1_far, lse1_ref, do1_far, o2_far, lse2_ref, do2_far,
    part_far, dh1_far, dh2_far, x_far, gb_ref,
    dqkv_far, gt_ref, sums_ref,
    w_ref, incl_ref, qkve_ref, o1_ref, do1_ref, o2_ref, do2_ref, part_ref, dh1_ref, dh2_ref, x_ref,
    dqkv_ref, da_ref, sems,
):
    groups = lse1_ref.shape[0]
    moves = Moves(sems)
    even = pl.ds(0, rows * seq)
    arrive = [
        moves.groups(*t)
        for t in (
            (qkve_far, qkve_ref), (o1_far, o1_ref), (do1_far, do1_ref), (o2_far.at[0], o2_ref),
            (do2_far.at[0], do2_ref), (part_far, part_ref),
        )
    ]
    leave = [moves.groups(dqkv_ref, dqkv_far)]
    for start, _ in arrive:
        start(0)
    mask = moves.whole(incl_far, incl_ref)
    for g in range(1, groups):
        for start, _ in arrive:
            start(g)
    late = [
        moves.whole(*t)
        for t in ((w_far, w_ref), (dh1_far, dh1_ref), (dh2_far.at[even], dh2_ref), (x_far, x_ref))
    ]
    mask()
    sc = HD**-0.5

    def row(i, _):
        r, group = i % rows, i // rows
        lanes = pl.multiple_of(group * GROUP, GROUP)
        all_of = pl.ds(pl.multiple_of(r * seq, seq), seq)

        @pl.when(r == 0)
        def _():
            for _, wait in arrive:
                wait(group)

        for p in range(GROUP // (2 * HD)):
            ln = pl.ds(lanes + p * 2 * HD, 2 * HD)
            k, v = qkve_ref[1, all_of, ln], qkve_ref[2, all_of, ln]
            kt = k.T
            tasks = []
            for b in reversed(range(seq // QB)):
                sl, n = rows_of(r, seq, b), (b + 1) * QB
                incl = twice(incl_ref[r, :n, b * QB : n])
                lse1 = pair_row(lse1_ref[group, :, sl], p)
                ratio = jnp.exp(lse1 - pair_row(lse2_ref[0, group, :, sl], p))
                do1, do2 = do1_ref[sl, ln].astype(F32), do2_ref[sl, ln].astype(F32)
                delta = row_products(do1, o1_ref[sl, ln].astype(F32))
                delta += ratio * row_products(do2, o2_ref[sl, ln].astype(F32))
                both = do1 + own_lanes(twice(do2.T), ratio).T
                q, do = cat_heads(qkve_ref[0, sl, ln], sc), cat_heads(both.astype(BF16))
                tasks.append((k[:n], v[:n], kt[:, :n], incl, q, do, lse1, delta))
            dka = dva = None
            for b, (dv, dk, dq) in zip(reversed(range(seq // QB)), blocks_back(tasks)):
                sl = rows_of(r, seq, b)
                dva, dka = add_rows(dva, dv), add_rows(dka, dk)
                dqkv_ref[0, sl, ln] = (own_lanes(dq).T * sc + part_ref[0, sl, ln].astype(F32)).astype(BF16)
            dqkv_ref[1, all_of, ln] = (dka + part_ref[1, all_of, ln].astype(F32)).astype(BF16)
            dqkv_ref[2, all_of, ln] = (dva + part_ref[2, all_of, ln].astype(F32)).astype(BF16)

        @pl.when(r == rows - 1)
        def _():
            for start, _ in leave:
                start(group)

        return 0

    lax.fori_loop(0, rows * groups, row, 0)
    for wait in late:
        wait()
    da = dot_nt(dqkv_ref[0], w_ref[0])
    da += dot_nt(dqkv_ref[1], w_ref[1])
    da += dot_nt(dqkv_ref[2], w_ref[2])
    da_ref[...] = da
    gain_sum = jnp.zeros_like(gb_ref[0:1])
    bias_sum = jnp.zeros_like(gb_ref[0:1])
    for i in range(rows):
        sl = slice(i * seq, (i + 1) * seq)
        normal, inverse = norm_stats(x_ref[sl].astype(F32))
        da = da_ref[sl]
        gain_sum += jnp.sum(da * normal, axis=0, keepdims=True)
        bias_sum += jnp.sum(da, axis=0, keepdims=True)
        back = norm_back(da, normal, inverse, gb_ref[0:1])
        gt_ref[sl] = (dh1_ref[sl] + dh2_ref[sl] + back).astype(BF16)
    sums_ref[0:1] = gain_sum
    sums_ref[1:2] = bias_sum
    for g in range(groups):
        for _, wait in leave:
            wait(g)


def attend_back_even(w, incl, qkve, o1, lse1, do1, o2, lse2, do2, part, dh1, dh2, x, gb):
    rows, seq = incl.shape[0], incl.shape[1]
    n, d = x.shape
    f = w.shape[2]
    qkv, one = sds((3, n, f), BF16), sds((n, f), BF16)
    near = (w, incl, qkv, one, one, one, one, qkv, dh1, dh1, x, qkv, sds((n, d), F32))
    far = lambda *ts: [(t, FAR) for t in ts]
    return resident(
        functools.partial(attend_back_even_body, rows, seq),
        far(w, incl, qkve, o1)
        + [lse1]
        + far(do1, o2)
        + [lse2]
        + far(do2.reshape(2, n, f), part, dh1, dh2, x)
        + [gb],
        [(qkv, FAR), sds((n, d), BF16), sds((2, d), F32)],
        scratch=[pltpu.VMEM(t.shape, t.dtype) for t in near] + [pltpu.SemaphoreType.DMA((32,))],
        flops=6 * n * d * f + 40 * n * seq * f,
        vmem=40,
        name="attend_back_even",
    )


def mlp_first_body(
    x_ref, o_ref, wout_ref, gb_ref, wup_ref, wdown_ref,
    h1_ref, n2_ref, g_ref, d_ref, ho_ref, ao_ref,
):
    j = pl.program_id(0)

    @pl.when(j == 0)
    def _():
        h1 = x_ref[...].astype(F32) + dot(o_ref[...], wout_ref[...])
        h1_ref[...] = h1
        normal, _ = norm_stats(h1)
        n2_ref[...] = (normal * gb_ref[1:2] + gb_ref[3:4]).astype(BF16)
        ho_ref[...] = h1 + gb_ref[4:5]

    u = dot(n2_ref[...], wup_ref[...])
    g, d = gelu_parts(u)
    g = g.astype(BF16)
    g_ref[...] = g
    d_ref[...] = d.astype(BF16)
    ho_ref[...] += dot(g, wdown_ref[...])

    @pl.when(j == pl.num_programs(0) - 1)
    def _():
        normal, _ = norm_stats(ho_ref[...])
        ao_ref[...] = (normal * gb_ref[0:1] + gb_ref[2:3]).astype(BF16)


def mlp_first(x, o, wout, gb, wup, wdown):
    n, d = x.shape
    ff = wup.shape[1]
    c = 512
    return call(
        mlp_first_body,
        (ff // c,),
        [
            (x, whole(x.shape)),
            (o, whole(o.shape)),
            (wout, whole(wout.shape)),
            (gb, whole(gb.shape)),
            (wup, pl.BlockSpec((d, c), lambda j: (0, j))),
            (wdown, pl.BlockSpec((c, d), lambda j: (j, 0))),
        ],
        [
            (sds((n, d), F32), whole((n, d))),
            (sds((n, d), BF16), whole((n, d))),
            (sds((n, ff), BF16), pl.BlockSpec((n, c), lambda j: (0, j))),
            (sds((n, ff), BF16), pl.BlockSpec((n, c), lambda j: (0, j))),
            (sds((n, d), F32), whole((n, d))),
            (sds((n, d), BF16), whole((n, d))),
        ],
        cost=(2 * n * d * (2 * ff + d), 0),
        name="mlp_first",
    )


def weave(seq):
    i = lax.broadcasted_iota(jnp.int32, (2 * seq, 2 * seq), 0)
    k = lax.broadcasted_iota(jnp.int32, (2 * seq, 2 * seq), 1)
    place = jnp.where(k < seq, 2 * k, 2 * (k - seq) + 1)
    return jnp.where(i == place, 1.0, 0.0).astype(BF16)


def mlp_second_body(
    rows, seq, x_ref, ho_ref, o_ref, cot_ref, wout_ref, gb_ref, wup_ref, wdown_ref,
    out_ref, n2_ref, g_ref, du_ref, dh1_ref, dp_ref, do_ref, sums_ref, dm_ref,
    h1_ref, z_ref, dn_ref,
):
    j = pl.program_id(0)
    n = rows * seq
    halves = (slice(0, n), slice(n, 2 * n))

    @pl.when(j == 0)
    def _():
        for i, sl in enumerate(halves):
            start = x_ref[...].astype(F32) if i == 0 else ho_ref[...]
            h1 = start + dot(o_ref[i], wout_ref[...])
            h1_ref[sl] = h1
            normal, _ = norm_stats(h1)
            n2_ref[sl] = (normal * gb_ref[1:2] + gb_ref[3:4]).astype(BF16)
        z_ref[...] = jnp.zeros_like(z_ref)
        dn_ref[...] = jnp.zeros_like(dn_ref)
        mix = weave(seq)
        for r in range(rows):
            parted = dot_tn(mix, cot_ref[r]).astype(BF16)
            for i in range(2):
                dm_ref[i * n + r * seq : i * n + (r + 1) * seq] = parted[i * seq : (i + 1) * seq]

    for sl in halves:
        u = dot(n2_ref[sl], wup_ref[...])
        dg = dot_nt(dm_ref[sl], wdown_ref[...])
        g, d = gelu_parts(u)
        g = g.astype(BF16)
        du = (dg * d).astype(BF16)
        g_ref[sl] = g
        du_ref[sl] = du
        z_ref[sl] += dot(g, wdown_ref[...])
        dn_ref[sl] += dot_nt(du, wup_ref[...])

    @pl.when(j == pl.num_programs(0) - 1)
    def _():
        mix = weave(seq)
        for r in range(rows):
            pair = [slice(i * n + r * seq, i * n + (r + 1) * seq) for i in range(2)]
            z = jnp.concatenate([(h1_ref[s] + z_ref[s]).astype(BF16) for s in pair], axis=0)
            out_ref[r] = dot(mix, z).astype(BF16)
        gain_sum = jnp.zeros_like(gb_ref[0:1])
        bias_sum = jnp.zeros_like(gb_ref[0:1])
        for i in range(2 * rows):
            sl = slice(i * seq, (i + 1) * seq)
            normal, inverse = norm_stats(h1_ref[sl])
            dn = dn_ref[sl]
            gain_sum += jnp.sum(dn * normal, axis=0, keepdims=True)
            bias_sum += jnp.sum(dn, axis=0, keepdims=True)
            dh1 = dm_ref[sl].astype(F32) + norm_back(dn, normal, inverse, gb_ref[1:2])
            dh1_ref[sl] = dh1
            dp = dh1.astype(BF16)
            dp_ref[sl] = dp
            do_ref[sl] = dot_nt(dp, wout_ref[...]).astype(BF16)
        sums_ref[0:1] = gain_sum
        sums_ref[1:2] = bias_sum


def mlp_second(x, ho, o2, cot, wout, gb, wup, wdown, seq):
    n, d = x.shape
    ff = wup.shape[1]
    rows = n // seq
    c = 512
    blk = pl.BlockSpec((2 * n, c), lambda j: (0, j))
    return call(
        functools.partial(mlp_second_body, rows, seq),
        (ff // c,),
        [
            (x, whole(x.shape)),
            (ho, whole(ho.shape)),
            (o2, whole(o2.shape)),
            (cot, whole(cot.shape)),
            (wout, whole(wout.shape)),
            (gb, whole(gb.shape)),
            (wup, pl.BlockSpec((d, c), lambda j: (0, j))),
            (wdown, pl.BlockSpec((c, d), lambda j: (j, 0))),
        ],
        [
            (sds((rows, 2 * seq, d), BF16), whole((rows, 2 * seq, d))),
            (sds((2 * n, d), BF16), whole((2 * n, d))),
            (sds((2 * n, ff), BF16), blk),
            (sds((2 * n, ff), BF16), blk),
            (sds((2 * n, d), F32), whole((2 * n, d))),
            (sds((2 * n, d), BF16), whole((2 * n, d))),
            (sds((2 * n, d), BF16), whole((2 * n, d))),
            (sds((2, d), F32), whole((2, d))),
            (sds((2 * n, d), BF16), whole((2 * n, d))),
        ],
        scratch=[pltpu.VMEM((2 * n, d), F32)] * 3,
        cost=(2 * n * d * (8 * ff + 4 * d), 0),
        name="mlp_second",
    )


def mlp_back_body(
    rows, seq, dy_ref, h1_ref, wout_ref, gb_ref, d_ref, wup_ref, wdown_ref,
    du_ref, dh1_ref, dp_ref, do_ref, sums_ref, dm_ref, dn_ref,
):
    j = pl.program_id(0)

    @pl.when(j == 0)
    def _():
        dm_ref[...] = dy_ref[...].astype(BF16)
        dn_ref[...] = jnp.zeros_like(dn_ref)

    dg = dot_nt(dm_ref[...], wdown_ref[...])
    du = (dg * d_ref[...].astype(F32)).astype(BF16)
    du_ref[...] = du
    dn_ref[...] += dot_nt(du, wup_ref[...])

    @pl.when(j == pl.num_programs(0) - 1)
    def _():
        gain_sum = jnp.zeros_like(gb_ref[0:1])
        bias_sum = jnp.zeros_like(gb_ref[0:1])
        for i in range(rows):
            sl = slice(i * seq, (i + 1) * seq)
            normal, inverse = norm_stats(h1_ref[sl])
            dn = dn_ref[sl]
            gain_sum += jnp.sum(dn * normal, axis=0, keepdims=True)
            bias_sum += jnp.sum(dn, axis=0, keepdims=True)
            dh1 = dy_ref[sl] + norm_back(dn, normal, inverse, gb_ref[1:2])
            dh1_ref[sl] = dh1
            dp = dh1.astype(BF16)
            dp_ref[sl] = dp
            do_ref[sl] = dot_nt(dp, wout_ref[...]).astype(BF16)
        sums_ref[0:1] = gain_sum
        sums_ref[1:2] = bias_sum


def mlp_back(dy, h1, wout, gb, dgelu, wup, wdown, seq):
    n, d = dy.shape
    ff = wup.shape[1]
    c = 512
    blk = pl.BlockSpec((n, c), lambda j: (0, j))
    return call(
        functools.partial(mlp_back_body, n // seq, seq),
        (ff // c,),
        [
            (dy, whole(dy.shape)),
            (h1, whole(h1.shape)),
            (wout, whole(wout.shape)),
            (gb, whole(gb.shape)),
            (dgelu, blk),
            (wup, pl.BlockSpec((d, c), lambda j: (0, j))),
            (wdown, pl.BlockSpec((c, d), lambda j: (j, 0))),
        ],
        [
            (sds((n, ff), BF16), blk),
            (sds((n, d), F32), whole((n, d))),
            (sds((n, d), BF16), whole((n, d))),
            (sds((n, d), BF16), whole((n, d))),
            (sds((2, d), F32), whole((2, d))),
        ],
        scratch=[pltpu.VMEM((n, d), BF16), pltpu.VMEM((n, d), F32)],
        cost=(2 * n * d * (2 * ff + d), 0),
        name="mlp_back",
    )


def packed_call(body, grid, me, ins, outs, scratch=(), flops=0, aliases={}, name=None):
    return pl.pallas_call(
        body,
        grid_spec=pltpu.PrefetchScalarGridSpec(
            num_scalar_prefetch=1,
            grid=grid,
            in_specs=[s for _, s in ins],
            out_specs=[s for _, s in outs],
            scratch_shapes=scratch,
        ),
        out_shape=[a for a, _ in outs],
        input_output_aliases=aliases,
        compiler_params=pltpu.CompilerParams(
            dimension_semantics=("arbitrary",) * len(grid), vmem_limit_bytes=VMEM_LIMIT
        ),
        cost_estimate=pl.CostEstimate(flops=int(flops) // 16, bytes_accessed=0, transcendentals=0),
        name=name,
    )(me, *[a for a, _ in ins])


def place_of(quarter, y, me):
    return jnp.where(y == 0, 4 + (quarter ^ me[1]), quarter)


def grad_down_body(me_ref, g1_ref, g2_ref, dm1_ref, dm2_ref, out_ref, acc_ref):
    low = me_ref[0] % 4
    acc = dot_tn(g1_ref[...], dm1_ref[...])
    acc += dot_tn(g2_ref[...], dm2_ref[...])
    acc_ref[...] = acc.reshape(acc_ref.shape)
    for s in range(4):
        out_ref[0, s] = acc_ref[s ^ low].astype(BF16)


def grad_down(me, side, g1, g2, dm1, dm2):
    n, d = dm1.shape
    ff = g1.shape[1]
    b = ff // 8
    pick = lambda y, h, me: (0, place_of((((me[0] // 8) ^ side) * 2 + h), y, me))
    const = lambda y, h, me: (0, 0)
    return packed_call(
        grad_down_body,
        (2, 2),
        me,
        [
            (g1, pl.BlockSpec((n, b), pick)),
            (g2, pl.BlockSpec((2 * n, b), pick)),
            (dm1, pl.BlockSpec((n, d), const)),
            (dm2, pl.BlockSpec((2 * n, d), const)),
        ],
        [
            (
                sds((2, 8, b // 4, d), BF16),
                pl.BlockSpec((1, 4, b // 4, d), lambda y, h, me: (y, h ^ ((me[0] // 4) % 2), 0, 0)),
            )
        ],
        scratch=[pltpu.VMEM((4, b // 4, d), F32)],
        flops=2 * 3 * n * d * ff // 2,
        name="grad_down",
    )[0]


def grad_up_body(
    me_ref, n1_ref, n2_ref, du1_ref, du2_ref, dp1_ref, dp2_ref, o1_ref, o2_ref, out_ref, t1_ref, t2_ref, acc_ref
):
    low = me_ref[0] % 8
    j, last = pl.program_id(1), pl.num_programs(1) - 1

    @pl.when((pl.program_id(0) == 0) & (j == 0))
    def _():
        t1_ref[...] = n1_ref[...].T
        t2_ref[...] = n2_ref[...].T

    def write(acc):
        acc_ref[...] = acc.reshape(acc_ref.shape)
        for s in range(8):
            out_ref[0, s] = acc_ref[s ^ low].astype(BF16)

    @pl.when(j < last)
    def _():
        write(dot(t1_ref[...], du1_ref[...]) + dot(t2_ref[...], du2_ref[...]))

    @pl.when(j == last)
    def _():
        write(dot_tn(dp1_ref[...], o1_ref[...]) + dot_tn(dp2_ref[...], o2_ref[...]))


def grad_up(me, side, n1, n2, du1, du2, dp1, dp2, o1, o2):
    n, d = n1.shape
    ff = du1.shape[1]
    b, c = d // 2, o1.shape[1] // 2
    parts = ff // 2 // c
    rows = lambda y, j, me: (0, (me[0] // 8) ^ side)
    cols = lambda y, j, me: (0, place_of(jnp.minimum(j, parts - 1), y, me))
    half = lambda y, j, me: (0, 1 - y)
    return packed_call(
        grad_up_body,
        (2, parts + 1),
        me,
        [
            (n1, pl.BlockSpec((n, b), rows)),
            (n2, pl.BlockSpec((2 * n, b), rows)),
            (du1, pl.BlockSpec((n, c), cols)),
            (du2, pl.BlockSpec((2 * n, c), cols)),
            (dp1, pl.BlockSpec((n, b), rows)),
            (dp2, pl.BlockSpec((2 * n, b), rows)),
            (o1, pl.BlockSpec((n, c), half)),
            (o2, pl.BlockSpec((2 * n, c), half)),
        ],
        [
            (
                sds((2, 8, b // 8, (parts + 1) * c), BF16),
                pl.BlockSpec((1, 8, b // 8, c), lambda y, j, me: (y, 0, 0, j)),
            )
        ],
        scratch=[
            pltpu.VMEM((b, n), BF16),
            pltpu.VMEM((b, 2 * n), BF16),
            pltpu.VMEM((8, b // 8, c), F32),
        ],
        flops=2 * 3 * n * d * (ff + d) // 2,
        name="grad_up",
    )[0]


def grad_qkv_body(me_ref, ae_ref, ao_ref, de_ref, do_ref, out_ref, acc_ref):
    low = me_ref[0] % 8
    f = de_ref.shape[2]
    for j in range(3):
        acc = dot_tn(ae_ref[...], de_ref[j])
        acc += dot_tn(ao_ref[...], do_ref[j])
        acc_ref[...] = acc.reshape(acc_ref.shape)
        for s in range(8):
            out_ref[0, s, :, j * f : (j + 1) * f] = acc_ref[s ^ low].astype(BF16)


def grad_qkv(me, side, ae, ao, dqkv_e, dqkv_o):
    n, d = ae.shape
    b, f = d // 2, dqkv_e.shape[2] // 2
    rows = lambda y, me: (0, (me[0] // 8) ^ side)
    cols3 = lambda y, me: (0, 0, 1 - y)
    return packed_call(
        grad_qkv_body,
        (2,),
        me,
        [
            (ae, pl.BlockSpec((n, b), rows)),
            (ao, pl.BlockSpec((n, b), rows)),
            (dqkv_e, pl.BlockSpec((3, n, f), cols3)),
            (dqkv_o, pl.BlockSpec((3, n, f), cols3)),
        ],
        [
            (
                sds((2, 8, b // 8, 3 * f), BF16),
                pl.BlockSpec((1, 8, b // 8, 3 * f), lambda y, me: (y, 0, 0, 0)),
            )
        ],
        scratch=[pltpu.VMEM((8, b // 8, f), F32)],
        flops=2 * 2 * 3 * n * d * f,
        name="grad_qkv",
    )[0]


def unpack_body(kind, me_ref, part_ref, *refs):
    low = me_ref[0] % 8
    rows, width = part_ref.shape[1:]
    first = refs[-2] if kind == "up" else refs[-1]
    if kind == "up":
        first, second, wide = refs[-3:]
    for s in range(8):
        sl = slice(s * rows, (s + 1) * rows)
        if kind == "down":
            first[sl] = part_ref[s ^ low].astype(F32)
        elif kind == "up":
            f = first.shape[1]
            first[sl] = part_ref[s ^ low, :, :f].astype(F32)
            wide[sl] = part_ref[s ^ low, :, f:].astype(F32)
        else:
            f = width // 3
            for j in range(3):
                first[j, sl] = part_ref[s ^ low, :, j * f : (j + 1) * f].astype(F32)
    if kind == "up":
        second[...] = wide[...].T


def unpack(kind, me, side, part, into=()):
    _, r, w = part.shape
    half = 8 * r
    at = lambda me: (me[0] // 8) ^ side
    scratch = []
    if kind == "down":
        outs = [(sds((2 * half, w), F32), pl.BlockSpec((half, w), lambda i, me: (at(me), 0)))]
    elif kind == "up":
        f = half
        outs = [
            (sds((2 * half, w - f), F32), pl.BlockSpec((half, w - f), lambda i, me: (at(me), 0))),
            (sds((f, 2 * half), F32), pl.BlockSpec((f, half), lambda i, me: (0, at(me)))),
        ]
        scratch = [pltpu.VMEM((half, f), F32)]
    else:
        f = w // 3
        outs = [(sds((3, 2 * half, f), F32), pl.BlockSpec((3, half, f), lambda i, me: (0, at(me), 0)))]
    ins = [(part, pl.BlockSpec(part.shape, lambda i, me: (0, 0, 0)))]
    ins += [(t, pl.BlockSpec(memory_space=pl.ANY)) for t in into]
    return packed_call(
        functools.partial(unpack_body, kind),
        (1,),
        me,
        ins,
        outs,
        scratch=scratch,
        aliases={2 + i: i for i in range(len(into))},
        name="unpack_" + kind,
    )


def fold(*parts):
    return sum(p.astype(F32) for p in parts).astype(BF16)


def after(value, *first):
    return lax.optimization_barrier((value, first))[0]


class Chunk:
    def __init__(self, outer, keep, got, order):
        every = {"x": ("x", 2, 1), "z": ("o", outer, 1), "w": ("o", outer, 2)}
        self.steps = [every[name] for name in order]
        self.extra = [("o", outer, 1 << b) for b in range(2, outer.bit_length() - 1)]
        self.keep, self.got = keep, got
        self.sent = None

    def wait(self, *also):
        self.got, also = lax.optimization_barrier((self.got, also))
        return also

    def to_partner(self):
        total = fold(self.keep, self.got)
        self.keep, self.sent = total[1], total[0]
        self.got = lax.ppermute(self.sent, "tensor", FLIP)

    def scatter(self, number):
        total = fold(self.keep, self.got)
        half = total.shape[-3] // 2
        self.keep, self.sent = total[..., :half, :, :], total[..., half:, :, :]
        self.got = flip_bit(self.sent, *self.steps[number])

    def all_summed(self):
        total = fold(self.keep, self.got)
        for s in self.extra:
            total = fold(total, flip_bit(total, *s))
        self.keep = self.sent = total

    def gather(self, number):
        self.got = flip_bit(self.keep, *self.steps[number])

    def joined(self):
        self.keep = self.sent = jnp.concatenate([self.keep, self.got], axis=0)

    def gather_core(self):
        self.got = lax.ppermute(self.keep, "core", FLIP)


def mask_biases(seg):
    seq = seg.shape[1]
    place = jnp.arange(seq, dtype=jnp.int32)
    same = seg[:, :, None] == seg[:, None, :]
    below = (place[:, None] < place[None, :])[None]
    incl = (place[:, None] <= place[None, :])[None]
    bias = lambda m: jnp.where(same & m, 0.0, NEG).astype(F32)
    return bias(incl), bias(below)


def sync(*values):
    return lax.optimization_barrier(values)


class Link:
    def __init__(self, outer, w_qkv, w_out, w_up, w_down):
        self.outer = outer
        self.own = (w_qkv, w_out, w_up, w_down)
        self.core_at, self.x_at, o = (lax.axis_index(a) for a in ("core", "x", "o"))
        bits = {"x": self.x_at, "z": o % 2, "w": (o // 2) % 2}
        self.fetch_bits = self.core_at * 2 + self.x_at
        self.me = {}
        for order in ("zxw", "xzw"):
            slot = self.core_at
            for name in order:
                slot = slot * 2 + bits[name]
            self.me[order] = jnp.stack([slot, self.fetch_bits]).astype(jnp.int32)

    def quarter(self, own):
        flat = own.reshape(-1, own.shape[-1])
        return take_half(take_half(flat, self.core_at), self.x_at)

    def over_x(self, t):
        return lax.ppermute(t, "x", FLIP)

    def fetch(self, own_work):
        own = self.own
        size = own[2].shape[1] // 4
        part = lambda t, axis, bits: lax.dynamic_slice_in_dim(t, bits * size, size, axis)
        pieces = [
            self.quarter(own[1]),
            part(own[2], 1, self.fetch_bits),
            jnp.concatenate([part(own[3], 0, self.fetch_bits), part(own[3], 0, self.fetch_bits ^ 1)], axis=0),
        ]
        qkv = self.partner(self.quarter(own[0]))
        up, out, down = (self.partner(pieces[i]) for i in (1, 0, 2))
        qkv, own_work = sync(qkv, own_work)
        qkv, out, up = sync(ordered(self.x_at, qkv, self.over_x(qkv)).reshape(-1, qkv.shape[-1]), out, up)
        qkv_core, out_x, up_x = self.core(qkv), self.over_x(out), self.over_x(up)
        qkv = ordered(self.core_at, qkv, qkv_core).reshape(own[0].shape)

        def rest(*work):
            nonlocal out, up, out_x, up_x, down
            work, out, up, out_x, up_x = lax.optimization_barrier((work, out, up, out_x, up_x))
            ups = jnp.concatenate([up, up_x], axis=1)
            ups_core = self.core(ups)
            out = ordered(self.x_at, out, out_x).reshape(-1, out.shape[-1])
            out = ordered(self.core_at, out, self.core(out)).reshape(own[1].shape)
            wout = jnp.concatenate([own[1], out], axis=0)
            wup = jnp.concatenate([own[2], ups, ups_core], axis=1)
            down = after(down, wout, wup)
            wdown = jnp.concatenate([own[3], down, self.core(down)], axis=0)
            return work, wout, wup, wdown

        return own_work, own[0], qkv, jnp.concatenate([own[0], qkv], axis=2), rest

    def partner(self, t):
        return lax.ppermute(t, "tensor", FLIP)

    def core(self, t):
        return lax.ppermute(t, "core", FLIP)

    def chunk(self, keep, got, order):
        return Chunk(self.outer, keep, got, order)

    def small_steps(self):
        return [("core", 2, 1), ("tensor", 2, 1)] + steps_of(self.outer)

    def flip(self, t, step):
        return flip_bit(t, *step)


def local_part(x, seg, cot, gb, link):
    rows, seq = seg.shape
    n, width = x.shape
    me_z, me_x = link.me["zxw"], link.me["xzw"]
    incl, strict = mask_biases(seg)
    normal, _ = norm_stats(x.astype(F32))
    a_e = (normal * gb[0] + gb[2]).astype(BF16)
    first = attend_first(a_e, link.own[0], incl)
    (a_e, first), wq_own, fetched, wqkv, rest = link.fetch((a_e, first))
    second = attend_first(a_e, fetched, incl)
    qkv_e, o1 = (jnp.concatenate([s, t], axis=-1) for s, t in zip(first[:2], second[:2]))
    lse1 = jnp.concatenate([first[2], second[2]], axis=0).reshape(-1, GROUP // HD, n)
    (qkv_e, o1, lse1, wqkv), wout, wup, wdown = rest(qkv_e, o1, lse1, wqkv)
    h1, n2_1, g1, d1, ho, a_o = mlp_first(x, o1, wout, gb, wup, wdown)
    qkv_o, o2, lse2 = attend_second(a_o, wqkv, incl, strict, qkv_e, o1, lse1)
    out, n2_2, g2, du2, dh1_2, dp2, do2, sums2, dm2 = mlp_second(x, ho, o2, cot, wout, gb, wup, wdown, seq)
    out_got = link.partner(out[: rows // 2])
    dqkv_o, part, dy, sums_o = attend_back(wqkv, incl, strict, qkv_e, qkv_o, o2, lse2, do2, dh1_2, ho, gb)
    o2_flat = o2.reshape(2 * n, width)

    dm1 = dy.astype(BF16)
    out_got, dm1 = sync(out_got, dm1)
    down_go = grad_down(me_z, 1, g1, g2, dm1, dm2)
    down_got = link.core(down_go)
    down_keep = grad_down(me_z, 0, g1, g2, dm1, after(dm2, down_go))
    down = link.chunk(down_keep, down_got, "zxw")
    (down.keep,) = down.wait(down_keep)
    down.to_partner()
    du1, dh1_1, dp1, do1, sums1 = mlp_back(after(dy, down.sent), h1, wout, gb, d1, wup, wdown, seq)
    parts = (n2_1, n2_2, du1, du2, dp1, dp2, o1)
    up_go = grad_up(me_x, 1, *parts, o2_flat)
    (up_go,) = down.wait(up_go)
    down.scatter(0)
    up_got = link.core(up_go)
    up_keep = grad_up(me_x, 0, *parts, after(o2_flat, up_go, down.sent))
    up = link.chunk(up_keep, up_got, "xzw")
    (up.keep,) = up.wait(up_keep)
    up.scatter(0)
    do1 = after(do1, up.sent)
    dqkv_e, gt, sums_e = attend_back_even(wqkv, incl, qkv_e, o1, lse1, do1, o2, lse2, do2, part, dh1_1, dh1_2, x, gb)
    dqkv_e, gt, sums_e = down.wait(dqkv_e, gt, sums_e)
    down.scatter(1)
    small = jnp.stack([sums_e[0] + sums_o[0], sums1[0] + sums2[0], sums_e[1] + sums_o[1], sums1[1] + sums2[1], sums_o[2]])
    qkv_go = grad_qkv(me_z, 1, a_e, a_o, after(dqkv_e, down.sent), dqkv_o)
    (qkv_go,) = up.wait(qkv_go)
    up.to_partner()
    qkv_got = link.core(qkv_go)
    small_steps = iter(link.small_steps())
    small_got = link.flip(after(small, qkv_go), next(small_steps))
    qkv_keep = grad_qkv(me_z, 0, a_e, a_o, after(dqkv_e, up.sent, qkv_go), dqkv_o)
    qkv = link.chunk(qkv_keep, qkv_got, "zxw")
    qkv.keep, down.got = qkv.wait(qkv_keep, down.got)
    qkv.to_partner()

    def small_hop(chunk):
        nonlocal small, small_got
        small = small + chunk.wait(small_got)[0]
        step = next(small_steps, None)
        small_got = None if step is None else link.flip(small, step)

    def then(chunk, previous, *what):
        chunk.wait(previous.sent)
        for name, *args in what:
            getattr(chunk, name)(*args)

    gt_got = link.partner(after(gt, qkv.sent))
    then(down, qkv, ("scatter", 2))
    small_hop(up)
    then(up, down, ("scatter", 1))
    small_hop(qkv)
    then(qkv, up, ("scatter", 0))
    out_last = link.partner(after(out[rows // 2 :], qkv.sent))
    small_hop(down)
    then(down, qkv, ("all_summed",), ("gather", 2))
    then(down, up, ("joined",), ("gather", 1))
    then(qkv, down, ("scatter", 1))
    then(up, qkv, ("scatter", 2))
    small_hop(down)
    then(down, up, ("joined",), ("gather", 0))
    then(qkv, down, ("scatter", 2))
    (gt_got,) = up.wait(gt_got)
    small_hop(up)
    while small_got is not None:
        small_hop(up)
    then(up, qkv, ("all_summed",), ("gather", 2))
    then(qkv, up, ("all_summed",), ("gather", 2))
    out, gt = link.finish(out, sync(jnp.concatenate([out_got, out_last], axis=0), qkv.sent)[0], gt, gt_got)
    then(down, qkv, ("joined",), ("gather_core",))
    then(up, down, ("joined",), ("gather", 1))
    then(qkv, up, ("joined",), ("gather", 1))
    (g_down,) = unpack("down", me_z, 0, after(down.keep, qkv.sent))
    out, gt, *_ = down.wait(out, gt, g_down)
    g_down, = unpack("down", me_z, 1, down.got, (g_down,))
    qkv.wait(g_down, out, gt)
    qkv.joined()
    qkv.gather(0)
    then(up, qkv, ("joined",), ("gather", 0))
    then(qkv, up, ("joined",), ("gather_core",))
    (g_qkv,) = unpack("qkv", me_z, 0, qkv.keep)
    (g_qkv,) = up.wait(g_qkv)
    up.joined()
    up.gather_core()
    g_up = unpack("up", me_x, 0, up.keep)
    qkv.wait(up.sent)
    (g_qkv,) = unpack("qkv", me_z, 1, qkv.got, (g_qkv,))
    up.wait(g_qkv, *g_up)
    g_up, g_out = unpack("up", me_x, 1, up.got, g_up)
    return out, gt, (g_qkv, g_out, g_up, g_down), small


def shards(outer, tokens, segments, pass_embed, w_qkv, w_out, w_up, w_down, gain, bias, cotangent):
    ty = lax.axis_index("tensor")
    rows = tokens.shape[0] // 2
    width = tokens.shape[2]
    mine = lambda t: lax.dynamic_slice_in_dim(t, ty * rows, rows, 0)
    x = mine(tokens).reshape(-1, width)
    gb = jnp.concatenate([gain, bias, pass_embed[None]], axis=0)
    link = Link(outer, w_qkv, w_out, w_up, w_down)
    link.finish = lambda out, out_got, gt, gt_got: (
        ordered(ty, out, out_got).reshape(cotangent.shape),
        ordered(ty, gt, gt_got).reshape(tokens.shape).astype(F32),
    )
    out, gt, grads, small = local_part(x, mine(segments), mine(cotangent), gb, link)
    return out, gt, *grads, small[0:2], small[2:4], small[4]


def solution(mesh):
    outer = mesh.shape["dp"] // 4
    fine = Mesh(mesh.devices.reshape(outer, 2, 2, mesh.shape["tensor"]), ("o", "x", "core", "tensor"))
    rows = ROWS_OVER
    placed = (
        P(rows, None, None),
        P(rows, None),
        P(),
        P(None, None, "tensor"),
        P("tensor", None),
        P(None, "tensor"),
        P("tensor", None),
        P(),
        P(),
        P(rows, None, None),
    )

    def body(*args):
        return shards(outer, *args)

    return jax.shard_map(
        body,
        mesh=fine,
        in_specs=placed,
        out_specs=(
            P(rows, None, None),
            P(rows, None, None),
            P(None, None, "tensor"),
            P("tensor", None),
            P(None, "tensor"),
            P("tensor", None),
            P(),
            P(),
            P(),
        ),
        check_vma=False,
    )
```

time: 551 us -> 433 us (0.79)
  waiting for transfers between devices: 208 us -> 87.8 us
  Pallas kernels: 216 us -> 198 us
  starting transfers between devices: 33.6 us -> 49.3 us
  local copies, waits for them, and re-layouts: 23.2 us -> 35.7 us
  other arithmetic: 58.6 us -> 52.2 us
    ppermute x21 -> x16, waiting for transfers between devices: 108 us -> 13.3 us  [the longest x3 6.9 us: over_x(): return lax.ppermute(t, 'x', FLIP)]
    pallas_call x8 -> x3, Pallas kernels: 152 us -> 69.3 us  [call(): pl.pallas_call(body, grid=grid, in_specs=[s for _, s in ins], out_specs=[...]
    pallas_call x0 -> x5, Pallas kernels: none -> 46.2 us  [resident(): pl.pallas_call(body, in_specs=[s for _, s in ins], out_specs=[s for _, s...]
    ppermute x23, waiting for transfers between devices: 92.7 us -> 64.3 us  [flip_bit(): return lax.ppermute(array, axis, [(i, i ^ bit) for i in range(size)])]
    pallas_call x9 -> x12, Pallas kernels: 63.8 us -> 82.4 us  [packed_call(): pl.pallas_call(body, grid_spec=pltpu.PrefetchScalarGridSpec(num_scalar_pr...]
    ppermute x23, starting transfers between devices: 16.7 us -> 31.7 us  [flip_bit(): return lax.ppermute(array, axis, [(i, i ^ bit) for i in range(size)])]
    another operation x20 -> x12, other arithmetic: 18.8 us -> 8.74 us  [ordered(): jnp.stack([jnp.where(first, mine, theirs), jnp.where(first, theirs, mine)])]
    unnamed x55 -> x103, local copies, waits for them, and re-layouts: 8.44 us -> 15.9 us
  transfers between devices with their start and end apart: 46 -> 46, of which waited for: 23 -> 20; matrix products, arithmetic and copies ran while one was open for 13% -> 14% of each run, Pallas kernels for 18% -> 28%
where the time goes in v1:
time: 433 us; the launch traced here: 425 us
  Pallas kernels  198 us (46%)
  waiting for transfers between devices  87.8 us (20%)
  other arithmetic  52.2 us (12%)
  starting transfers between devices  49.3 us (11%)
  local copies, waits for them, and re-layouts  35.7 us (8%)
    pallas_call x12, Pallas kernels, packed_call(): pl.pallas_call(body, grid_spec=pltpu.PrefetchScalarGridSpec(num_scalar_pr...  82.4 us
    pallas_call x3, Pallas kernels, call(): pl.pallas_call(body, grid=grid, in_specs=[s for _, s in ins], out_specs=[...  69.3 us
    ppermute x23, waiting for transfers between devices, flip_bit(): return lax.ppermute(array, axis, [(i, i ^ bit) for i in range(size)])  64.3 us
    pallas_call x5, Pallas kernels, resident(): pl.pallas_call(body, in_specs=[s for _, s in ins], out_specs=[s for _, s...  46.2 us
    ppermute x23, starting transfers between devices, flip_bit(): return lax.ppermute(array, axis, [(i, i ^ bit) for i in range(size)])  31.7 us
    convert_element_type x15, other arithmetic, fold(): return sum((p.astype(F32) for p in parts)).astype(BF16)  18.3 us
    unnamed x103, local copies, waits for them, and re-layouts  15.9 us
    ppermute x7, waiting for transfers between devices, partner(): return lax.ppermute(t, 'tensor', FLIP)  10.2 us
  transfers between devices with their start and end apart: 46, of which 20 were waited for; matrix products, arithmetic and copies ran while one was open for 14% of the time, Pallas kernels for 28%

profile of v1, /device:TPU:0, one launch (start us, length us, event | category | flops | bytes accessed | tf_op | source)
XLA Modules:
  0.0 424.6 jit_solution(5494321724583071258)
XLA Ops:
  0.7 2.0 constant_dynamic-slice_fusion.6
  2.7 3.0 collective-permute-start
  9.7 2.4 attend_first.2
  14.1 2.1 collective-permute-done
  16.2 1.7 collective-permute-start.1
  17.9 1.9 constant_dynamic-slice_fusion.3
  19.8 1.5 collective-permute-start.3
  21.3 1.6 constant_dynamic-slice_fusion.4
  23.5 4.4 %collective-permute-done.1 = bf16[576,384]{1,0:T(8,128)(2,1)} collective-permute-done((bf16[576,384]{1,0:T(8,128)(2,1)}, bf16[576,384]{1,0:T(8,128)(2,1)}, u32[]{:S(2)}, u32[]{:S(2)}) %collective-permute-start.1) | collective-permute-done | bytes 442400 | tf_op jit(solution)/shard_map/ppermute | solution.py:1117
  30.1 7.1 %collective-permute-done.2 = bf16[96,768]{1,0:T(8,128)(2,1)} collective-permute-done((bf16[96,768]{1,0:T(8,128)(2,1)}, bf16[96,768]{1,0:T(8,128)(2,1)}, u32[]{:S(2)}, u32[]{:S(2)}) %collective-permute-start.2) | collective-permute-done | bytes 147488 | tf_op jit(solution)/shard_map/ppermute | solution.py:1151
  39.6 1.5 collective-permute-start.9
  43.2 1.6 select_bitcast_fusion.3
  46.1 2.4 attend_first.3
  49.3 1.6 pad_maximum_fusion.2.qkve_far
  51.5 2.1 pad_maximum_fusion.w_far
  55.6 1.9 pad_maximum_fusion.13.o_ref.o1_far.o1_ref
  57.6 2.5 collective-permute-done.6
  72.4 2.2 copy-done.16
  74.6 16.1 %mlp_first.1 = (f32[512,768]{1,0:T(8,128)}, bf16[512,768]{1,0:T(8,128)(2,1)}, bf16[512,3072]{1,0:T(8,128)(2,1)}, bf16[512,3072]{1,0:T(8,128)(2,1)}, f32[512,768]{1,0:T(8,128)}, /*index=5*/bf16[512,768]{1,0:T(8,128)(2,1)}) custom-call(bf16[512,768]{1,0:T(8,128)(2,1)} %bitcast.73, bf16[512,768]{1,0:T(8,128)(2,1)} %pad_maximum_fusion.13.o_ref.o1_far.o1_ref, ...), custom_call_target="tpu_custom_call" | custom-call | flops 339738624 | tf_op jit(solution)/shard_map/mlp_first/pallas_call | solution.py:87
  90.6 13.2 %attend_second.1 = (bf16[3,512,768]{2,1,0:T(8,128)(2,1)}, bf16[2,512,768]{2,1,0:T(8,128)(2,1)}, f32[2,3,4,512]{3,2,1,0:T(4,128)S(1)}) custom-call(bf16[512,768]{1,0:T(8,128)(2,1)} %get-tuple-element.152.a_far.ao_ref, bf16[3,768,768]{2,1,0:T(8,128)(2,1)} %pad_maximum_fusion.w_far, f32[2,256,256]{2,1,0:T(8,128)} %copy-done.4, ...), custom_call_target="tpu_custom_call" | custom-call | flops 415236096 | tf_op jit(solution)/shard_map/attend_second/pallas_call | solution.py:112
  103.8 38.1 %mlp_second.1 = (bf16[2,512,768]{2,1,0:T(8,128)(2,1)}, bf16[1024,768]{1,0:T(8,128)(2,1)}, bf16[1024,3072]{1,0:T(8,128)(2,1)}, bf16[1024,3072]{1,0:T(8,128)(2,1)}...) custom-call(bf16[512,768]{1,0:T(8,128)(2,1)} %bitcast.74, ...), custom_call_target="tpu_custom_call" | custom-call | flops 1358954496 | tf_op jit(solution)/shard_map/mlp_second/pallas_call | solution.py:87
  141.9 2.6 fusion.8
  146.2 17.0 %attend_back.1 = (bf16[3,512,768]{2,1,0:T(8,128)(2,1)}, bf16[3,512,768]{2,1,0:T(8,128)(2,1)}, f32[512,768]{1,0:T(8,128)S(1)}, f32[3,768]{1,0:T(4,128)S(1)}) custom-call(bf16[3,768,768]{2,1,0:T(8,128)(2,1)} %pad_maximum_fusion.w_far, f32[2,256,256]{2,1,0:T(8,128)} %copy-done.4, f32[2,256,256]{2,1,0:T(8,128)} %get-tuple-element.276.strict_far, ...), custom_call_target="tpu_custom_call" | custom-call | flops 868220928 | tf_op jit(solution)/shard_map/attend_back/pallas_call | solution.py:112
  164.3 8.7 %grad_down.2 = bf16[2,8,96,768]{3,2,1,0:T(8,128)(2,1)} custom-call(s32[2]{0:T(128)} %pad_add_fusion.me_ref, bf16[512,3072]{1,0:T(8,128)(2,1)} %get-tuple-element.150.g1_ref, bf16[1024,3072]{1,0:T(8,128)(2,1)} %get-tuple-element.157.g2_ref, bf16[512,768]{1,0:T(8,128)(2,1)} %convert_element_type.166.dm1_ref, bf16[1024,768]{1,0:T(8,128)(2,1)} %get-tuple-element.166.dm2_ref), custom_call_target="tpu_custom_call" | custom-call | flops 226492416 | tf_op jit(solution)/shard_map/grad_down/pallas_call | solution.py:823
  173.2 8.7 %grad_down.3 = bf16[2,8,96,768]{3,2,1,0:T(8,128)(2,1)} custom-call(s32[2]{0:T(128)} %pad_add_fusion.me_ref, bf16[512,3072]{1,0:T(8,128)(2,1)} %get-tuple-element.150.g1_ref, bf16[1024,3072]{1,0:T(8,128)(2,1)} %get-tuple-element.157.g2_ref, bf16[512,768]{1,0:T(8,128)(2,1)} %convert_element_type.166.dm1_ref, bf16[1024,768]{1,0:T(8,128)(2,1)} %get-tuple-element.166.dm2_ref), custom_call_target="tpu_custom_call" | custom-call | flops 226492416 | tf_op jit(solution)/shard_map/grad_down/pallas_call | solution.py:823
  181.9 3.1 add_convert_fusion.1
  189.6 15.1 %mlp_back.1 = (bf16[512,3072]{1,0:T(8,128)(2,1)}, f32[512,768]{1,0:T(8,128)}, bf16[512,768]{1,0:T(8,128)(2,1)}, bf16[512,768]{1,0:T(8,128)(2,1)}, f32[2,768]{1,0:T(2,128)}) custom-call(f32[512,768]{1,0:T(8,128)} %copy-done.8, f32[512,768]{1,0:T(8,128)} %get-tuple-element.172.h1_ref, bf16[768,768]{1,0:T(8,128)(2,1)} %pad_maximum_fusion.7.wout_ref, ...), custom_call_target="tpu_custom_call" | custom-call | flops 339738624 | tf_op jit(solution)/shard_map/mlp_back/pallas_call | solution.py:87
  204.7 15.2 %grad_up.2 = bf16[2,8,48,1920]{3,2,1,0:T(8,128)(2,1)} custom-call(s32[2]{0:T(128)} %pad_add_fusion.1.me_ref, bf16[512,768]{1,0:T(8,128)(2,1)} %get-tuple-element.169.n1_ref, bf16[1024,768]{1,0:T(8,128)(2,1)} %get-tuple-element.170.n2_ref, bf16[512,3072]{1,0:T(8,128)(2,1)} %get-tuple-element.174.du1_ref, bf16[1024,3072]{1,0:T(8,128)(2,1)} %get-tuple-element.175.du2_ref, ...), custom_call_target="tpu_custom_call" | custom-call | flops 283115520 | tf_op jit(solution)/shard_map/grad_up/pallas_call | solution.py:823
  221.1 1.9 fusion
  223.1 15.5 %grad_up.3 = bf16[2,8,48,1920]{3,2,1,0:T(8,128)(2,1)} custom-call(s32[2]{0:T(128)} %pad_add_fusion.1.me_ref, bf16[512,768]{1,0:T(8,128)(2,1)} %get-tuple-element.169.n1_ref, bf16[1024,768]{1,0:T(8,128)(2,1)} %get-tuple-element.170.n2_ref, bf16[512,3072]{1,0:T(8,128)(2,1)} %get-tuple-element.174.du1_ref, bf16[1024,3072]{1,0:T(8,128)(2,1)} %get-tuple-element.175.du2_ref, ...), custom_call_target="tpu_custom_call" | custom-call | flops 283115520 | tf_op jit(solution)/shard_map/grad_up/pallas_call | solution.py:823
  238.6 3.4 add_convert_fusion
  244.0 1.6 collective-permute-start.14
  245.6 11.2 %attend_back_even.1 = (bf16[3,512,768]{2,1,0:T(8,128)(2,1)}, bf16[512,768]{1,0:T(8,128)(2,1)S(1)}, f32[2,768]{1,0:T(2,128)S(1)}) custom-call(bf16[3,768,768]{2,1,0:T(8,128)(2,1)} %pad_maximum_fusion.w_far, f32[2,256,256]{2,1,0:T(8,128)} %copy-done.4, bf16[3,512,768]{2,1,0:T(8,128)(2,1)} %pad_maximum_fusion.2.qkve_far, ...), custom_call_target="tpu_custom_call" | custom-call | flops 364904448 | tf_op jit(solution)/shard_map/attend_back_even/pallas_call | solution.py:112
  256.8 2.4 collective-permute-done.14
  259.4 6.5 %grad_qkv.2 = bf16[2,8,48,1152]{3,2,1,0:T(8,128)(2,1)} custom-call(s32[2]{0:T(128)} %pad_add_fusion.me_ref, bf16[512,768]{1,0:T(8,128)(2,1)} %copy-done.2, bf16[512,768]{1,0:T(8,128)(2,1)} %get-tuple-element.152.a_far.ao_ref, bf16[3,512,768]{2,1,0:T(8,128)(2,1)} %get-tuple-element.196.de_ref, bf16[3,512,768]{2,1,0:T(8,128)(2,1)} %get-tuple-element.193.do_ref), custom_call_target="tpu_custom_call" | custom-call | flops 113246208 | tf_op jit(solution)/shard_map/grad_qkv/pallas_call | solution.py:823
  265.9 12.3 %collective-permute-done.16 = bf16[2,4,48,1920]{3,2,1,0:T(8,128)(2,1)} collective-permute-done((bf16[2,4,48,1920]{3,2,1,0:T(8,128)(2,1)}, bf16[2,4,48,1920]{3,2,1,0:T(8,128)(2,1)}, u32[]{:S(2)}, u32[]{:S(2)}) %collective-permute-start.16) | collective-permute-done | bytes 1474592 | tf_op jit(solution)/shard_map/ppermute | solution.py:32
  278.9 2.2 add_convert_fusion.3
  282.7 6.5 %grad_qkv.3 = bf16[2,8,48,1152]{3,2,1,0:T(8,128)(2,1)} custom-call(s32[2]{0:T(128)} %pad_add_fusion.me_ref, bf16[512,768]{1,0:T(8,128)(2,1)} %copy-done.2, bf16[512,768]{1,0:T(8,128)(2,1)} %get-tuple-element.152.a_far.ao_ref, bf16[3,512,768]{2,1,0:T(8,128)(2,1)} %get-tuple-element.196.de_ref, bf16[3,512,768]{2,1,0:T(8,128)(2,1)} %get-tuple-element.193.do_ref), custom_call_target="tpu_custom_call" | custom-call | flops 113246208 | tf_op jit(solution)/shard_map/grad_qkv/pallas_call | solution.py:823
  289.3 2.4 add_convert_fusion.2
  295.4 6.3 %collective-permute-done.20 = bf16[4,48,1920]{2,1,0:T(8,128)(2,1)} collective-permute-done((bf16[4,48,1920]{2,1,0:T(8,128)(2,1)}, bf16[4,48,1920]{2,1,0:T(8,128)(2,1)}, u32[]{:S(2)}, u32[]{:S(2)}) %collective-permute-start.20) | collective-permute-done | bytes 737312 | tf_op jit(solution)/shard_map/ppermute | solution.py:1060
  303.4 2.7 collective-permute-start.19
  307.6 12.7 %collective-permute-done.23 = f32[5,768]{1,0:T(8,128)S(1)} collective-permute-done((f32[5,768]{1,0:T(8,128)S(1)}, f32[5,768]{1,0:T(8,128)S(1)}, u32[]{:S(2)}, u32[]{:S(2)}) %collective-permute-start.23) | collective-permute-done | bytes 15392 | tf_op jit(solution)/shard_map/ppermute | solution.py:32
  320.4 1.6 collective-permute-start.24
  323.4 1.7 collective-permute-start.29
  325.1 2.6 collective-permute-start.25
  329.3 9.5 %collective-permute-done.25 = bf16[1,96,768]{2,1,0:T(8,128)(2,1)S(1)} collective-permute-done((bf16[1,96,768]{2,1,0:T(8,128)(2,1)S(1)}, bf16[1,96,768]{2,1,0:T(8,128)(2,1)S(1)}, u32[]{:S(2)}, u32[]{:S(2)}) %collective-permute-start.25) | collective-permute-done | bytes 147488 | tf_op jit(solution)/shard_map/ppermute | solution.py:32
  341.0 4.8 %collective-permute-done.28 = bf16[2,48,1920]{2,1,0:T(8,128)(2,1)S(1)} collective-permute-done((bf16[2,48,1920]{2,1,0:T(8,128)(2,1)S(1)}, bf16[2,48,1920]{2,1,0:T(8,128)(2,1)S(1)}, u32[]{:S(2)}, u32[]{:S(2)}) %collective-permute-start.28) | collective-permute-done | bytes 368672 | tf_op jit(solution)/shard_map/ppermute | solution.py:32
  345.9 2.7 collective-permute-start.33
  348.6 1.6 collective-permute-start.27
  353.0 2.0 collective-permute-start.35
  358.6 1.9 convert.7
  360.7 2.2 collective-permute-start.32
  364.7 6.2 %collective-permute-done.32 = bf16[1,48,1152]{2,1,0:T(8,128)(2,1)S(1)} collective-permute-done((bf16[1,48,1152]{2,1,0:T(8,128)(2,1)S(1)}, bf16[1,48,1152]{2,1,0:T(8,128)(2,1)S(1)}, u32[]{:S(2)}, u32[]{:S(2)}) %collective-permute-start.32) | collective-permute-done | bytes 110624 | tf_op jit(solution)/shard_map/ppermute | solution.py:32
  371.0 3.5 collective-permute-start.38
  380.5 2.0 collective-permute-start.42
  382.5 1.9 pad_maximum_fusion.1
  384.5 3.5 unpack_down.2.refs_0_
  387.9 3.5 unpack_down.3
  393.6 9.4 %collective-permute-done.41 = bf16[4,48,1152]{2,1,0:T(8,128)(2,1)S(1)} collective-permute-done((bf16[4,48,1152]{2,1,0:T(8,128)(2,1)S(1)}, bf16[4,48,1152]{2,1,0:T(8,128)(2,1)S(1)}, u32[]{:S(2)}, u32[]{:S(2)}) %collective-permute-start.41) | collective-permute-done | bytes 442400 | tf_op jit(solution)/shard_map/ppermute | solution.py:32
  404.1 3.2 unpack_qkv.2.refs_0_
  407.2 2.0 collective-permute-done.44
  412.3 3.9 unpack_up.2
  417.1 3.2 unpack_qkv.3
  420.3 4.1 unpack_up.3
  (241 shorter events, 76.8 us)
Async XLA Ops:
  0.6 68.3 %copy-start = (bf16[4,512,768]{2,1,0:T(8,128)(2,1)S(1)}, bf16[4,512,768]{2,1,0:T(8,128)(2,1)}, u32[]{:S(2)}) copy-start(bf16[4,512,768]{2,1,0:T(8,128)(2,1)} %param.19) | copy-start | bytes 9437188
  2.7 13.4 %collective-permute-start = (bf16[576,384]{1,0:T(8,128)(2,1)}, bf16[576,384]{1,0:T(8,128)(2,1)}, u32[]{:S(2)}, u32[]{:S(2)}) collective-permute-start(bf16[576,384]{1,0:T(8,128)(2,1)} %constant_dynamic-slice_fusion.6), channel_id=1, source_target_pairs={{0,1},{1,0},{2,3},{3,2},{4,5},{5,4},{6,7},{7,6},{8,9},{9,8},{10,11... | collective-permute-start | bytes 1327112 | tf_op jit(solution)/shard_map/ppermute | solution.py:1151
  16.2 11.7 %collective-permute-start.1 = (bf16[576,384]{1,0:T(8,128)(2,1)}, bf16[576,384]{1,0:T(8,128)(2,1)}, u32[]{:S(2)}, u32[]{:S(2)}) collective-permute-start(bf16[576,384]{1,0:T(8,128)(2,1)} %collective-permute-done), channel_id=1, source_target_pairs={{0,4},{4,0},{1,5},{5,1},{2,6},{6,2},{3,7},{7,3},{8,12},{12,8},{9,1... | collective-permute-start | bytes 1327112 | tf_op jit(solution)/shard_map/ppermute | solution.py:1117
  19.8 17.4 %collective-permute-start.3 = (bf16[768,384]{1,0:T(8,128)(2,1)}, bf16[768,384]{1,0:T(8,128)(2,1)}, u32[]{:S(2)}, u32[]{:S(2)}) collective-permute-start(bf16[768,384]{1,0:T(8,128)(2,1)} %constant_dynamic-slice_fusion.3), channel_id=1, source_target_pairs={{0,1},{1,0},{2,3},{3,2},{4,5},{5,4},{6,7},{7,6},{8,9},{9,8},{10,11... | collective-permute-start | bytes 1769480 | tf_op jit(solution)/shard_map/ppermute | solution.py:1151
  22.9 14.3 %collective-permute-start.2 = (bf16[96,768]{1,0:T(8,128)(2,1)}, bf16[96,768]{1,0:T(8,128)(2,1)}, u32[]{:S(2)}, u32[]{:S(2)}) collective-permute-start(bf16[96,768]{1,0:T(8,128)(2,1)} %constant_dynamic-slice_fusion.4), channel_id=1, source_target_pairs={{0,1},{1,0},{2,3},{3,2},{4,5},{5,4},{6,7},{7,6},{8,9},{9,8},{10,11... | collective-permute-start | bytes 442376 | tf_op jit(solution)/shard_map/ppermute | solution.py:1151
  37.2 6.0 %collective-permute-start.4 = (bf16[1152,384]{1,0:T(8,128)(2,1)}, bf16[1152,384]{1,0:T(8,128)(2,1)}, u32[]{:S(2)}, u32[]{:S(2)}) collective-permute-start(bf16[1152,384]{1,0:T(8,128)(2,1)} %bitcast.6), channel_id=1, source_target_pairs={{0,2},{2,0},{1,3},{3,1},{4,6},{6,4},{5,7},{7,5},{8,10},{10,8},{9,1... | collective-permute-start | bytes 2654216 | tf_op jit(solution)/shard_map/ppermute | solution.py:1154
  39.6 28.7 %collective-permute-start.9 = (bf16[768,768]{1,0:T(8,128)(2,1)}, bf16[768,768]{1,0:T(8,128)(2,1)}, u32[]{:S(2)}, u32[]{:S(2)}) collective-permute-start(bf16[768,768]{1,0:T(8,128)(2,1)} %pad_maximum_fusion.9), channel_id=1, source_target_pairs={{0,1},{1,0},{2,3},{3,2},{4,5},{5,4},{6,7},{7,6},{8,9},{9,8},{10,11... | collective-permute-start | bytes 3538952 | tf_op jit(solution)/shard_map/ppermute | solution.py:1151
  41.1 16.4 %collective-permute-start.5 = (bf16[96,768]{1,0:T(8,128)(2,1)}, bf16[96,768]{1,0:T(8,128)(2,1)}, u32[]{:S(2)}, u32[]{:S(2)}) collective-permute-start(bf16[96,768]{1,0:T(8,128)(2,1)} %collective-permute-done.2), channel_id=1, source_target_pairs={{0,4},{4,0},{1,5},{5,1},{2,6},{6,2},{3,7},{7,3},{8,12},{12,8},{9,1... | collective-permute-start | bytes 442376 | tf_op jit(solution)/shard_map/ppermute | solution.py:1117
  41.7 18.4 %collective-permute-start.6 = (bf16[768,384]{1,0:T(8,128)(2,1)}, bf16[768,384]{1,0:T(8,128)(2,1)}, u32[]{:S(2)}, u32[]{:S(2)}) collective-permute-start(bf16[768,384]{1,0:T(8,128)(2,1)} %collective-permute-done.3), channel_id=1, source_target_pairs={{0,4},{4,0},{1,5},{5,1},{2,6},{6,2},{3,7},{7,3},{8,12},{12,8},{9,1... | collective-permute-start | bytes 1769480 | tf_op jit(solution)/shard_map/ppermute | solution.py:1117
  45.0 4.2 %copy-start.10 = (bf16[3,512,384]{2,1,0:T(8,128)(2,1)S(1)}, bf16[3,512,384]{2,1,0:T(8,128)(2,1)}, u32[]{:S(2)}) copy-start(bf16[3,512,384]{2,1,0:T(8,128)(2,1)} %copy-done.9) | copy-start | bytes 3538948
  57.6 5.6 %copy-start.24 = (bf16[768,1536]{1,0:T(8,128)(2,1)S(1)}, bf16[768,1536]{1,0:T(8,128)(2,1)}, u32[]{:S(2)}) copy-start(bf16[768,1536]{1,0:T(8,128)(2,1)} %param.15) | copy-start | bytes 7077892
  61.4 5.8 %collective-permute-start.8 = (bf16[768,768]{1,0:T(8,128)(2,1)S(1)}, bf16[768,768]{1,0:T(8,128)(2,1)S(1)}, u32[]{:S(2)}, u32[]{:S(2)}) collective-permute-start(bf16[768,768]{1,0:T(8,128)(2,1)S(1)} %pad_maximum_fusion.8), channel_id=1, source_target_pairs={{0,2},{2,0},{1,3},{3,1},{4,6},{6,4},{5,7},{7,5},{8,10},{10,8},{9,1... | collective-permute-start | bytes 3538952 | tf_op jit(solution)/shard_map/ppermute | solution.py:1154
  62.5 3.4 collective-permute-start.7
  68.3 4.0 collective-permute-start.10
  74.6 16.1 %copy-start.14 = (f32[3,4,512]{2,1,0:T(4,128)S(1)}, f32[3,4,512]{2,1,0:T(4,128)}, u32[]{:S(2)}) copy-start(f32[3,4,512]{2,1,0:T(4,128)} %reshape.120.lse1_ref) | copy-start | bytes 73732
  141.9 4.3 %copy-start.11 = (f32[5,768]{1,0:T(8,128)S(1)}, f32[5,768]{1,0:T(8,128)}, u32[]{:S(2)}) copy-start(f32[5,768]{1,0:T(8,128)} %pad_maximum_fusion.23.gb_ref) | copy-start | bytes 46084
  144.5 19.8 %collective-permute-start.11 = (bf16[1,512,768]{2,1,0:T(8,128)(2,1)}, bf16[1,512,768]{2,1,0:T(8,128)(2,1)}, u32[]{:S(2)}, u32[]{:S(2)}) collective-permute-start(bf16[1,512,768]{2,1,0:T(8,128)(2,1)} %get-tuple-element.262), channel_id=1, source_target_pairs={{0,1},{1,0},{2,3},{3,2},{4,5},{5,4},{6,7},{7,6},{8,9},{9,8},{10,11... | collective-permute-start | bytes 2359304 | tf_op jit(solution)/shard_map/ppermute | solution.py:1151
  163.2 9.8 %copy-start.8 = (f32[512,768]{1,0:T(8,128)}, f32[512,768]{1,0:T(8,128)S(1)}, u32[]{:S(2)}) copy-start(f32[512,768]{1,0:T(8,128)S(1)} %get-tuple-element.171.dy_ref) | copy-start | bytes 4718596
  173.0 8.9 %collective-permute-start.12 = (bf16[2,8,96,768]{3,2,1,0:T(8,128)(2,1)}, bf16[2,8,96,768]{3,2,1,0:T(8,128)(2,1)}, u32[]{:S(2)}, u32[]{:S(2)}) collective-permute-start(bf16[2,8,96,768]{3,2,1,0:T(8,128)(2,1)} %grad_down.2), channel_id=1, source_target_pairs={{0,2},{2,0},{1,3},{3,1},{4,6},{6,4},{5,7},{7,5},{8,10},{10,8},{9,1... | collective-permute-start | bytes 7077896 | tf_op jit(solution)/shard_map/ppermute | solution.py:1154
  187.6 32.3 %collective-permute-start.13 = (bf16[8,96,768]{2,1,0:T(8,128)(2,1)}, bf16[8,96,768]{2,1,0:T(8,128)(2,1)S(1)}, u32[]{:S(2)}, u32[]{:S(2)}) collective-permute-start(bf16[8,96,768]{2,1,0:T(8,128)(2,1)} %slice_bitcast_fusion), channel_id=1, source_target_pairs={{0,1},{1,0},{2,3},{3,2},{4,5},{5,4},{6,7},{7,6},{8,9},{9,8},{10,11... | collective-permute-start | bytes 3538952 | tf_op jit(solution)/shard_map/ppermute | solution.py:1060
  220.9 17.7 %collective-permute-start.15 = (bf16[2,8,48,1920]{3,2,1,0:T(8,128)(2,1)}, bf16[2,8,48,1920]{3,2,1,0:T(8,128)(2,1)}, u32[]{:S(2)}, u32[]{:S(2)}) collective-permute-start(bf16[2,8,48,1920]{3,2,1,0:T(8,128)(2,1)} %grad_up.2), channel_id=1, source_target_pairs={{0,2},{2,0},{1,3},{3,1},{4,6},{6,4},{5,7},{7,5},{8,10},{10,8},{9,1... | collective-permute-start | bytes 8847368 | tf_op jit(solution)/shard_map/ppermute | solution.py:1154
  243.4 34.8 %collective-permute-start.16 = (bf16[2,4,48,1920]{3,2,1,0:T(8,128)(2,1)}, bf16[2,4,48,1920]{3,2,1,0:T(8,128)(2,1)}, u32[]{:S(2)}, u32[]{:S(2)}) collective-permute-start(bf16[2,4,48,1920]{3,2,1,0:T(8,128)(2,1)} %slice.164), channel_id=1, source_target_pairs={{0,4},{4,0},{1,5},{5,1},{2,6},{6,2},{3,7},{7,3},{8,12},{12,8},{9,1... | collective-permute-start | bytes 4423688 | tf_op jit(solution)/shard_map/ppermute | solution.py:32
  244.0 15.3 %collective-permute-start.14 = (bf16[4,96,768]{2,1,0:T(8,128)(2,1)S(1)}, bf16[4,96,768]{2,1,0:T(8,128)(2,1)S(1)}, u32[]{:S(2)}, u32[]{:S(2)}) collective-permute-start(bf16[4,96,768]{2,1,0:T(8,128)(2,1)S(1)} %slice.163), channel_id=1, source_target_pairs={{0,8},{8,0},{16,24},{24,16},{1,9},{9,1},{17,25},{25,17},{2,10},{10... | collective-permute-start | bytes 1769480 | tf_op jit(solution)/shard_map/ppermute | solution.py:32
  259.4 6.6 %copy-start.26 = (bf16[4,96,768]{2,1,0:T(8,128)(2,1)}, bf16[4,96,768]{2,1,0:T(8,128)(2,1)S(1)}, u32[]{:S(2)}) copy-start(bf16[4,96,768]{2,1,0:T(8,128)(2,1)S(1)} %add_convert_fusion.5) | copy-start | bytes 1769476
  259.4 18.8 %copy-start.45 = (f32[2,768]{1,0:T(2,128)S(1)}, f32[2,768]{1,0:T(2,128)}, u32[]{:S(2)}) copy-start(f32[2,768]{1,0:T(2,128)} %get-tuple-element.204) | copy-start | bytes 18436
  259.4 18.8 %copy-start.46 = (f32[2,768]{1,0:T(2,128)S(1)}, f32[2,768]{1,0:T(2,128)}, u32[]{:S(2)}) copy-start(f32[2,768]{1,0:T(2,128)} %get-tuple-element.203) | copy-start | bytes 18436
  278.2 11.1 %collective-permute-start.17 = (bf16[2,8,48,1152]{3,2,1,0:T(8,128)(2,1)}, bf16[2,8,48,1152]{3,2,1,0:T(8,128)(2,1)}, u32[]{:S(2)}, u32[]{:S(2)}) collective-permute-start(bf16[2,8,48,1152]{3,2,1,0:T(8,128)(2,1)} %grad_qkv.2), channel_id=1, source_target_pairs={{0,2},{2,0},{1,3},{3,1},{4,6},{6,4},{5,7},{7,5},{8,10},{10,8},{9,1... | collective-permute-start | bytes 5308424 | tf_op jit(solution)/shard_map/ppermute | solution.py:1154
  278.3 11.0 %collective-permute-start.18 = (bf16[2,96,768]{2,1,0:T(8,128)(2,1)S(1)}, bf16[2,96,768]{2,1,0:T(8,128)(2,1)S(1)}, u32[]{:S(2)}, u32[]{:S(2)}) collective-permute-start(bf16[2,96,768]{2,1,0:T(8,128)(2,1)S(1)} %slice.166), channel_id=1, source_target_pairs={{0,4},{4,0},{1,5},{5,1},{2,6},{6,2},{3,7},{7,3},{8,12},{12,8},{9,1... | collective-permute-start | bytes 884744 | tf_op jit(solution)/shard_map/ppermute | solution.py:32
  281.0 8.3 %copy-start.21 = (bf16[2,4,48,1920]{3,2,1,0:T(8,128)(2,1)}, bf16[2,4,48,1920]{3,2,1,0:T(8,128)(2,1)S(1)}, u32[]{:S(2)}) copy-start(bf16[2,4,48,1920]{3,2,1,0:T(8,128)(2,1)S(1)} %add_convert_fusion.3) | copy-start | bytes 4423684
  282.1 19.6 %collective-permute-start.20 = (bf16[4,48,1920]{2,1,0:T(8,128)(2,1)}, bf16[4,48,1920]{2,1,0:T(8,128)(2,1)}, u32[]{:S(2)}, u32[]{:S(2)}) collective-permute-start(bf16[4,48,1920]{2,1,0:T(8,128)(2,1)} %slice_bitcast_fusion.5), channel_id=1, source_target_pairs={{0,1},{1,0},{2,3},{3,2},{4,5},{5,4},{6,7},{7,6},{8,9},{9,8},{10,11... | collective-permute-start | bytes 2211848 | tf_op jit(solution)/shard_map/ppermute | solution.py:1060
  292.7 27.6 %collective-permute-start.22 = (bf16[8,48,1152]{2,1,0:T(8,128)(2,1)}, bf16[8,48,1152]{2,1,0:T(8,128)(2,1)}, u32[]{:S(2)}, u32[]{:S(2)}) collective-permute-start(bf16[8,48,1152]{2,1,0:T(8,128)(2,1)} %slice_bitcast_fusion.3), channel_id=1, source_target_pairs={{0,1},{1,0},{2,3},{3,2},{4,5},{5,4},{6,7},{7,6},{8,9},{9,8},{10,11... | collective-permute-start | bytes 2654216 | tf_op jit(solution)/shard_map/ppermute | solution.py:1060
  294.1 1.3 collective-permute-start.21
  301.7 18.7 %collective-permute-start.23 = (f32[5,768]{1,0:T(8,128)S(1)}, f32[5,768]{1,0:T(8,128)S(1)}, u32[]{:S(2)}, u32[]{:S(2)}) collective-permute-start(f32[5,768]{1,0:T(8,128)S(1)} %add.184), channel_id=1, source_target_pairs={{0,1},{1,0},{2,3},{3,2},{4,5},{5,4},{6,7},{7,6},{8,9},{9,8},{10,11... | collective-permute-start | bytes 46088 | tf_op jit(solution)/shard_map/ppermute | solution.py:32
  303.4 21.6 %collective-permute-start.19 = (bf16[1,96,768]{2,1,0:T(8,128)(2,1)S(1)}, bf16[1,96,768]{2,1,0:T(8,128)(2,1)S(1)}, u32[]{:S(2)}, u32[]{:S(2)}) collective-permute-start(bf16[1,96,768]{2,1,0:T(8,128)(2,1)S(1)} %slice.171), channel_id=1, source_target_pairs={{0,16},{8,24},{16,0},{24,8},{1,17},{9,25},{17,1},{25,9},{2,18},{10... | collective-permute-start | bytes 442376 | tf_op jit(solution)/shard_map/ppermute | solution.py:32
  320.4 4.7 %collective-permute-start.24 = (f32[5,768]{1,0:T(8,128)S(1)}, f32[5,768]{1,0:T(8,128)S(1)}, u32[]{:S(2)}, u32[]{:S(2)}) collective-permute-start(f32[5,768]{1,0:T(8,128)S(1)} %add.185), channel_id=1, source_target_pairs={{0,4},{4,0},{1,5},{5,1},{2,6},{6,2},{3,7},{7,3},{8,12},{12,8},{9,1... | collective-permute-start | bytes 46088 | tf_op jit(solution)/shard_map/ppermute | solution.py:32
  323.4 16.8 %collective-permute-start.29 = (bf16[4,48,1152]{2,1,0:T(8,128)(2,1)S(1)}, bf16[4,48,1152]{2,1,0:T(8,128)(2,1)S(1)}, u32[]{:S(2)}, u32[]{:S(2)}) collective-permute-start(bf16[4,48,1152]{2,1,0:T(8,128)(2,1)S(1)} %slice.175), channel_id=1, source_target_pairs={{0,8},{8,0},{16,24},{24,16},{1,9},{9,1},{17,25},{25,17},{2,10},{10... | collective-permute-start | bytes 1327112 | tf_op jit(solution)/shard_map/ppermute | solution.py:32
  325.1 13.7 %collective-permute-start.25 = (bf16[1,96,768]{2,1,0:T(8,128)(2,1)S(1)}, bf16[1,96,768]{2,1,0:T(8,128)(2,1)S(1)}, u32[]{:S(2)}, u32[]{:S(2)}) collective-permute-start(bf16[1,96,768]{2,1,0:T(8,128)(2,1)S(1)} %add_convert_fusion.11), channel_id=1, source_target_pairs={{0,16},{8,24},{16,0},{24,8},{1,17},{9,25},{17,1},{25,9},{2,18},{10... | collective-permute-start | bytes 442376 | tf_op jit(solution)/shard_map/ppermute | solution.py:32
  327.8 18.0 %collective-permute-start.28 = (bf16[2,48,1920]{2,1,0:T(8,128)(2,1)S(1)}, bf16[2,48,1920]{2,1,0:T(8,128)(2,1)S(1)}, u32[]{:S(2)}, u32[]{:S(2)}) collective-permute-start(bf16[2,48,1920]{2,1,0:T(8,128)(2,1)S(1)} %slice.174), channel_id=1, source_target_pairs={{0,8},{8,0},{16,24},{24,16},{1,9},{9,1},{17,25},{25,17},{2,10},{10... | collective-permute-start | bytes 1105928 | tf_op jit(solution)/shard_map/ppermute | solution.py:32
  328.6 26.4 %collective-permute-start.34 = (bf16[512,768]{1,0:T(8,128)(2,1)S(1)}, bf16[512,768]{1,0:T(8,128)(2,1)S(1)}, u32[]{:S(2)}, u32[]{:S(2)}) collective-permute-start(bf16[512,768]{1,0:T(8,128)(2,1)S(1)} %get-tuple-element.222), channel_id=1, source_target_pairs={{0,1},{1,0},{2,3},{3,2},{4,5},{5,4},{6,7},{7,6},{8,9},{9,8},{10,11... | collective-permute-start | bytes 2359304 | tf_op jit(solution)/shard_map/ppermute | solution.py:1151
  339.6 13.4 %collective-permute-start.26 = (bf16[2,96,768]{2,1,0:T(8,128)(2,1)}, bf16[2,96,768]{2,1,0:T(8,128)(2,1)S(1)}, u32[]{:S(2)}, u32[]{:S(2)}) collective-permute-start(bf16[2,96,768]{2,1,0:T(8,128)(2,1)} %pad_maximum_fusion.20), channel_id=1, source_target_pairs={{0,4},{4,0},{1,5},{5,1},{2,6},{6,2},{3,7},{7,3},{8,12},{12,8},{9,1... | collective-permute-start | bytes 884744 | tf_op jit(solution)/shard_map/ppermute | solution.py:32
  340.2 17.4 %copy-start.27 = (bf16[4,48,1152]{2,1,0:T(8,128)(2,1)}, bf16[4,48,1152]{2,1,0:T(8,128)(2,1)S(1)}, u32[]{:S(2)}) copy-start(bf16[4,48,1152]{2,1,0:T(8,128)(2,1)S(1)} %add_convert_fusion.6) | copy-start | bytes 1327108
  345.9 9.8 %copy-start.29 = (bf16[2,48,1920]{2,1,0:T(8,128)(2,1)}, bf16[2,48,1920]{2,1,0:T(8,128)(2,1)S(1)}, u32[]{:S(2)}) copy-start(bf16[2,48,1920]{2,1,0:T(8,128)(2,1)S(1)} %add_convert_fusion.7) | copy-start | bytes 1105924
  345.9 10.5 %collective-permute-start.33 = (bf16[1,48,1920]{2,1,0:T(8,128)(2,1)S(1)}, bf16[1,48,1920]{2,1,0:T(8,128)(2,1)}, u32[]{:S(2)}, u32[]{:S(2)}) collective-permute-start(bf16[1,48,1920]{2,1,0:T(8,128)(2,1)S(1)} %slice.179), channel_id=1, source_target_pairs={{0,16},{8,24},{16,0},{24,8},{1,17},{9,25},{17,1},{25,9},{2,18},{10... | collective-permute-start | bytes 552968 | tf_op jit(solution)/shard_map/ppermute | solution.py:32
  348.6 3.8 collective-permute-start.27
  350.2 25.9 %collective-permute-start.37 = (bf16[1,512,768]{2,1,0:T(8,128)(2,1)}, bf16[1,512,768]{2,1,0:T(8,128)(2,1)S(1)}, u32[]{:S(2)}, u32[]{:S(2)}) collective-permute-start(bf16[1,512,768]{2,1,0:T(8,128)(2,1)} %get-tuple-element.230), channel_id=1, source_target_pairs={{0,1},{1,0},{2,3},{3,2},{4,5},{5,4},{6,7},{7,6},{8,9},{9,8},{10,11... | collective-permute-start | bytes 2359304 | tf_op jit(solution)/shard_map/ppermute | solution.py:1151
  352.4 8.2 %collective-permute-start.31 = (bf16[2,48,1152]{2,1,0:T(8,128)(2,1)}, bf16[2,48,1152]{2,1,0:T(8,128)(2,1)S(1)}, u32[]{:S(2)}, u32[]{:S(2)}) collective-permute-start(bf16[2,48,1152]{2,1,0:T(8,128)(2,1)} %slice.178), channel_id=1, source_target_pairs={{0,4},{4,0},{1,5},{5,1},{2,6},{6,2},{3,7},{7,3},{8,12},{12,8},{9,1... | collective-permute-start | bytes 663560 | tf_op jit(solution)/shard_map/ppermute | solution.py:32
  353.0 4.7 %copy-start.37 = (f32[5,768]{1,0:T(8,128)}, f32[5,768]{1,0:T(8,128)S(1)}, u32[]{:S(2)}) copy-start(f32[5,768]{1,0:T(8,128)S(1)} %add.193) | copy-start | bytes 46084
  353.0 4.9 %collective-permute-start.35 = (f32[5,768]{1,0:T(8,128)S(1)}, f32[5,768]{1,0:T(8,128)S(1)}, u32[]{:S(2)}, u32[]{:S(2)}) collective-permute-start(f32[5,768]{1,0:T(8,128)S(1)} %add.193), channel_id=1, source_target_pairs={{0,16},{8,24},{16,0},{24,8},{1,17},{9,25},{17,1},{25,9},{2,18},{10... | collective-permute-start | bytes 46088 | tf_op jit(solution)/shard_map/ppermute | solution.py:32
  355.1 19.8 %collective-permute-start.30 = (bf16[4,96,768]{2,1,0:T(8,128)(2,1)S(1)}, bf16[4,96,768]{2,1,0:T(8,128)(2,1)S(1)}, u32[]{:S(2)}, u32[]{:S(2)}) collective-permute-start(bf16[4,96,768]{2,1,0:T(8,128)(2,1)S(1)} %pad_maximum_fusion.16), channel_id=1, source_target_pairs={{0,8},{8,0},{16,24},{24,16},{1,9},{9,1},{17,25},{25,17},{2,10},{10... | collective-permute-start | bytes 1769480 | tf_op jit(solution)/shard_map/ppermute | solution.py:32
  358.6 4.3 %copy-start.30 = (bf16[2,48,1920]{2,1,0:T(8,128)(2,1)S(1)}, bf16[2,48,1920]{2,1,0:T(8,128)(2,1)}, u32[]{:S(2)}) copy-start(bf16[2,48,1920]{2,1,0:T(8,128)(2,1)} %copy-done.29) | copy-start | bytes 1105924
  360.6 14.4 %copy-start.33 = (bf16[2,96,768]{2,1,0:T(8,128)(2,1)S(1)}, bf16[2,96,768]{2,1,0:T(8,128)(2,1)}, u32[]{:S(2)}) copy-start(bf16[2,96,768]{2,1,0:T(8,128)(2,1)} %copy-done.32) | copy-start | bytes 884740
  360.7 10.3 %collective-permute-start.32 = (bf16[1,48,1152]{2,1,0:T(8,128)(2,1)S(1)}, bf16[1,48,1152]{2,1,0:T(8,128)(2,1)S(1)}, u32[]{:S(2)}, u32[]{:S(2)}) collective-permute-start(bf16[1,48,1152]{2,1,0:T(8,128)(2,1)S(1)} %slice.182), channel_id=1, source_target_pairs={{0,16},{8,24},{16,0},{24,8},{1,17},{9,25},{17,1},{25,9},{2,18},{10... | collective-permute-start | bytes 331784 | tf_op jit(solution)/shard_map/ppermute | solution.py:32
  363.9 13.6 %collective-permute-start.39 = (bf16[1,48,1920]{2,1,0:T(8,128)(2,1)S(1)}, bf16[1,48,1920]{2,1,0:T(8,128)(2,1)S(1)}, u32[]{:S(2)}, u32[]{:S(2)}) collective-permute-start(bf16[1,48,1920]{2,1,0:T(8,128)(2,1)S(1)} %add_convert_fusion.10), channel_id=1, source_target_pairs={{0,16},{8,24},{16,0},{24,8},{1,17},{9,25},{17,1},{25,9},{2,18},{10... | collective-permute-start | bytes 552968 | tf_op jit(solution)/shard_map/ppermute | solution.py:32
  371.0 8.4 %collective-permute-start.38 = (bf16[1,48,1152]{2,1,0:T(8,128)(2,1)S(1)}, bf16[1,48,1152]{2,1,0:T(8,128)(2,1)S(1)}, u32[]{:S(2)}, u32[]{:S(2)}) collective-permute-start(bf16[1,48,1152]{2,1,0:T(8,128)(2,1)S(1)} %add_convert_fusion.12), channel_id=1, source_target_pairs={{0,16},{8,24},{16,0},{24,8},{1,17},{9,25},{17,1},{25,9},{2,18},{10... | collective-permute-start | bytes 331784 | tf_op jit(solution)/shard_map/ppermute | solution.py:32
  376.1 4.3 %copy-start.20 = (bf16[2,512,768]{2,1,0:T(8,128)(2,1)S(1)}, bf16[2,512,768]{2,1,0:T(8,128)(2,1)}, u32[]{:S(2)}) copy-start(bf16[2,512,768]{2,1,0:T(8,128)(2,1)} %get-tuple-element.158) | copy-start | bytes 4718596
  376.1 11.9 %collective-permute-start.36 = (bf16[8,96,768]{2,1,0:T(8,128)(2,1)}, bf16[8,96,768]{2,1,0:T(8,128)(2,1)}, u32[]{:S(2)}, u32[]{:S(2)}) collective-permute-start(bf16[8,96,768]{2,1,0:T(8,128)(2,1)} %pad_maximum_fusion.10.part_ref), channel_id=1, source_target_pairs={{0,2},{2,0},{1,3},{3,1},{4,6},{6,4},{5,7},{7,5},{8,10},{10,8},{9,1... | collective-permute-start | bytes 3538952 | tf_op jit(solution)/shard_map/ppermute | solution.py:1081
  380.1 11.3 %collective-permute-start.40 = (bf16[2,48,1152]{2,1,0:T(8,128)(2,1)}, bf16[2,48,1152]{2,1,0:T(8,128)(2,1)S(1)}, u32[]{:S(2)}, u32[]{:S(2)}) collective-permute-start(bf16[2,48,1152]{2,1,0:T(8,128)(2,1)} %pad_maximum_fusion.21), channel_id=1, source_target_pairs={{0,4},{4,0},{1,5},{5,1},{2,6},{6,2},{3,7},{7,3},{8,12},{12,8},{9,1... | collective-permute-start | bytes 663560 | tf_op jit(solution)/shard_map/ppermute | solution.py:32
  380.5 11.0 %collective-permute-start.42 = (bf16[2,48,1920]{2,1,0:T(8,128)(2,1)}, bf16[2,48,1920]{2,1,0:T(8,128)(2,1)S(1)}, u32[]{:S(2)}, u32[]{:S(2)}) collective-permute-start(bf16[2,48,1920]{2,1,0:T(8,128)(2,1)} %pad_maximum_fusion.18), channel_id=1, source_target_pairs={{0,8},{8,0},{16,24},{24,16},{1,9},{9,1},{17,25},{25,17},{2,10},{10... | collective-permute-start | bytes 1105928 | tf_op jit(solution)/shard_map/ppermute | solution.py:32
  391.6 17.6 %collective-permute-start.44 = (bf16[4,48,1920]{2,1,0:T(8,128)(2,1)S(1)}, bf16[4,48,1920]{2,1,0:T(8,128)(2,1)}, u32[]{:S(2)}, u32[]{:S(2)}) collective-permute-start(bf16[4,48,1920]{2,1,0:T(8,128)(2,1)S(1)} %pad_maximum_fusion.14), channel_id=1, source_target_pairs={{0,4},{4,0},{1,5},{5,1},{2,6},{6,2},{3,7},{7,3},{8,12},{12,8},{9,1... | collective-permute-start | bytes 2211848 | tf_op jit(solution)/shard_map/ppermute | solution.py:32
  392.8 10.3 %collective-permute-start.41 = (bf16[4,48,1152]{2,1,0:T(8,128)(2,1)S(1)}, bf16[4,48,1152]{2,1,0:T(8,128)(2,1)S(1)}, u32[]{:S(2)}, u32[]{:S(2)}) collective-permute-start(bf16[4,48,1152]{2,1,0:T(8,128)(2,1)S(1)} %pad_maximum_fusion.17), channel_id=1, source_target_pairs={{0,8},{8,0},{16,24},{24,16},{1,9},{9,1},{17,25},{25,17},{2,10},{10... | collective-permute-start | bytes 1327112 | tf_op jit(solution)/shard_map/ppermute | solution.py:32
  407.2 3.9 copy-start.40
  410.5 9.7 %collective-permute-start.45 = (bf16[8,48,1920]{2,1,0:T(8,128)(2,1)S(1)}, bf16[8,48,1920]{2,1,0:T(8,128)(2,1)}, u32[]{:S(2)}, u32[]{:S(2)}) collective-permute-start(bf16[8,48,1920]{2,1,0:T(8,128)(2,1)S(1)} %pad_maximum_fusion.6.part_ref), channel_id=1, source_target_pairs={{0,2},{2,0},{1,3},{3,1},{4,6},{6,4},{5,7},{7,5},{8,10},{10,8},{9,1... | collective-permute-start | bytes 4423688 | tf_op jit(solution)/shard_map/ppermute | solution.py:1081
  410.6 5.6 %collective-permute-start.43 = (bf16[8,48,1152]{2,1,0:T(8,128)(2,1)S(1)}, bf16[8,48,1152]{2,1,0:T(8,128)(2,1)S(1)}, u32[]{:S(2)}, u32[]{:S(2)}) collective-permute-start(bf16[8,48,1152]{2,1,0:T(8,128)(2,1)S(1)} %copy-done.25), channel_id=1, source_target_pairs={{0,2},{2,0},{1,3},{3,1},{4,6},{6,4},{5,7},{7,5},{8,10},{10,8},{9,1... | collective-permute-start | bytes 2654216 | tf_op jit(solution)/shard_map/ppermute | solution.py:1081
  420.3 4.1 copy-start.1
  (30 other events, 59.5 us)
